TPU v7x, 32 devices: a whole 2x2x4 slice. The times are simulated.
32 devices in a mesh: dp: 8 (over y, x, core), tensor: 4 (over z).
Axes of the slice: x: 2, y: 2, z: 4, core: 2. Of those that a mesh axis runs over, the one named last changes fastest.
Arguments:
- hidden_in: bfloat16 [4096, 2048], P(('dp', 'tensor')), may hold values from -6 to 6
- ln1_gain: float32 [2048], replicated, may hold values from 0.5 to 1.5
- ln1_bias: float32 [2048], replicated, may hold values from -1.8 to 1.8
- qkv_weight: bfloat16 [2048, 6144], P('dp', 'tensor'), may hold values from -0.125 to 0.125
- joined_bias: float32 [6144], P('tensor'), may hold values from -1.8 to 1.8
- out_weight: bfloat16 [2048, 2048], P('tensor', 'dp'), may hold values from -0.5 to 0.5
- output_bias: float32 [2048], replicated, may hold values from -1.8 to 1.8
- ln2_gain: float32 [2048], replicated, may hold values from 0.5 to 1.5
- ln2_bias: float32 [2048], replicated, may hold values from -1.8 to 1.8
- fc1_weight: bfloat16 [2048, 8192], P('dp', 'tensor'), may hold values from -0.125 to 0.125
- first_feed_bias: float32 [8192], P('tensor'), may hold values from -1.8 to 1.8
- fc2_weight: bfloat16 [8192, 2048], P('tensor', 'dp'), may hold values from -0.0625 to 0.0625
- second_feed_bias: float32 [2048], replicated, may hold values from -1.8 to 1.8
- qkv_down: bfloat16 [8, 16, 2048], replicated, may hold values from -0.125 to 0.125
- qkv_up: bfloat16 [8, 16, 6144], replicated, may hold values from -1.5 to 1.5
- out_down: bfloat16 [8, 16, 2048], replicated, may hold values from -0.125 to 0.125
- out_up: bfloat16 [8, 16, 2048], replicated, may hold values from -1.5 to 1.5
- fc1_down: bfloat16 [8, 16, 2048], replicated, may hold values from -0.125 to 0.125
- fc1_up: bfloat16 [8, 16, 8192], replicated, may hold values from -1.5 to 1.5
- fc2_down: bfloat16 [8, 16, 8192], replicated, may hold values from -0.0625 to 0.0625
- fc2_up: bfloat16 [8, 16, 2048], replicated, may hold values from -1.5 to 1.5
- seq_adapter: int32 [2], replicated, may hold values from 0 to 7, as said below
- span_starts: int32 [2, 3], replicated, may hold values from 0 to 1790, as said below
- cotangent: bfloat16 [4096, 2048], P(('dp', 'tensor')), may hold values from -6 to 6
Outputs:
- layer_output: bfloat16 [4096, 2048], P(('dp', 'tensor'))
- hidden_grad: float32 [4096, 2048], P(('dp', 'tensor'))
- qkv_down_grad: float32 [8, 16, 2048], P(None, None, ('dp', 'tensor'))
- qkv_up_grad: float32 [8, 16, 6144], P(None, None, ('dp', 'tensor'))
- out_down_grad: float32 [8, 16, 2048], P(None, None, ('dp', 'tensor'))
- out_up_grad: float32 [8, 16, 2048], P(None, None, ('dp', 'tensor'))
- fc1_down_grad: float32 [8, 16, 2048], P(None, None, ('dp', 'tensor'))
- fc1_up_grad: float32 [8, 16, 8192], P(None, None, ('dp', 'tensor'))
- fc2_down_grad: float32 [8, 16, 8192], P(None, None, ('dp', 'tensor'))
- fc2_up_grad: float32 [8, 16, 2048], P(None, None, ('dp', 'tensor'))
Inputs may be any that keep to these rules, and one draw needn't show every extreme that they name: `span_starts`: in every sequence, picture span j starts between j times the floor of 2048 / 3 and that plus the floor of 2048 / 3 minus 256, so spans never intersect. `seq_adapter`: two sequences use the same adapter only if their numbers differ by a multiple of 8.
All inputs are finite; a program needn't handle non-finite values.
Results may differ from a plain program's by a relative error of at most 0.02.
Values may be sent and summed in bfloat16 or wider, within the bound.
No kernel may reach another device: no remote copies, remote signals or barrier semaphores. Data moves between devices by JAX's collectives and lax.ppermute only.
A program may use at most 88 MiB of HBM per device.

v0:
```python
import jax
import jax.numpy as jnp
from jax import lax
from jax.sharding import PartitionSpec as P

H = 32
HD = 64
ADAPTERS = 8
SEQ_DEVS = 4
PIC = 256


EPS = 1e-05
ADAPTER_FACTOR = 0.5


def partner(array, axis, distance):
    return lax.ppermute(array, axis, [(i, i ^ 1 << distance) for i in range(lax.axis_size(axis))])


def dense_product(left_side, right_side):
    return jnp.dot(left_side, right_side, preferred_element_type=jnp.float32)


def multiply_by_transpose(left_side, right_side):
    return lax.dot_general(
        left_side, right_side, (((1,), (1,)), ((), ())), preferred_element_type=jnp.float32
    )


def transpose_multiply(left_side, right_side):
    return lax.dot_general(
        left_side, right_side, (((0,), (0,)), ((), ())), preferred_element_type=jnp.float32
    )


def gelu_exact(values):
    return jax.nn.gelu(values, approximate=False)


def norm_forward(values, norm_gain, norm_shift):
    centred = values - jnp.mean(values, axis=-1, keepdims=True)
    inverse = lax.rsqrt(jnp.mean(centred * centred, axis=-1, keepdims=True) + EPS)
    unit_rows = centred * inverse
    return (unit_rows * norm_gain + norm_shift, unit_rows, inverse)


def norm_backward(upstream, unit_rows, inverse, norm_gain):
    scaled = upstream * norm_gain
    return inverse * (
        scaled
        - jnp.mean(scaled, axis=-1, keepdims=True)
        - unit_rows * jnp.mean(scaled * unit_rows, axis=-1, keepdims=True)
    )


def span_label(positions, starts):
    inside = (positions[:, None] >= starts[None, :]) & (positions[:, None] < starts[None, :] + PIC)
    span_order = jnp.arange(1, starts.shape[0] + 1, dtype=jnp.int32)
    return jnp.sum(jnp.where(inside, span_order[None, :], 0), axis=1) - 1


def allowed_block(row_pos, col_pos, row_label, col_label):
    return (col_pos[None, :] <= row_pos[:, None]) | (row_label[:, None] == col_label[None, :]) & (
        row_label[:, None] >= 0
    )


def score_block(query_rows, key_cols, row_pos, col_pos, slopes, allowed):
    raw_scores = jnp.einsum(
        "qhd,khd->hqk", query_rows, key_cols, preferred_element_type=jnp.float32
    )
    offset = (col_pos[None, :] - row_pos[:, None]).astype(jnp.float32)
    scores = (raw_scores + slopes[:, None, None] * offset[None]) * 0.125
    return jnp.where(allowed[None], scores, -1e30)


def attend_forward(queries, key_all, value_all, row_base, starts, slopes):
    token_count = queries.shape[0]
    head_count = slopes.shape[0]
    head_width = queries.shape[1] // head_count
    total_keys = key_all.shape[0]
    row_block = min(512, token_count)
    col_block = min(512, total_keys)
    col_labels = span_label(jnp.arange(total_keys, dtype=jnp.int32), starts)

    def one_block(block_index):
        row_start = block_index * row_block
        query_rows = lax.dynamic_slice_in_dim(queries, row_start, row_block, 0).reshape(
            row_block, head_count, head_width
        )
        row_pos = row_base + row_start + jnp.arange(row_block, dtype=jnp.int32)
        row_label = span_label(row_pos, starts)

        def block_mask(col_index):
            col_start = col_index * col_block
            col_pos = col_start + jnp.arange(col_block, dtype=jnp.int32)
            col_label = lax.dynamic_slice_in_dim(col_labels, col_start, col_block, 0)
            return (col_start, col_pos, allowed_block(row_pos, col_pos, row_label, col_label))

        def stats_step(col_index, stat_state):
            col_start, col_pos, allowed = block_mask(col_index)

            def stats_compute(current):
                row_top, row_total = current
                key_cols = lax.dynamic_slice_in_dim(key_all, col_start, col_block, 0).reshape(
                    col_block, head_count, head_width
                )
                scores = score_block(query_rows, key_cols, row_pos, col_pos, slopes, allowed)
                new_top = jnp.maximum(row_top, jnp.max(scores, axis=-1))
                new_total = row_total * jnp.exp(row_top - new_top) + jnp.sum(
                    jnp.exp(scores - new_top[:, :, None]), axis=-1
                )
                return (new_top, new_total)

            return lax.cond(jnp.any(allowed), stats_compute, lambda current: current, stat_state)

        start_state = (
            jnp.full((head_count, row_block), -1e30, jnp.float32),
            jnp.zeros((head_count, row_block), jnp.float32),
        )
        row_top, row_total = lax.fori_loop(0, total_keys // col_block, stats_step, start_state)
        log_total = row_top + jnp.log(row_total)

        def value_step(col_index, summed):
            col_start, col_pos, allowed = block_mask(col_index)

            def value_compute(current):
                key_cols = lax.dynamic_slice_in_dim(key_all, col_start, col_block, 0).reshape(
                    col_block, head_count, head_width
                )
                value_cols = lax.dynamic_slice_in_dim(value_all, col_start, col_block, 0).reshape(
                    col_block, head_count, head_width
                )
                scores = score_block(query_rows, key_cols, row_pos, col_pos, slopes, allowed)
                probability = jnp.exp(scores - log_total[:, :, None]).astype(jnp.bfloat16)
                return current + jnp.einsum(
                    "hqk,khd->qhd", probability, value_cols, preferred_element_type=jnp.float32
                )

            return lax.cond(jnp.any(allowed), value_compute, lambda current: current, summed)

        output = lax.fori_loop(
            0,
            total_keys // col_block,
            value_step,
            jnp.zeros((row_block, head_count, head_width), jnp.float32),
        )
        return (output.reshape(row_block, head_count * head_width), log_total)

    outputs, log_totals = lax.map(one_block, jnp.arange(token_count // row_block, dtype=jnp.int32))
    return (outputs.reshape(token_count, -1), log_totals)


def attend_backward(
    queries, key_all, value_all, outputs, grad_out, log_totals, row_base, starts, slopes
):
    token_count = queries.shape[0]
    head_count = slopes.shape[0]
    head_width = queries.shape[1] // head_count
    total_keys = key_all.shape[0]
    row_block = min(512, token_count)
    col_block = min(512, total_keys)
    col_labels = span_label(jnp.arange(total_keys, dtype=jnp.int32), starts)

    def block_step(block_index, carry_all):
        grad_queries, grad_keys, grad_values = carry_all
        row_start = block_index * row_block
        query_rows = lax.dynamic_slice_in_dim(queries, row_start, row_block, 0).reshape(
            row_block, head_count, head_width
        )
        grad_rows = lax.dynamic_slice_in_dim(grad_out, row_start, row_block, 0).reshape(
            row_block, head_count, head_width
        )
        out_rows = lax.dynamic_slice_in_dim(outputs, row_start, row_block, 0).reshape(
            row_block, head_count, head_width
        )
        delta = jnp.sum(grad_rows.astype(jnp.float32) * out_rows, axis=-1).T
        log_total = lax.dynamic_index_in_dim(log_totals, block_index, 0, keepdims=False)
        row_pos = row_base + row_start + jnp.arange(row_block, dtype=jnp.int32)
        row_label = span_label(row_pos, starts)

        def col_step(col_index, inner_carry):
            col_start = col_index * col_block
            col_pos = col_start + jnp.arange(col_block, dtype=jnp.int32)
            col_label = lax.dynamic_slice_in_dim(col_labels, col_start, col_block, 0)
            allowed = allowed_block(row_pos, col_pos, row_label, col_label)

            def col_compute(current):
                rows_grad, keys_grad, values_grad = current
                key_cols = lax.dynamic_slice_in_dim(key_all, col_start, col_block, 0).reshape(
                    col_block, head_count, head_width
                )
                value_cols = lax.dynamic_slice_in_dim(value_all, col_start, col_block, 0).reshape(
                    col_block, head_count, head_width
                )
                scores = score_block(query_rows, key_cols, row_pos, col_pos, slopes, allowed)
                probability = jnp.exp(scores - log_total[:, :, None])
                grad_prob = jnp.einsum(
                    "qhd,khd->hqk", grad_rows, value_cols, preferred_element_type=jnp.float32
                )
                grad_scores = (probability * (grad_prob - delta[:, :, None])).astype(jnp.bfloat16)
                rows_grad = rows_grad + 0.125 * jnp.einsum(
                    "hqk,khd->qhd", grad_scores, key_cols, preferred_element_type=jnp.float32
                )
                key_part = 0.125 * jnp.einsum(
                    "hqk,qhd->khd", grad_scores, query_rows, preferred_element_type=jnp.float32
                )
                value_part = jnp.einsum(
                    "hqk,qhd->khd",
                    probability.astype(jnp.bfloat16),
                    grad_rows,
                    preferred_element_type=jnp.float32,
                )
                keys_grad = lax.dynamic_update_slice_in_dim(
                    keys_grad,
                    lax.dynamic_slice_in_dim(keys_grad, col_start, col_block, 0)
                    + key_part.reshape(col_block, -1),
                    col_start,
                    0,
                )
                values_grad = lax.dynamic_update_slice_in_dim(
                    values_grad,
                    lax.dynamic_slice_in_dim(values_grad, col_start, col_block, 0)
                    + value_part.reshape(col_block, -1),
                    col_start,
                    0,
                )
                return (rows_grad, keys_grad, values_grad)

            return lax.cond(jnp.any(allowed), col_compute, lambda current: current, inner_carry)

        start_rows = jnp.zeros((row_block, head_count, head_width), jnp.float32)
        rows_grad, grad_keys, grad_values = lax.fori_loop(
            0, total_keys // col_block, col_step, (start_rows, grad_keys, grad_values)
        )
        grad_queries = lax.dynamic_update_slice_in_dim(
            grad_queries, rows_grad.reshape(row_block, -1), row_start, 0
        )
        return (grad_queries, grad_keys, grad_values)

    start_all = (
        jnp.zeros(queries.shape, jnp.float32),
        jnp.zeros(key_all.shape, jnp.float32),
        jnp.zeros(value_all.shape, jnp.float32),
    )
    return lax.fori_loop(0, token_count // row_block, block_step, start_all)


def local(
    hidden_in,
    ln1_gain,
    ln1_bias,
    qkv_weight,
    joined_bias,
    out_weight,
    output_bias,
    ln2_gain,
    ln2_bias,
    fc1_weight,
    first_feed_bias,
    fc2_weight,
    second_feed_bias,
    qkv_down,
    qkv_up,
    out_down,
    out_up,
    fc1_down,
    fc1_up,
    fc2_down,
    fc2_up,
    seq_adapter,
    span_starts,
    cotangent,
):
    tensor_index = lax.axis_index("tensor")
    data_index = lax.axis_index("dp")
    group_index = data_index // SEQ_DEVS
    group_part = data_index % SEQ_DEVS
    adapter_slot = lax.dynamic_index_in_dim(seq_adapter, group_index, 0, keepdims=False)
    starts = lax.dynamic_index_in_dim(span_starts, group_index, 0, keepdims=False)
    qkv_cols = qkv_weight.shape[1]
    context_cols = out_weight.shape[0]
    hidden_cols = fc1_weight.shape[1]
    head_count = qkv_cols // (3 * HD)
    head_first = tensor_index * head_count
    slopes = jnp.exp2(
        -8.0
        * ((head_first + jnp.arange(head_count, dtype=jnp.int32)).astype(jnp.float32) + 1.0)
        / H
    )

    def pick(stack_all):
        return lax.dynamic_index_in_dim(stack_all, adapter_slot, 0, keepdims=False)

    def local_cols(matrix, count):
        return lax.dynamic_slice_in_dim(matrix, tensor_index * count, count, 1)

    down_qkv = pick(qkv_down)
    joined_raise = local_cols(pick(qkv_up), qkv_cols)
    down_out = local_cols(pick(out_down), context_cols)
    output_raise = pick(out_up)
    down_fc1 = pick(fc1_down)
    first_feed_raise = local_cols(pick(fc1_up), hidden_cols)
    down_fc2 = local_cols(pick(fc2_down), hidden_cols)
    second_feed_raise = pick(fc2_up)
    whole_joined_projection, full_out, whole_first_feed, full_fc2 = (
        lax.all_gather(qkv_weight, "dp", axis=0, tiled=True),
        lax.all_gather(out_weight, "dp", axis=1, tiled=True),
        lax.all_gather(fc1_weight, "dp", axis=0, tiled=True),
        lax.all_gather(fc2_weight, "dp", axis=1, tiled=True),
    )
    residual_stream = hidden_in.astype(jnp.float32)
    normed1, unit1, inverse1 = norm_forward(residual_stream, ln1_gain, ln1_bias)
    normed1 = normed1.astype(jnp.bfloat16)
    lowrank1 = multiply_by_transpose(normed1, down_qkv).astype(jnp.bfloat16)
    sequence_normalized1, sequence_adapter1 = (
        lax.all_gather(normed1, "tensor", axis=0, tiled=True),
        lax.all_gather(lowrank1, "tensor", axis=0, tiled=True),
    )
    joined_projection = (
        dense_product(sequence_normalized1, whole_joined_projection)
        + ADAPTER_FACTOR * dense_product(sequence_adapter1, joined_raise)
        + joined_bias
    ).astype(jnp.bfloat16)
    token_count = joined_projection.shape[0]
    grouped = joined_projection.reshape(token_count, head_count, 3, HD)
    queries = grouped[:, :, 0].reshape(token_count, -1)
    key_all = grouped[:, :, 1].reshape(token_count, -1)
    value_all = grouped[:, :, 2].reshape(token_count, -1)
    level_count = SEQ_DEVS.bit_length() - 1
    for bit_level in range(level_count):
        other_keys, other_values = partner((key_all, value_all), "dp", bit_level)
        upper_half = data_index // (1 << bit_level) % 2 == 1
        key_all = jnp.concatenate(
            [
                jnp.where(upper_half, other_keys, key_all),
                jnp.where(upper_half, key_all, other_keys),
            ],
            axis=0,
        )
        value_all = jnp.concatenate(
            [
                jnp.where(upper_half, other_values, value_all),
                jnp.where(upper_half, value_all, other_values),
            ],
            axis=0,
        )
    row_base = group_part * token_count
    attended, log_totals = attend_forward(queries, key_all, value_all, row_base, starts, slopes)
    attended_context = attended.astype(jnp.bfloat16)
    part_out = dense_product(attended_context, full_out)
    part_lowrank = multiply_by_transpose(attended_context, down_out)
    output_rows, rows_lowrank = (
        lax.psum_scatter(
            part_out.astype(jnp.bfloat16), "tensor", scatter_dimension=0, tiled=True
        ).astype(jnp.float32),
        lax.psum_scatter(
            part_lowrank.astype(jnp.bfloat16), "tensor", scatter_dimension=0, tiled=True
        ).astype(jnp.float32),
    )
    adapter_product2 = rows_lowrank.astype(jnp.bfloat16)
    middle_activation = residual_stream + (
        output_rows + ADAPTER_FACTOR * dense_product(adapter_product2, output_raise) + output_bias
    )
    normed2, unit2, inverse2 = norm_forward(middle_activation, ln2_gain, ln2_bias)
    normed2 = normed2.astype(jnp.bfloat16)
    lowrank3 = multiply_by_transpose(normed2, down_fc1).astype(jnp.bfloat16)
    sequence_normalized2, sequence_adapter3 = (
        lax.all_gather(normed2, "tensor", axis=0, tiled=True),
        lax.all_gather(lowrank3, "tensor", axis=0, tiled=True),
    )
    preactivation = (
        dense_product(sequence_normalized2, whole_first_feed)
        + ADAPTER_FACTOR * dense_product(sequence_adapter3, first_feed_raise)
        + first_feed_bias
    )
    activated_rows = gelu_exact(preactivation).astype(jnp.bfloat16)
    part_mlp = dense_product(activated_rows, full_fc2)
    part_mlp_lowrank = multiply_by_transpose(activated_rows, down_fc2)
    feedforward_rows, rows_mlp_lowrank = (
        lax.psum_scatter(
            part_mlp.astype(jnp.bfloat16), "tensor", scatter_dimension=0, tiled=True
        ).astype(jnp.float32),
        lax.psum_scatter(
            part_mlp_lowrank.astype(jnp.bfloat16), "tensor", scatter_dimension=0, tiled=True
        ).astype(jnp.float32),
    )
    adapter_product4 = rows_mlp_lowrank.astype(jnp.bfloat16)
    layer_output = (
        middle_activation
        + (
            feedforward_rows
            + ADAPTER_FACTOR * dense_product(adapter_product4, second_feed_raise)
            + second_feed_bias
        )
    ).astype(jnp.bfloat16)
    grad_top = cotangent.astype(jnp.float32)
    second_feed_raise_gradient = ADAPTER_FACTOR * transpose_multiply(adapter_product4, cotangent)
    adapter_gradient4 = (
        ADAPTER_FACTOR * multiply_by_transpose(cotangent, second_feed_raise)
    ).astype(jnp.bfloat16)
    back_qkv, back_out, back_fc1, back_fc2 = (
        lax.all_gather(qkv_weight, "dp", axis=0, tiled=True),
        lax.all_gather(out_weight, "dp", axis=1, tiled=True),
        lax.all_gather(fc1_weight, "dp", axis=0, tiled=True),
        lax.all_gather(fc2_weight, "dp", axis=1, tiled=True),
    )
    seq_grad_top, seq_grad_lowrank4 = (
        lax.all_gather(cotangent, "tensor", axis=0, tiled=True),
        lax.all_gather(adapter_gradient4, "tensor", axis=0, tiled=True),
    )
    grad_active = multiply_by_transpose(seq_grad_top, back_fc2) + dense_product(
        seq_grad_lowrank4, down_fc2
    )
    down_fc2_grad = transpose_multiply(seq_grad_lowrank4, activated_rows)
    gelu_pull = jax.vjp(gelu_exact, preactivation)[1]
    preactivation_gradient = gelu_pull(grad_active)[0].astype(jnp.bfloat16)
    part_in2 = multiply_by_transpose(preactivation_gradient, back_fc1)
    first_feed_raise_gradient = ADAPTER_FACTOR * transpose_multiply(
        sequence_adapter3, preactivation_gradient
    )
    partial_adapter_input2 = ADAPTER_FACTOR * multiply_by_transpose(
        preactivation_gradient, first_feed_raise
    )
    rows_in2, rows_lowrank_in2 = (
        lax.psum_scatter(
            part_in2.astype(jnp.bfloat16), "tensor", scatter_dimension=0, tiled=True
        ).astype(jnp.float32),
        lax.psum_scatter(
            partial_adapter_input2.astype(jnp.bfloat16), "tensor", scatter_dimension=0, tiled=True
        ).astype(jnp.float32),
    )
    grad_lowrank3 = rows_lowrank_in2.astype(jnp.bfloat16)
    down_fc1_grad = transpose_multiply(grad_lowrank3, normed2)
    grad_normed2 = rows_in2 + dense_product(grad_lowrank3, down_fc1)
    grad_middle = grad_top + norm_backward(grad_normed2, unit2, inverse2, ln2_gain)
    branch_gradient = grad_middle.astype(jnp.bfloat16)
    output_raise_gradient = ADAPTER_FACTOR * transpose_multiply(adapter_product2, branch_gradient)
    adapter_gradient2 = (
        ADAPTER_FACTOR * multiply_by_transpose(branch_gradient, output_raise)
    ).astype(jnp.bfloat16)
    seq_grad_branch, seq_grad_lowrank2 = (
        lax.all_gather(branch_gradient, "tensor", axis=0, tiled=True),
        lax.all_gather(adapter_gradient2, "tensor", axis=0, tiled=True),
    )
    grad_context = (
        multiply_by_transpose(seq_grad_branch, back_out)
        + dense_product(seq_grad_lowrank2, down_out)
    ).astype(jnp.bfloat16)
    down_out_grad = transpose_multiply(seq_grad_lowrank2, attended_context)
    grad_queries, grad_keys, grad_values = attend_backward(
        queries, key_all, value_all, attended, grad_context, log_totals, row_base, starts, slopes
    )
    for bit_level in reversed(range(level_count)):
        half_rows = grad_keys.shape[0] // 2
        upper_half = data_index // (1 << bit_level) % 2 == 1
        own_keys = jnp.where(upper_half, grad_keys[half_rows:], grad_keys[:half_rows])
        sent_keys = jnp.where(upper_half, grad_keys[:half_rows], grad_keys[half_rows:])
        own_values = jnp.where(upper_half, grad_values[half_rows:], grad_values[:half_rows])
        sent_values = jnp.where(upper_half, grad_values[:half_rows], grad_values[half_rows:])
        got_keys, got_values = (
            partner(sent_keys.astype(jnp.bfloat16), "dp", bit_level).astype(sent_keys.dtype),
            partner(sent_values.astype(jnp.bfloat16), "dp", bit_level).astype(sent_values.dtype),
        )
        grad_keys = own_keys + got_keys
        grad_values = own_values + got_values
    joined_gradient = (
        jnp.stack(
            [
                grad_queries.reshape(token_count, head_count, HD),
                grad_keys.reshape(token_count, head_count, HD),
                grad_values.reshape(token_count, head_count, HD),
            ],
            axis=2,
        )
        .reshape(token_count, -1)
        .astype(jnp.bfloat16)
    )
    part_in1 = multiply_by_transpose(joined_gradient, back_qkv)
    joined_raise_gradient = ADAPTER_FACTOR * transpose_multiply(sequence_adapter1, joined_gradient)
    partial_adapter_input1 = ADAPTER_FACTOR * multiply_by_transpose(joined_gradient, joined_raise)
    rows_in1, rows_lowrank_in1 = (
        lax.psum_scatter(
            part_in1.astype(jnp.bfloat16), "tensor", scatter_dimension=0, tiled=True
        ).astype(jnp.float32),
        lax.psum_scatter(
            partial_adapter_input1.astype(jnp.bfloat16), "tensor", scatter_dimension=0, tiled=True
        ).astype(jnp.float32),
    )
    grad_lowrank1 = rows_lowrank_in1.astype(jnp.bfloat16)
    down_qkv_grad = transpose_multiply(grad_lowrank1, normed1)
    grad_normed1 = rows_in1 + dense_product(grad_lowrank1, down_qkv)
    hidden_grad = grad_middle + norm_backward(grad_normed1, unit1, inverse1, ln1_gain)

    def widened(grad_piece, full_width, count):
        wide_piece = jnp.zeros((grad_piece.shape[0], full_width), jnp.float32)
        return lax.dynamic_update_slice_in_dim(wide_piece, grad_piece, tensor_index * count, 1)

    selector = (jnp.arange(ADAPTERS, dtype=jnp.int32) == adapter_slot).astype(jnp.float32)

    def stacked(grad_piece):
        return selector[:, None, None] * grad_piece[None]

    summed = (
        lax.psum_scatter(stacked(down_qkv_grad), ("dp", "tensor"), scatter_dimension=2, tiled=True),
        lax.psum_scatter(
            stacked(widened(joined_raise_gradient, qkv_up.shape[2], qkv_cols)),
            ("dp", "tensor"),
            scatter_dimension=2,
            tiled=True,
        ),
        lax.psum_scatter(
            stacked(widened(down_out_grad, out_down.shape[2], context_cols)),
            ("dp", "tensor"),
            scatter_dimension=2,
            tiled=True,
        ),
        lax.psum_scatter(
            stacked(output_raise_gradient), ("dp", "tensor"), scatter_dimension=2, tiled=True
        ),
        lax.psum_scatter(stacked(down_fc1_grad), ("dp", "tensor"), scatter_dimension=2, tiled=True),
        lax.psum_scatter(
            stacked(widened(first_feed_raise_gradient, fc1_up.shape[2], hidden_cols)),
            ("dp", "tensor"),
            scatter_dimension=2,
            tiled=True,
        ),
        lax.psum_scatter(
            stacked(widened(down_fc2_grad, fc2_down.shape[2], hidden_cols)),
            ("dp", "tensor"),
            scatter_dimension=2,
            tiled=True,
        ),
        lax.psum_scatter(
            stacked(second_feed_raise_gradient), ("dp", "tensor"), scatter_dimension=2, tiled=True
        ),
    )
    return (
        layer_output,
        hidden_grad,
        summed[0],
        summed[1],
        summed[2],
        summed[3],
        summed[4],
        summed[5],
        summed[6],
        summed[7],
    )


def solution(mesh):
    placed = (
        P(("dp", "tensor"), None),
        P(),
        P(),
        P("dp", "tensor"),
        P("tensor"),
        P("tensor", "dp"),
        P(),
        P(),
        P(),
        P("dp", "tensor"),
        P("tensor"),
        P("tensor", "dp"),
        P(),
        P(),
        P(),
        P(),
        P(),
        P(),
        P(),
        P(),
        P(),
        P(),
        P(),
        P(("dp", "tensor"), None),
    )
    return jax.shard_map(
        local,
        mesh=mesh,
        in_specs=placed,
        out_specs=(
            P(("dp", "tensor"), None),
            P(("dp", "tensor"), None),
            P(None, None, ("dp", "tensor")),
            P(None, None, ("dp", "tensor")),
            P(None, None, ("dp", "tensor")),
            P(None, None, ("dp", "tensor")),
            P(None, None, ("dp", "tensor")),
            P(None, None, ("dp", "tensor")),
            P(None, None, ("dp", "tensor")),
            P(None, None, ("dp", "tensor")),
        ),
        check_vma=False,
    )
```

profile of v0, /device:TPU:0, one launch (start us, length us, event | category | flops | bytes accessed | tf_op | source)
XLA Modules:
  0.0 2020.3 jit_solution(12374928960784732922)
XLA Ops:
  18.1 13.8 all_gather.42
  31.9 29.8 %all-gather.9.cloned.1.call-done = bf16[512,2048]{1,0:T(8,128)(2,1)} async-done(((bf16[128,2048]{1,0:T(8,128)(2,1)}), bf16[512,2048]{1,0:T(8,128)(2,1)}) %all-gather.9.cloned.1.call-update) | async-done | bytes 2097168 | tf_op jit(solution)/shard_map/all_gather | solution.py:318
  61.7 46.2 %all-gather.11.cloned.1.call-done = bf16[2048,1536]{1,0:T(8,128)(2,1)} async-done(((bf16[256,1536]{1,0:T(8,128)(2,1)}), bf16[2048,1536]{1,0:T(8,128)(2,1)}) %all-gather.11.cloned.1.call-update) | async-done | bytes 6291472 | tf_op jit(solution)/shard_map/all_gather | solution.py:308
  132.0 23.5 %collective-permute-done.3 = bf16[1024,512]{0,1:T(8,128)(2,1)} collective-permute-done((bf16[1024,512]{0,1:T(8,128)(2,1)}, bf16[1024,512]{0,1:T(8,128)(2,1)}, u32[]{:S(2)}, u32[]{:S(2)}) %collective-permute-start.3) | collective-permute-done | bytes 1048608 | tf_op jit(solution)/shard_map/ppermute | solution.py:18
  155.6 27.2 %collective-permute-done.1 = bf16[1024,512]{0,1:T(8,128)(2,1)} collective-permute-done((bf16[1024,512]{0,1:T(8,128)(2,1)}, bf16[1024,512]{0,1:T(8,128)(2,1)}, u32[]{:S(2)}, u32[]{:S(2)}) %collective-permute-start.1) | collective-permute-done | bytes 1048608 | tf_op jit(solution)/shard_map/ppermute | solution.py:18
  188.3 14.6 while.75
  190.1 7.4 conditional.9
  207.3 16.8 while.76
  209.1 9.6 conditional.10
  235.0 62.2 %reduce-scatter.49.cloned.1.call-done = bf16[128,16]{1,0:T(8,128)(2,1)} async-done(((bf16[512,16]{1,0:T(8,128)(2,1)}), bf16[128,16]{1,0:T(8,128)(2,1)}) %reduce-scatter.49.cloned.1.call-update) | async-done | bytes 4112
  297.2 44.3 %reduce-scatter.37.cloned.1.call-done = bf16[128,2048]{1,0:T(8,128)(2,1)} async-done(((bf16[512,2048]{1,0:T(8,128)(2,1)}), bf16[128,2048]{1,0:T(8,128)(2,1)}) %reduce-scatter.37.cloned.1.call-update) | async-done | bytes 524304 | tf_op jit(solution)/shard_map/reduce_scatter | solution.py:355
  346.6 12.1 all_gather.49
  358.7 29.6 %all-gather.21.cloned.1.call-done = bf16[512,2048]{1,0:T(8,128)(2,1)} async-done(((bf16[128,2048]{1,0:T(8,128)(2,1)}), bf16[512,2048]{1,0:T(8,128)(2,1)}) %all-gather.21.cloned.1.call-update) | async-done | bytes 2097168 | tf_op jit(solution)/shard_map/all_gather | solution.py:410
  388.3 57.0 %all-gather.19.cloned.1.call-done = bf16[2048,2048]{1,0:T(8,128)(2,1)} async-done(((bf16[2048,256]{1,0:T(8,128)(2,1)}), bf16[2048,2048]{1,0:T(8,128)(2,1)}) %all-gather.19.cloned.1.call-update) | async-done | bytes 8388624 | tf_op jit(solution)/shard_map/all_gather | solution.py:311
  445.3 10.5 fusion.146
  457.0 11.9 all_gather.46
  468.9 32.8 %all-gather.17.cloned.1.call-done = bf16[2048,2048]{1,0:T(8,128)(2,1)} async-done(((bf16[256,2048]{1,0:T(8,128)(2,1)}), bf16[2048,2048]{1,0:T(8,128)(2,1)}) %all-gather.17.cloned.1.call-update) | async-done | bytes 8388624 | tf_op jit(solution)/shard_map/all_gather | solution.py:310
  501.6 47.5 %all-gather.15.cloned.1.call-done = bf16[512,2048]{1,0:T(8,128)(2,1)} async-done(((bf16[128,2048]{1,0:T(8,128)(2,1)}), bf16[512,2048]{1,0:T(8,128)(2,1)}) %all-gather.15.cloned.1.call-update) | async-done | bytes 2097168 | tf_op jit(solution)/shard_map/all_gather | solution.py:370
  549.2 7.6 fusion.145
  556.8 11.8 multiply_convert_fusion
  574.6 10.0 convolution_convert_fusion.1
  584.6 7.9 reduce-scatter.53.cloned.1.call-done
  592.5 44.6 %reduce-scatter.41.cloned.1.call-done = bf16[128,2048]{1,0:T(8,128)(2,1)} async-done(((bf16[512,2048]{1,0:T(8,128)(2,1)}), bf16[128,2048]{1,0:T(8,128)(2,1)}) %reduce-scatter.41.cloned.1.call-update) | async-done | bytes 524304 | tf_op jit(solution)/shard_map/reduce_scatter | solution.py:427
  641.7 12.0 all_gather.51
  653.7 32.1 %all-gather.23.cloned.1.call-done = bf16[512,2048]{1,0:T(8,128)(2,1)} async-done(((bf16[128,2048]{1,0:T(8,128)(2,1)}), bf16[512,2048]{1,0:T(8,128)(2,1)}) %all-gather.23.cloned.1.call-update) | async-done | bytes 2097168 | tf_op jit(solution)/shard_map/all_gather | solution.py:444
  696.4 23.7 %while.77 = (s32[]{:T(128)}, f32[512,8,64]{0,2,1:T(8,128)S(1)}, f32[2048,512]{0,1:T(8,128)}, f32[2048,512]{0,1:T(8,128)}, s32[512]{0:T(512)S(1)}, /*index=5*/s32...) while((s32[]{:T(128)}, f32[512,8,64]{0,2,1:T(8,128)S(1)}, ...), condition=%wide.region_31.32_spmd.clone, body=%wide.region_27.31_spmd.clone.sunk | while | flops 1374685184 | bytes 60110468 | solution.py:234
  698.4 16.2 conditional.11
  722.7 33.7 %collective-permute-start.6 = (bf16[1024,512]{0,1:T(8,128)(2,1)S(1)}, bf16[1024,512]{0,1:T(8,128)(2,1)S(1)}, u32[]{:S(2)}, u32[]{:S(2)}) collective-permute-start(bf16[1024,512]{0,1:T(8,128)(2,1)S(1)} %select_convert_fusion), channel_id=1, source_target_pairs={{0,8},{4,12},{8,0},{12,4},{16,24},{20,28},{24,16},{28,20},{1,9},{5... | collective-permute-start | bytes 3145736 | tf_op jit(solution)/shard_map/ppermute | solution.py:18
  758.9 10.3 collective-permute-done.6
  770.1 22.4 %collective-permute-start.7 = (bf16[512,512]{0,1:T(8,128)(2,1)S(1)}, bf16[512,512]{0,1:T(8,128)(2,1)}, u32[]{:S(2)}, u32[]{:S(2)}) collective-permute-start(bf16[512,512]{0,1:T(8,128)(2,1)S(1)} %select_convert_fusion.2), channel_id=1, source_target_pairs={{0,4},{4,0},{8,12},{12,8},{16,20},{20,16},{24,28},{28,24},{1,5},{5... | collective-permute-start | bytes 1572872 | tf_op jit(solution)/shard_map/ppermute | solution.py:18
  794.6 10.3 collective-permute-start.5
  814.6 9.9 convolution_convert_fusion.2
  828.2 18.1 reduce-scatter.55.cloned.1.call-done
  856.2 6.5 reshape.318
  868.8 6.5 reshape.322
  902.5 6.6 reshape.328
  912.0 13.3 copy.71
  925.4 16.3 reshape.320
  941.7 7.5 convolution_convert_fusion
  959.7 67.6 %reduce-scatter.57.cloned.1.call-done = f32[64,128]{1,0:T(8,128)} async-done(((f32[2048,128]{1,0:T(8,128)}), f32[64,128]{1,0:T(8,128)}) %reduce-scatter.57.cloned.1.call-update) | async-done | bytes 32784
  1029.0 133.2 %reduce-scatter.61.cloned.1.call-done = f32[64,128]{1,0:T(8,128)} async-done(((f32[2048,128]{1,0:T(8,128)}), f32[64,128]{1,0:T(8,128)}) %reduce-scatter.61.cloned.1.call-update) | async-done | bytes 32784
  1163.9 132.4 %reduce-scatter.63.cloned.1.call-done = f32[64,128]{1,0:T(8,128)} async-done(((f32[2048,128]{1,0:T(8,128)}), f32[64,128]{1,0:T(8,128)}) %reduce-scatter.63.cloned.1.call-update) | async-done | bytes 32784
  1298.0 132.5 %reduce-scatter.65.cloned.1.call-done = f32[64,128]{1,0:T(8,128)} async-done(((f32[2048,128]{1,0:T(8,128)}), f32[64,128]{1,0:T(8,128)}) %reduce-scatter.65.cloned.1.call-update) | async-done | bytes 32784
  1432.2 132.6 %reduce-scatter.67.cloned.1.call-done = f32[64,128]{1,0:T(8,128)} async-done(((f32[2048,128]{1,0:T(8,128)}), f32[64,128]{1,0:T(8,128)}) %reduce-scatter.67.cloned.1.call-update) | async-done | bytes 32784
  1566.5 102.0 %reduce-scatter.59.cloned.1.call-done = f32[192,128]{1,0:T(8,128)} async-done(((f32[6144,128]{1,0:T(8,128)}), f32[192,128]{1,0:T(8,128)}) %reduce-scatter.59.cloned.1.call-update) | async-done | bytes 98320
  1670.6 43.0 %reduce-scatter.43.cloned.1.call-done = bf16[128,2048]{1,0:T(8,128)(2,1)} async-done(((bf16[512,2048]{1,0:T(8,128)(2,1)}), bf16[128,2048]{1,0:T(8,128)(2,1)}) %reduce-scatter.43.cloned.1.call-update) | async-done | bytes 524304 | tf_op jit(solution)/shard_map/reduce_scatter | solution.py:484
  1717.8 146.0 %reduce-scatter.45.cloned.1.call-done = f32[8,16,256]{2,1,0:T(8,128)} async-done(((f32[8,16,8192]{2,1,0:T(8,128)}), f32[8,16,256]{2,1,0:T(8,128)}) %reduce-scatter.45.cloned.1.call-update) | async-done | bytes 131088 | tf_op jit(solution)/shard_map/reduce_scatter | solution.py:523
  1863.8 149.3 %reduce-scatter.47.cloned.1.call-done = f32[8,16,256]{2,1,0:T(8,128)} async-done(((f32[8,16,8192]{2,1,0:T(8,128)}), f32[8,16,256]{2,1,0:T(8,128)}) %reduce-scatter.47.cloned.1.call-update) | async-done | bytes 131088 | tf_op jit(solution)/shard_map/reduce_scatter | solution.py:529
  (381 shorter events, 219.9 us)
Async XLA Ops:
  7.2 549.6 %copy-start = (bf16[8,16,8192]{2,1,0:T(8,128)(2,1)S(1)}, bf16[8,16,8192]{2,1,0:T(8,128)(2,1)}, u32[]{:S(2)}) copy-start(bf16[8,16,8192]{2,1,0:T(8,128)(2,1)} %param.54) | copy-start | bytes 6291460
  7.2 54.5 %all-gather.9.cloned.1.call-start = ((), (), s32[]{:S(2)}) async-start(), calls=%async_computation.16 | async-start | bytes 2621440 | tf_op jit(solution)/shard_map/all_gather | solution.py:318
  12.8 95.1 %all-gather.11.cloned.1.call-start = ((), (), s32[]{:S(2)}) async-start(), calls=%async_computation.17 | async-start | bytes 7077888 | tf_op jit(solution)/shard_map/all_gather | solution.py:308
  13.5 214.6 %all-gather.13.cloned.1.call-start = ((), (), s32[]{:S(2)}) async-start(), calls=%async_computation.18 | async-start | bytes 2359296 | tf_op jit(solution)/shard_map/all_gather | solution.py:309
  31.8 82.2 %copy-start.41 = (f32[1536]{0:T(1024)S(1)}, f32[1536]{0:T(1024)}, u32[]{:S(2)}) copy-start(f32[1536]{0:T(1024)} %param.40) | copy-start | bytes 18436
  121.8 2.0 collective-permute-start.2
  122.0 5.7 collective-permute-start
  126.2 29.3 %collective-permute-start.3 = (bf16[1024,512]{0,1:T(8,128)(2,1)}, bf16[1024,512]{0,1:T(8,128)(2,1)}, u32[]{:S(2)}, u32[]{:S(2)}) collective-permute-start(bf16[1024,512]{0,1:T(8,128)(2,1)} %pad_maximum_fusion.3), channel_id=1, source_target_pairs={{0,8},{4,12},{8,0},{12,4},{16,24},{20,28},{24,16},{28,20},{1,9},{5... | collective-permute-start | bytes 3145736 | tf_op jit(solution)/shard_map/ppermute | solution.py:18
  130.9 51.9 %collective-permute-start.1 = (bf16[1024,512]{0,1:T(8,128)(2,1)}, bf16[1024,512]{0,1:T(8,128)(2,1)}, u32[]{:S(2)}, u32[]{:S(2)}) collective-permute-start(bf16[1024,512]{0,1:T(8,128)(2,1)} %pad_maximum_fusion.2), channel_id=1, source_target_pairs={{0,8},{4,12},{8,0},{12,4},{16,24},{20,28},{24,16},{28,20},{1,9},{5... | collective-permute-start | bytes 3145736 | tf_op jit(solution)/shard_map/ppermute | solution.py:18
  131.5 165.7 %reduce-scatter.49.cloned.1.call-start = ((), (), s32[]{:S(2)}) async-start(), calls=%async_computation.30 | async-start | bytes 163840
  228.0 113.6 %copy-start.10 = (bf16[128,2048]{1,0:T(8,128)(2,1)S(1)}, bf16[128,2048]{1,0:T(8,128)(2,1)}, u32[]{:S(2)}) copy-start(bf16[128,2048]{1,0:T(8,128)(2,1)} %param.36) | copy-start | bytes 1572868
  228.0 113.6 %copy-start.42 = (f32[2048]{0:T(1024)S(1)}, f32[2048]{0:T(1024)}, u32[]{:S(2)}) copy-start(f32[2048]{0:T(1024)} %param.42) | copy-start | bytes 24580
  228.0 113.5 %reduce-scatter.37.cloned.1.call-start = ((), (), s32[]{:S(2)}) async-start(), calls=%async_computation.19 | async-start | bytes 2621440 | tf_op jit(solution)/shard_map/reduce_scatter | solution.py:355
  232.5 111.7 %copy-start.39 = (f32[2048]{0:T(1024)S(1)}, f32[2048]{0:T(1024)}, u32[]{:S(2)}) copy-start(f32[2048]{0:T(1024)} %param.43) | copy-start | bytes 24580
  232.5 111.7 %copy-start.43 = (f32[2048]{0:T(1024)S(1)}, f32[2048]{0:T(1024)}, u32[]{:S(2)}) copy-start(f32[2048]{0:T(1024)} %param.44) | copy-start | bytes 24580
  232.5 155.8 %all-gather.21.cloned.1.call-start = ((), (), s32[]{:S(2)}) async-start(), calls=%async_computation.24 | async-start | bytes 2621440 | tf_op jit(solution)/shard_map/all_gather | solution.py:410
  233.1 212.2 %all-gather.19.cloned.1.call-start = ((), (), s32[]{:S(2)}) async-start(), calls=%async_computation.22 | async-start | bytes 9437184 | tf_op jit(solution)/shard_map/all_gather | solution.py:311
  233.8 267.8 %all-gather.17.cloned.1.call-start = ((), (), s32[]{:S(2)}) async-start(), calls=%async_computation.21 | async-start | bytes 9437184 | tf_op jit(solution)/shard_map/all_gather | solution.py:310
  234.6 314.6 %all-gather.15.cloned.1.call-start = ((), (), s32[]{:S(2)}) async-start(), calls=%async_computation.20 | async-start | bytes 2621440 | tf_op jit(solution)/shard_map/all_gather | solution.py:370
  345.2 247.2 %reduce-scatter.53.cloned.1.call-start = ((), (), s32[]{:S(2)}) async-start(), calls=%async_computation.32 | async-start | bytes 163840
  358.7 209.9 %copy-start.35 = (bf16[512,16]{0,1:T(8,128)(2,1)}, bf16[512,16]{0,1:T(8,128)(2,1)S(1)}, u32[]{:S(2)}) copy-start(bf16[512,16]{0,1:T(8,128)(2,1)S(1)} %all_gather.49) | copy-start | bytes 49156
  358.7 97.2 %copy-start.20 = (bf16[128,2048]{1,0:T(8,128)(2,1)S(1)}, bf16[128,2048]{1,0:T(8,128)(2,1)}, u32[]{:S(2)}) copy-start(bf16[128,2048]{1,0:T(8,128)(2,1)} %add_convert_fusion.4) | copy-start | bytes 1572868
  468.9 87.9 %copy-start.37 = (bf16[512,16]{0,1:T(8,128)(2,1)}, bf16[512,16]{0,1:T(8,128)(2,1)S(1)}, u32[]{:S(2)}) copy-start(bf16[512,16]{0,1:T(8,128)(2,1)S(1)} %all_gather.46) | copy-start | bytes 49156
  468.9 87.9 %copy-start.52 = (f32[2048]{0:T(1024)S(1)}, f32[2048]{0:T(1024)}, u32[]{:S(2)}) copy-start(f32[2048]{0:T(1024)} %param.46) | copy-start | bytes 24580
  574.5 62.5 %reduce-scatter.41.cloned.1.call-start = ((), (), s32[]{:S(2)}) async-start(), calls=%async_computation.25 | async-start | bytes 2621440 | tf_op jit(solution)/shard_map/reduce_scatter | solution.py:427
  584.5 101.2 %all-gather.23.cloned.1.call-start = ((), (), s32[]{:S(2)}) async-start(), calls=%async_computation.26 | async-start | bytes 2621440 | tf_op jit(solution)/shard_map/all_gather | solution.py:444
  640.3 185.7 %reduce-scatter.51.cloned.1.call-start = ((), (), s32[]{:S(2)}) async-start(), calls=%async_computation.31 | async-start | bytes 163840
  722.7 46.5 %collective-permute-start.6 = (bf16[1024,512]{0,1:T(8,128)(2,1)S(1)}, bf16[1024,512]{0,1:T(8,128)(2,1)S(1)}, u32[]{:S(2)}, u32[]{:S(2)}) collective-permute-start(bf16[1024,512]{0,1:T(8,128)(2,1)S(1)} %select_convert_fusion), channel_id=1, source_target_pairs={{0,8},{4,12},{8,0},{12,4},{16,24},{20,28},{24,16},{28,20},{1,9},{5... | collective-permute-start | bytes 3145736 | tf_op jit(solution)/shard_map/ppermute | solution.py:18
  758.9 33.6 %collective-permute-start.4 = (bf16[1024,512]{0,1:T(8,128)(2,1)S(1)}, bf16[1024,512]{0,1:T(8,128)(2,1)S(1)}, u32[]{:S(2)}, u32[]{:S(2)}) collective-permute-start(bf16[1024,512]{0,1:T(8,128)(2,1)S(1)} %select_convert_fusion.1), channel_id=1, source_target_pairs={{0,8},{4,12},{8,0},{12,4},{16,24},{20,28},{24,16},{28,20},{1,9},{5... | collective-permute-start | bytes 3145736 | tf_op jit(solution)/shard_map/ppermute | solution.py:18
  770.1 37.1 %collective-permute-start.7 = (bf16[512,512]{0,1:T(8,128)(2,1)S(1)}, bf16[512,512]{0,1:T(8,128)(2,1)}, u32[]{:S(2)}, u32[]{:S(2)}) collective-permute-start(bf16[512,512]{0,1:T(8,128)(2,1)S(1)} %select_convert_fusion.2), channel_id=1, source_target_pairs={{0,4},{4,0},{8,12},{12,8},{16,20},{20,16},{24,28},{28,24},{1,5},{5... | collective-permute-start | bytes 1572872 | tf_op jit(solution)/shard_map/ppermute | solution.py:18
  794.6 14.8 collective-permute-start.5
  807.2 39.0 %reduce-scatter.55.cloned.1.call-start = ((), (), s32[]{:S(2)}) async-start(), calls=%async_computation.33 | async-start | bytes 163840
  814.3 142.6 %reduce-scatter.39.cloned.1.call-start = ((), (), s32[]{:S(2)}) async-start(), calls=%async_computation.23 | async-start | bytes 2621440 | tf_op jit(solution)/shard_map/reduce_scatter | solution.py:382
  824.5 202.8 %reduce-scatter.57.cloned.1.call-start = ((), (), s32[]{:S(2)}) async-start(), calls=%async_computation.34 | async-start | bytes 1081344
  862.7 299.5 %reduce-scatter.61.cloned.1.call-start = ((), (), s32[]{:S(2)}) async-start(), calls=%async_computation.36 | async-start | bytes 1081344
  875.4 420.9 %reduce-scatter.63.cloned.1.call-start = ((), (), s32[]{:S(2)}) async-start(), calls=%async_computation.37 | async-start | bytes 1081344
  886.6 543.9 %reduce-scatter.65.cloned.1.call-start = ((), (), s32[]{:S(2)}) async-start(), calls=%async_computation.38 | async-start | bytes 1081344
  897.8 667.0 %reduce-scatter.67.cloned.1.call-start = ((), (), s32[]{:S(2)}) async-start(), calls=%async_computation.39 | async-start | bytes 1081344
  909.1 759.3 %reduce-scatter.59.cloned.1.call-start = ((), (), s32[]{:S(2)}) async-start(), calls=%async_computation.35 | async-start | bytes 3244032
  941.7 771.9 %reduce-scatter.43.cloned.1.call-start = ((), (), s32[]{:S(2)}) async-start(), calls=%async_computation.27 | async-start | bytes 2621440 | tf_op jit(solution)/shard_map/reduce_scatter | solution.py:484
  949.3 914.6 %reduce-scatter.45.cloned.1.call-start = ((), (), s32[]{:S(2)}) async-start(), calls=%async_computation.28 | async-start | bytes 4325376 | tf_op jit(solution)/shard_map/reduce_scatter | solution.py:523
  956.3 1056.9 %reduce-scatter.47.cloned.1.call-start = ((), (), s32[]{:S(2)}) async-start(), calls=%async_computation.29 | async-start | bytes 4325376 | tf_op jit(solution)/shard_map/reduce_scatter | solution.py:529
  956.9 756.7 %copy-start.11 = (bf16[128,2048]{1,0:T(8,128)(2,1)S(1)}, bf16[128,2048]{1,0:T(8,128)(2,1)}, u32[]{:S(2)}) copy-start(bf16[128,2048]{1,0:T(8,128)(2,1)} %param.36) | copy-start | bytes 1572868
  956.9 756.7 %copy-start.40 = (bf16[128,16]{1,0:T(8,128)(2,1)S(1)}, bf16[128,16]{1,0:T(8,128)(2,1)}, u32[]{:S(2)}) copy-start(bf16[128,16]{1,0:T(8,128)(2,1)} %reduce-scatter.55.cloned.1.call-done) | copy-start | bytes 12292
  956.9 756.7 %copy-start.45 = (f32[2048]{0:T(1024)S(1)}, f32[2048]{0:T(1024)}, u32[]{:S(2)}) copy-start(f32[2048]{0:T(1024)} %param.37) | copy-start | bytes 24580
  956.9 756.7 %copy-start.47 = (f32[128]{0:T(128)S(1)}, f32[128]{0:T(128)}, u32[]{:S(2)}) copy-start(f32[128]{0:T(128)} %copy-done.46) | copy-start | bytes 1540
  957.0 756.7 %copy-start.50 = (f32[128]{0:T(128)S(1)}, f32[128]{0:T(128)}, u32[]{:S(2)}) copy-start(f32[128]{0:T(128)} %copy-done.49) | copy-start | bytes 1540
  1431.4 581.8 %copy-start.1 = (bf16[8,16,8192]{2,1,0:T(8,128)(2,1)S(1)}, bf16[8,16,8192]{2,1,0:T(8,128)(2,1)}, u32[]{:S(2)}) copy-start(bf16[8,16,8192]{2,1,0:T(8,128)(2,1)} %param.54) | copy-start | bytes 6291460
  (38 other events, 530.2 us)
Sparse Core Ops, SparseCore 0:
  12.9 48.7 all-gather.8
  63.6 44.2 all-gather.10
  131.6 36.3 all-gather.12
  228.1 69.0 reduce-scatter.48
  299.5 42.0 reduce-scatter.36
  343.0 45.3 all-gather.20
  390.2 55.0 all-gather.18
  447.2 54.3 all-gather.16
  503.2 45.9 all-gather.14
  574.6 17.7 reduce-scatter.52
  594.9 42.1 reduce-scatter.40
  640.4 45.2 all-gather.22
  807.3 18.5 reduce-scatter.50
  828.7 17.4 reduce-scatter.54
  848.4 41.9 reduce-scatter.38
  892.6 134.6 reduce-scatter.56
  1030.0 132.1 reduce-scatter.60
  1164.4 131.8 reduce-scatter.62
  1298.5 131.9 reduce-scatter.64
  1432.7 132.0 reduce-scatter.66
  1570.2 98.1 reduce-scatter.58
  1670.7 42.8 reduce-scatter.42
  1716.5 147.2 reduce-scatter.44
  1866.6 146.4 reduce-scatter.46
where the time goes:
time: 2030 us; the launch traced here: 2020 us
  waiting for transfers between devices  1560 us (77%)
  local copies, waits for them, and re-layouts  128 us (6%)
  matrix products  122 us (6%)
  starting transfers between devices  71 us (3%)
  other arithmetic  66.2 us (3%)
  blocking collectives  49.7 us (2%)
    unnamed x34, waiting for transfers between devices  792 us
    reduce_scatter x1, waiting for transfers between devices, local(): lax.psum_scatter(stacked(widened(down_fc2_grad, fc2_down.shape[2], hidden...  149 us
    reduce_scatter x1, waiting for transfers between devices, local(): lax.psum_scatter(stacked(widened(first_feed_raise_gradient, fc1_up.shape[...  146 us
    unnamed x134, local copies, waits for them, and re-layouts  109 us
    ppermute x8, starting transfers between devices, partner(): lax.ppermute(array, axis, [(i, i ^ 1 << distance) for i in range(lax.axis...  69 us
    ppermute x8, waiting for transfers between devices, partner(): lax.ppermute(array, axis, [(i, i ^ 1 << distance) for i in range(lax.axis...  62.3 us
    all_gather x1, waiting for transfers between devices, local(): lax.all_gather(fc2_weight, 'dp', axis=1, tiled=True)  57 us
    dot_general x12, matrix products, dense_product(): return jnp.dot(left_side, right_side, preferred_element_type=jnp.float32)  54.4 us
  transfers between devices with their start and end apart: 32, of which 25 were waited for; matrix products, arithmetic and copies ran while one was open for 11% of the time, Pallas kernels for 0%

commit v1 on v0

v1 whole, which is shorter than its diff:
```python
import functools

import jax
import jax.numpy as jnp
from jax import lax
from jax.experimental import pallas as pl
from jax.experimental.pallas import tpu as pltpu
from jax.sharding import PartitionSpec as P

H = 32
HD = 64
ADAPTERS = 8
SEQ_DEVS = 4
PIC = 256
EPS = 1e-05
FACTOR = 0.5
BF = jnp.bfloat16
F32 = jnp.float32
BLOCK = 256
VMEM_BYTES = 56 * 1024 * 1024


def dot(a, b):
    return jnp.dot(a, b, preferred_element_type=F32)


def dot_nt(a, b):
    return lax.dot_general(a, b, (((1,), (1,)), ((), ())), preferred_element_type=F32)


def dot_tn(a, b):
    return lax.dot_general(a, b, (((0,), (0,)), ((), ())), preferred_element_type=F32)


def gelu_and_slope(f):
    phi = 0.5 * (1.0 + lax.erf(f * (0.5**0.5)))
    density = jnp.exp(-0.5 * f * f) * (0.5 / jnp.pi) ** 0.5
    return f * phi, phi + f * density


def norm_forward(values, gain, shift):
    centred = values - jnp.mean(values, axis=-1, keepdims=True)
    inverse = lax.rsqrt(jnp.mean(centred * centred, axis=-1, keepdims=True) + EPS)
    unit = centred * inverse
    return unit * gain + shift, unit, inverse


def norm_backward(upstream, unit, inverse, gain):
    scaled = upstream * gain
    return inverse * (
        scaled
        - jnp.mean(scaled, axis=-1, keepdims=True)
        - unit * jnp.mean(scaled * unit, axis=-1, keepdims=True)
    )


def shift_one(array, axis):
    n = lax.axis_size(axis)
    return lax.ppermute(array, axis, [(i, (i + 1) % n) for i in range(n)])


def ring_gather(array, axis):
    pieces = [array]
    for _ in range(lax.axis_size(axis) - 1):
        pieces.append(shift_one(pieces[-1], axis))
    return pieces


def ring_scatter(pieces, axis):
    total = pieces[1].astype(BF)
    for piece in pieces[2:] + pieces[:1]:
        total = shift_one(total, axis).astype(F32) + piece.astype(F32)
        if piece is not pieces[0]:
            total = total.astype(BF)
    return total


def exchange(array, distance):
    n = lax.axis_size("dp")
    return lax.ppermute(array, "dp", [(i, i ^ distance) for i in range(n)])


def span_of(positions, meta_ref, spans, outside):
    label = jnp.full(positions.shape, outside, jnp.int32)
    for j in range(spans):
        start = meta_ref[2 + j]
        label = jnp.where((positions >= start) & (positions < start + PIC), j, label)
    return label


def allowed_block(i, j, meta_ref, spans):
    key_pos = j * BLOCK + lax.broadcasted_iota(jnp.int32, (BLOCK, BLOCK), 0)
    row_pos = i * BLOCK + lax.broadcasted_iota(jnp.int32, (BLOCK, BLOCK), 1)
    key_label = span_of(key_pos, meta_ref, spans, -1)
    row_label = span_of(row_pos, meta_ref, spans, -2)
    return (key_pos <= row_pos) | (key_label == row_label)


def crosses(i, meta_ref, spans):
    edge = (i + 1) * BLOCK
    found = jnp.bool_(False)
    for j in range(spans):
        start = meta_ref[2 + j]
        found = found | ((start < edge) & (edge < start + PIC))
    return found


def block_rows(i):
    return pl.ds(pl.multiple_of(i * BLOCK, BLOCK), BLOCK)


def reorder_starts(meta_ref, parts, ring, rows):
    part, spot = meta_ref[0], meta_ref[1]
    for e in range(parts):
        for k in range(ring):
            back = spot - k
            back = jnp.where(back < 0, back + ring, back)
            true_start = ((part ^ e) * ring + back) * rows
            yield e, k, pl.ds(pl.multiple_of(true_start, rows), rows)


def prepare_block(b, heads, qkv_ref, slope_ref, kaug_ref, qaug_ref):
    rows = block_rows(b)
    lane = lax.broadcasted_iota(jnp.int32, (BLOCK, HD), 1)
    pos = b * BLOCK + lax.broadcasted_iota(jnp.int32, (BLOCK, HD), 0)
    ones = jnp.where(lane < 3, 1.0, 0.0).astype(BF)
    for h in range(heads):
        at = h * 3 * HD
        query = qkv_ref[rows, at : at + HD] * jnp.asarray(0.125, BF)
        key = qkv_ref[rows, at + HD : at + 2 * HD]
        offset = pos.astype(F32) * (slope_ref[h] * 0.125)
        high = offset.astype(BF).astype(F32)
        middle = (offset - high).astype(BF).astype(F32)
        low = offset - high - middle
        extra = jnp.where(
            lane == 0, high, jnp.where(lane == 1, middle, jnp.where(lane == 2, low, 0.0))
        ).astype(BF)
        qaug_ref[h, rows, :] = jnp.concatenate([query, ones], axis=1)
        kaug_ref[h, rows, :] = jnp.concatenate([key, extra], axis=1)


def forward_kernel(heads, parts, ring, rows, spans, meta_ref, slope_ref, *refs):
    piece_refs = refs[:parts]
    ctx_ref, qkv_ref, out_t_ref, log_ref, kaug_ref, qaug_ref, vt_ref = refs[parts:]
    length = qkv_ref.shape[0]
    blocks = length // BLOCK
    for e, k, dst in reorder_starts(meta_ref, parts, ring, rows):
        qkv_ref[dst, :] = piece_refs[e][k * rows : (k + 1) * rows, :]
    eye = (
        lax.broadcasted_iota(jnp.int32, (HD, HD), 0) == lax.broadcasted_iota(jnp.int32, (HD, HD), 1)
    ).astype(BF)

    def prepare(b, unused):
        prepare_block(b, heads, qkv_ref, slope_ref, kaug_ref, qaug_ref)
        cols = block_rows(b)
        for h in range(heads):
            at = h * 3 * HD + 2 * HD
            value = qkv_ref[cols, at : at + HD]
            vt_ref[h, :HD, cols] = dot_nt(eye, value).astype(BF)
            row = lax.broadcasted_iota(jnp.int32, (16, BLOCK), 0)
            vt_ref[h, HD:, cols] = jnp.where(row == 0, 1.0, 0.0).astype(BF)
        return unused

    lax.fori_loop(0, blocks, prepare, 0)

    def one_row_block(i, unused):
        rows_i = block_rows(i)
        queries = [qaug_ref[h, rows_i, :] for h in range(heads)]

        def step(j, state, allowed=None):
            cols = block_rows(j)
            new_state = []
            for h in range(heads):
                scores = dot_nt(kaug_ref[h, cols, :], queries[h])
                if allowed is not None:
                    scores = jnp.where(allowed, scores, -1e30)
                top = jnp.max(scores, axis=0, keepdims=True)
                if state is not None:
                    old_top, old_sum = state[h]
                    top = jnp.maximum(top, old_top)
                weight = jnp.exp(scores - top).astype(BF)
                total = dot(vt_ref[h, :, cols], weight)
                if state is not None:
                    total = total + old_sum * jnp.exp(old_top - top)
                new_state.append((top, total))
            return tuple(new_state)

        state = step(i, None, allowed_block(i, i, meta_ref, spans))
        state = lax.fori_loop(0, i, step, state)
        state = lax.cond(
            crosses(i, meta_ref, spans),
            lambda s: step(i + 1, s, allowed_block(i, i + 1, meta_ref, spans)),
            lambda s: s,
            state,
        )
        outs = []
        for h in range(heads):
            top, total = state[h]
            amount = total[HD : HD + 1]
            outs.append(total[:HD] / amount)
            log_ref[h : h + 1, rows_i] = top + jnp.log(amount)
        if heads * HD < 128:
            outs.append(jnp.zeros((128 - heads * HD, BLOCK), F32))
        out_t = jnp.concatenate(outs, axis=0)
        out_t_ref[:, rows_i] = out_t
        turned = out_t.T.astype(BF)[:, : heads * HD]
        for part in range(BLOCK // rows):
            block = i * (BLOCK // rows) + part
            e = (block // ring) ^ meta_ref[0]
            k = meta_ref[1] - block % ring
            k = jnp.where(k < 0, k + ring, k)
            start = pl.multiple_of((e * ring + k) * rows, rows)
            ctx_ref[pl.ds(start, rows), :] = turned[part * rows : (part + 1) * rows]
        return unused

    lax.fori_loop(0, blocks, one_row_block, 0)


def backward_kernel(heads, parts, ring, rows, spans, meta_ref, slope_ref, *refs):
    piece_refs = refs[:parts]
    (
        qkv_ref,
        out_t_ref,
        log_ref,
        grad_ref,
        g_ref,
        kaug_ref,
        qaug_ref,
        kt_ref,
        gq_ref,
        gg_ref,
        delta_ref,
        dqt_ref,
        dkv_ref,
    ) = refs[parts:]
    length = qkv_ref.shape[0]
    blocks = length // BLOCK
    for e, k, dst in reorder_starts(meta_ref, parts, ring, rows):
        g_ref[dst, :] = piece_refs[e][k * rows : (k + 1) * rows, :]
    eye = (
        lax.broadcasted_iota(jnp.int32, (HD, HD), 0) == lax.broadcasted_iota(jnp.int32, (HD, HD), 1)
    ).astype(BF)

    def prepare(b, unused):
        prepare_block(b, heads, qkv_ref, slope_ref, kaug_ref, qaug_ref)
        cols = block_rows(b)
        blank = jnp.zeros((BLOCK, HD), BF)
        grad_t = g_ref[cols, :].astype(F32)
        if heads * HD < 128:
            grad_t = jnp.concatenate([grad_t, jnp.zeros((BLOCK, 128 - heads * HD), F32)], axis=1)
        product = grad_t.T * out_t_ref[:, cols]
        for h in range(heads):
            at = h * 3 * HD
            kt_ref[h, :, cols] = dot_nt(eye, qkv_ref[cols, at + HD : at + 2 * HD]).astype(BF)
            query = qkv_ref[cols, at : at + HD] * jnp.asarray(0.125, BF)
            gq_ref[h, cols, :] = jnp.concatenate([blank, query], axis=1)
            gg_ref[h, cols, :] = jnp.concatenate([g_ref[cols, h * HD : (h + 1) * HD], blank], axis=1)
            delta_ref[h : h + 1, cols] = jnp.sum(
                product[h * HD : (h + 1) * HD], axis=0, keepdims=True
            )
            dkv_ref[h, cols, :] = jnp.zeros((BLOCK, 2 * HD), F32)
        return unused

    lax.fori_loop(0, blocks, prepare, 0)

    def one_row_block(i, unused):
        rows_i = block_rows(i)

        def step(j, state, allowed=None):
            cols = block_rows(j)
            new_state = []
            for h in range(heads):
                at = h * 3 * HD + 2 * HD
                scores = dot_nt(kaug_ref[h, cols, :], qaug_ref[h, rows_i, :])
                if allowed is not None:
                    scores = jnp.where(allowed, scores, -1e30)
                weight = jnp.exp(scores - log_ref[h : h + 1, rows_i])
                grad_weight = dot_nt(
                    qkv_ref[cols, at : at + HD], g_ref[rows_i, h * HD : (h + 1) * HD]
                )
                grad_score = (weight * (grad_weight - delta_ref[h : h + 1, rows_i])).astype(BF)
                dkv_ref[h, cols, :] += dot(weight.astype(BF), gg_ref[h, rows_i, :]) + dot(
                    grad_score, gq_ref[h, rows_i, :]
                )
                new_state.append(state[h] + dot(kt_ref[h, :, cols], grad_score))
            return tuple(new_state)

        state = tuple(jnp.zeros((HD, BLOCK), F32) for _ in range(heads))
        state = step(i, state, allowed_block(i, i, meta_ref, spans))
        state = lax.fori_loop(0, i, step, state)
        state = lax.cond(
            crosses(i, meta_ref, spans),
            lambda s: step(i + 1, s, allowed_block(i, i + 1, meta_ref, spans)),
            lambda s: s,
            state,
        )
        outs = list(state)
        if heads * HD < 128:
            outs.append(jnp.zeros((128 - heads * HD, BLOCK), F32))
        dqt_ref[rows_i, :] = jnp.concatenate(outs, axis=0).T * 0.125
        return unused

    lax.fori_loop(0, blocks, one_row_block, 0)

    def write(b, unused):
        cols = block_rows(b)
        columns = []
        for h in range(heads):
            dkv = dkv_ref[h, cols, :]
            columns += [dqt_ref[cols, h * HD : (h + 1) * HD], dkv[:, HD:], dkv[:, :HD]]
        whole = jnp.concatenate(columns, axis=1).astype(BF)
        for part in range(BLOCK // rows):
            block = b * (BLOCK // rows) + part
            e = (block // ring) ^ meta_ref[0]
            k = meta_ref[1] - block % ring
            k = jnp.where(k < 0, k + ring, k)
            start = pl.multiple_of((e * ring + k) * rows, rows)
            grad_ref[pl.ds(start, rows), :] = whole[part * rows : (part + 1) * rows]
        return unused

    lax.fori_loop(0, blocks, write, 0)


def specs(count_smem, count_vmem):
    return [pl.BlockSpec(memory_space=pltpu.SMEM)] * count_smem + [
        pl.BlockSpec(memory_space=pltpu.VMEM)
    ] * count_vmem


def attend_forward(pieces, meta, slopes, ring, rows):
    heads = slopes.shape[0]
    parts = len(pieces)
    length = parts * pieces[0].shape[0]
    wide = max(128, heads * HD)
    return pl.pallas_call(
        functools.partial(forward_kernel, heads, parts, ring, rows, meta.shape[0] - 2),
        out_shape=(
            jax.ShapeDtypeStruct((length, heads * HD), BF),
            jax.ShapeDtypeStruct((length, heads * 3 * HD), BF),
            jax.ShapeDtypeStruct((wide, length), F32),
            jax.ShapeDtypeStruct((8, length), F32),
        ),
        in_specs=specs(2, parts),
        out_specs=tuple(specs(0, 4)),
        scratch_shapes=[
            pltpu.VMEM((heads, length, 128), BF),
            pltpu.VMEM((heads, length, 128), BF),
            pltpu.VMEM((heads, HD + 16, length), BF),
        ],
        compiler_params=pltpu.CompilerParams(vmem_limit_bytes=VMEM_BYTES),
        cost_estimate=pl.CostEstimate(
            flops=heads * length * length * HD * 8,
            bytes_accessed=length * heads * HD * 20,
            transcendentals=heads * length * length // 2,
        ),
    )(meta, slopes, *pieces)


def attend_backward(pieces, qkv, out_t, logs, meta, slopes, ring, rows):
    heads = slopes.shape[0]
    parts = len(pieces)
    length = qkv.shape[0]
    wide = max(128, heads * HD)
    return pl.pallas_call(
        functools.partial(backward_kernel, heads, parts, ring, rows, meta.shape[0] - 2),
        out_shape=jax.ShapeDtypeStruct((length, heads * 3 * HD), BF),
        in_specs=specs(2, parts + 3),
        out_specs=specs(0, 1)[0],
        scratch_shapes=[
            pltpu.VMEM((length, heads * HD), BF),
            pltpu.VMEM((heads, length, 128), BF),
            pltpu.VMEM((heads, length, 128), BF),
            pltpu.VMEM((heads, HD, length), BF),
            pltpu.VMEM((heads, length, 128), BF),
            pltpu.VMEM((heads, length, 128), BF),
            pltpu.VMEM((8, length), F32),
            pltpu.VMEM((length, wide), F32),
            pltpu.VMEM((heads, length, 128), F32),
        ],
        compiler_params=pltpu.CompilerParams(vmem_limit_bytes=VMEM_BYTES),
        cost_estimate=pl.CostEstimate(
            flops=heads * length * length * HD * 16,
            bytes_accessed=length * heads * HD * 20,
            transcendentals=heads * length * length // 2,
        ),
    )(meta, slopes, *pieces, qkv, out_t, logs)


def reduce_full_width(stacks, groups):
    ring, n = lax.axis_size("tensor"), lax.axis_size("dp")
    spot, data = lax.axis_index("tensor"), lax.axis_index("dp")
    group, part = data // SEQ_DEVS, data % SEQ_DEVS
    widths = [s.shape[1] // (ring * n) for s in stacks]
    rank = stacks[0].shape[0]
    joined = jnp.concatenate(
        [s.reshape(rank, groups, SEQ_DEVS, ring, w) for s, w in zip(stacks, widths)], axis=4
    )
    joined = jnp.transpose(joined, (3, 2, 1, 0, 4))

    def spot_block(k):
        return lax.dynamic_index_in_dim(joined, (spot + k) % ring, 0, keepdims=False)

    total = spot_block(0)
    for k in range(1, ring):
        moved = lax.ppermute(
            spot_block(k).astype(BF), "tensor", [(i, (i + k) % ring) for i in range(ring)]
        )
        total = total + moved.astype(F32)

    own = lax.dynamic_index_in_dim(total, part, 0, keepdims=False)
    for e in range(1, SEQ_DEVS):
        block = lax.dynamic_index_in_dim(total, part ^ e, 0, keepdims=False)
        own = own + exchange(block.astype(BF), e).astype(F32)
    pieces = [lax.dynamic_index_in_dim(own, group, 0, keepdims=False)]
    for k in range(1, groups):
        block = lax.dynamic_index_in_dim(own, (group + k) % groups, 0, keepdims=False)
        pieces.append(
            lax.ppermute(
                block.astype(BF), "dp", [(i, (i + k * SEQ_DEVS) % n) for i in range(n)]
            ).astype(F32)
        )
    return [(piece, (group - k) % groups) for k, piece in enumerate(pieces)], widths


def reduce_own_columns(stacks, groups):
    ring, n = lax.axis_size("tensor"), lax.axis_size("dp")
    spot, data = lax.axis_index("tensor"), lax.axis_index("dp")
    group, part = data // SEQ_DEVS, data % SEQ_DEVS
    widths = [s.shape[1] // n for s in stacks]
    rank = stacks[0].shape[0]
    joined = jnp.concatenate(
        [s.reshape(rank, SEQ_DEVS, groups, w) for s, w in zip(stacks, widths)], axis=3
    )
    joined = jnp.transpose(joined, (1, 2, 0, 3))
    own = lax.dynamic_index_in_dim(joined, part, 0, keepdims=False)
    for e in range(1, SEQ_DEVS):
        block = lax.dynamic_index_in_dim(joined, part ^ e, 0, keepdims=False)
        own = own + exchange(block.astype(BF), e).astype(F32)
    pieces = []
    mine = (data * ring + spot) % groups
    for k in range(groups):
        pairs = []
        for i in range(n):
            for z in range(ring):
                r = (i // SEQ_DEVS + k) % groups
                pairs.append((i * ring + z, z * n + (i % SEQ_DEVS) * groups + r))
        block = lax.dynamic_index_in_dim(own, (group + k) % groups, 0, keepdims=False)
        moved = lax.ppermute(block.astype(BF), ("dp", "tensor"), pairs).astype(F32)
        pieces.append((moved, (mine - k) % groups))
    return pieces, widths


def place(pieces, widths, seq_adapter):
    slots = jnp.arange(ADAPTERS, dtype=jnp.int32)
    whole = 0.0
    for piece, sequence in pieces:
        slot = lax.dynamic_index_in_dim(seq_adapter, sequence, 0, keepdims=False)
        whole = whole + jnp.where((slots == slot)[:, None, None], piece[None], 0.0)
    outs, at = [], 0
    for width in widths:
        outs.append(whole[:, :, at : at + width])
        at += width
    return outs


def local(
    hidden_in,
    ln1_gain,
    ln1_bias,
    qkv_weight,
    joined_bias,
    out_weight,
    output_bias,
    ln2_gain,
    ln2_bias,
    fc1_weight,
    first_feed_bias,
    fc2_weight,
    second_feed_bias,
    qkv_down,
    qkv_up,
    out_down,
    out_up,
    fc1_down,
    fc1_up,
    fc2_down,
    fc2_up,
    seq_adapter,
    span_starts,
    cotangent,
):
    spot = lax.axis_index("tensor")
    data = lax.axis_index("dp")
    ring = lax.axis_size("tensor")
    groups = lax.axis_size("dp") // SEQ_DEVS
    group, part = data // SEQ_DEVS, data % SEQ_DEVS
    rows = hidden_in.shape[0]
    slot = lax.dynamic_index_in_dim(seq_adapter, group, 0, keepdims=False)
    starts = lax.dynamic_index_in_dim(span_starts, group, 0, keepdims=False)
    qkv_cols, ctx_cols, hidden_cols = qkv_weight.shape[1], out_weight.shape[0], fc1_weight.shape[1]
    heads = qkv_cols // (3 * HD) // SEQ_DEVS
    meta = jnp.concatenate([jnp.stack([part, spot]), starts]).astype(jnp.int32)
    first_head = (spot * SEQ_DEVS + part) * heads
    slopes = jnp.exp2(
        -8.0 * ((first_head + jnp.arange(heads, dtype=jnp.int32)).astype(F32) + 1.0) / H
    )

    def pick(stack):
        return lax.dynamic_index_in_dim(stack, slot, 0, keepdims=False)

    def own_cols(matrix, count):
        return lax.dynamic_slice_in_dim(matrix, spot * count, count, 1)

    a_q, b_q = pick(qkv_down), own_cols(pick(qkv_up), qkv_cols)
    a_o, b_o = own_cols(pick(out_down), ctx_cols), pick(out_up)
    a_1, b_1 = pick(fc1_down), own_cols(pick(fc1_up), hidden_cols)
    a_2, b_2 = own_cols(pick(fc2_down), hidden_cols), pick(fc2_up)

    w_qkv = lax.all_gather(qkv_weight, "dp", axis=0, tiled=True)
    w_out = lax.all_gather(out_weight, "dp", axis=1, tiled=True)
    w_fc1 = lax.all_gather(fc1_weight, "dp", axis=0, tiled=True)
    w_fc2 = lax.all_gather(fc2_weight, "dp", axis=1, tiled=True)

    def split(array):
        return [array[k * rows : (k + 1) * rows] for k in range(ring)]

    def up(low, matrix):
        return FACTOR * dot(low.astype(BF), matrix)

    x = hidden_in.astype(F32)
    normed1, unit1, inverse1 = norm_forward(x, ln1_gain, ln1_bias)
    n1 = jnp.concatenate(ring_gather(normed1.astype(BF), "tensor"), axis=0)
    gy = jnp.concatenate(ring_gather(cotangent, "tensor"), axis=0)
    u1 = dot_nt(n1, a_q).astype(BF)
    qkv = (dot(n1, w_qkv) + up(u1, b_q) + joined_bias).astype(BF)
    pieces = []
    for e in range(SEQ_DEVS):
        piece = lax.dynamic_slice_in_dim(qkv, (part ^ e) * (heads * 3 * HD), heads * 3 * HD, 1)
        pieces.append(exchange(piece, e) if e else piece)
    ctx_rel, qkv_true, out_t, logs = attend_forward(pieces, meta, slopes, ring, rows)
    count = ring * rows
    ctx = jnp.zeros((count, ctx_cols), BF)
    for e in range(SEQ_DEVS):
        piece = ctx_rel[e * count : (e + 1) * count]
        piece = exchange(piece, e) if e else piece
        ctx = lax.dynamic_update_slice_in_dim(ctx, piece, (part ^ e) * (heads * HD), 1)
    u2 = dot_nt(ctx, a_o).astype(BF)
    part_out = (dot(ctx, w_out) + up(u2, b_o)).astype(BF)
    mid = x + (ring_scatter(split(part_out), "tensor") + output_bias)

    normed2, unit2, inverse2 = norm_forward(mid, ln2_gain, ln2_bias)
    n2 = jnp.concatenate(ring_gather(normed2.astype(BF), "tensor"), axis=0)
    u3 = dot_nt(n2, a_1).astype(BF)
    act, slope = gelu_and_slope(dot(n2, w_fc1) + up(u3, b_1) + first_feed_bias)
    act = act.astype(BF)
    u4 = dot_nt(act, a_2).astype(BF)
    part_mlp = (dot(act, w_fc2) + up(u4, b_2)).astype(BF)

    gu4 = (FACTOR * dot_nt(gy, b_2)).astype(BF)
    gact = dot_nt(gy, w_fc2) + dot(gu4, a_2)
    gf = (gact * slope).astype(BF)
    gu3 = (FACTOR * dot_nt(gf, b_1)).astype(BF)
    part_in2 = (dot_nt(gf, w_fc1) + dot(gu3, a_1)).astype(BF)
    grad_n2 = ring_scatter(split(part_in2), "tensor")
    grad_mid = cotangent.astype(F32) + norm_backward(grad_n2, unit2, inverse2, ln2_gain)
    gm = jnp.concatenate(ring_gather(grad_mid.astype(BF), "tensor"), axis=0)
    layer_output = (mid + (ring_scatter(split(part_mlp), "tensor") + second_feed_bias)).astype(BF)

    gu2 = (FACTOR * dot_nt(gm, b_o)).astype(BF)
    gctx = (dot_nt(gm, w_out) + dot(gu2, a_o)).astype(BF)
    pieces = []
    for e in range(SEQ_DEVS):
        piece = lax.dynamic_slice_in_dim(gctx, (part ^ e) * (heads * HD), heads * HD, 1)
        pieces.append(exchange(piece, e) if e else piece)
    grad_rel = attend_backward(pieces, qkv_true, out_t, logs, meta, slopes, ring, rows)
    gqkv = jnp.zeros((count, qkv_cols), BF)
    for e in range(SEQ_DEVS):
        piece = grad_rel[e * count : (e + 1) * count]
        piece = exchange(piece, e) if e else piece
        gqkv = lax.dynamic_update_slice_in_dim(gqkv, piece, (part ^ e) * (heads * 3 * HD), 1)
    gu1 = (FACTOR * dot_nt(gqkv, b_q)).astype(BF)
    part_in1 = (dot_nt(gqkv, w_qkv) + dot(gu1, a_q)).astype(BF)
    grad_n1 = ring_scatter(split(part_in1), "tensor")
    hidden_grad = grad_mid + norm_backward(grad_n1, unit1, inverse1, ln1_gain)

    full_pieces, full_widths = reduce_full_width(
        [dot_tn(gu1, n1), FACTOR * dot_tn(u2, gm), dot_tn(gu3, n2), FACTOR * dot_tn(u4, gy)], groups
    )
    g_aq, g_bo, g_a1, g_b2 = place(full_pieces, full_widths, seq_adapter)
    col_pieces, col_widths = reduce_own_columns(
        [FACTOR * dot_tn(u1, gqkv), dot_tn(gu2, ctx), FACTOR * dot_tn(u3, gf), dot_tn(gu4, act)],
        groups,
    )
    g_bq, g_ao, g_b1, g_a2 = place(col_pieces, col_widths, seq_adapter)
    return (layer_output, hidden_grad, g_aq, g_bq, g_ao, g_bo, g_a1, g_b1, g_a2, g_b2)


def solution(mesh):
    rows, cols = P(("dp", "tensor"), None), P(None, None, ("dp", "tensor"))
    placed = (
        rows,
        P(),
        P(),
        P("dp", "tensor"),
        P("tensor"),
        P("tensor", "dp"),
        P(),
        P(),
        P(),
        P("dp", "tensor"),
        P("tensor"),
        P("tensor", "dp"),
    ) + (P(),) * 11 + (rows,)
    return jax.shard_map(
        local,
        mesh=mesh,
        in_specs=placed,
        out_specs=(rows, rows) + (cols,) * 8,
        check_vma=False,
    )
```

time: 2030 us -> 572 us (0.28)
  waiting for transfers between devices: 1560 us -> 318 us
  local copies, waits for them, and re-layouts: 128 us -> 24.6 us
  Pallas kernels: 0 us -> 63.4 us
  other arithmetic: 66.2 us -> 13.4 us
  blocking collectives: 49.7 us -> 0 us
  starting transfers between devices: 71 us -> 29 us
  matrix products: 122 us -> 95.5 us
    unnamed x34 -> x4, waiting for transfers between devices: 792 us -> 2.58 us
    reduce_scatter x6 -> x0, waiting for transfers between devices: 427 us -> none  [the longest x1 149 us: local(): lax.psum_scatter(stacked(widened(down_fc2_grad, fc2_down.shape[2], hidden...]
    all_gather x8 -> x4, waiting for transfers between devices: 275 us -> 0.01 us  [the longest x1 0.01 us: local(): w_qkv = lax.all_gather(qkv_weight, 'dp', axis=0, tiled=True)]
    ppermute x8 -> x48, waiting for transfers between devices: 62.3 us -> 316 us  [the longest x24 254 us: shift_one(): return lax.ppermute(array, axis, [(i, (i + 1) % n) for i in range(n)])]
    unnamed x134 -> x119, local copies, waits for them, and re-layouts: 109 us -> 8.28 us
    pallas_call x0 -> x2, Pallas kernels: none -> 63.4 us  [the longest x1 32.5 us: attend_forward(): pl.pallas_call(functools.partial(forward_kernel, heads, parts, ring, rows...]
    all_gather x4 -> x0, blocking collectives: 49.7 us -> none  [the longest x1 13.8 us: local(): lax.all_gather(lowrank1, 'tensor', axis=0, tiled=True)]
    ppermute x8 -> x48, starting transfers between devices: 69 us -> 28.8 us  [the longest x18 11.7 us: exchange(): return lax.ppermute(array, 'dp', [(i, i ^ distance) for i in range(n)])]
  transfers between devices with their start and end apart: 32 -> 52, of which waited for: 25 -> 33; matrix products, arithmetic and copies ran while one was open for 11% -> 15% of each run, Pallas kernels for 0% -> 6%
where the time goes in v1:
time: 572 us; the launch traced here: 561 us
  waiting for transfers between devices  318 us (56%)
  matrix products  95.5 us (17%)
  Pallas kernels  63.4 us (11%)
  starting transfers between devices  29 us (5%)
  local copies, waits for them, and re-layouts  24.6 us (4%)
  between operations  17.1 us (3%)
  other arithmetic  13.4 us (2%)
    ppermute x24, waiting for transfers between devices, shift_one(): return lax.ppermute(array, axis, [(i, (i + 1) % n) for i in range(n)])  254 us
    ppermute x18, waiting for transfers between devices, exchange(): return lax.ppermute(array, 'dp', [(i, i ^ distance) for i in range(n)])  52.5 us
    dot_general x12, matrix products, dot(): return jnp.dot(a, b, preferred_element_type=F32)  47.4 us
    dot_general x12, matrix products, dot_nt(): lax.dot_general(a, b, (((1,), (1,)), ((), ())), preferred_element_type=F32)  40 us
    pallas_call x1, Pallas kernels, attend_forward(): pl.pallas_call(functools.partial(forward_kernel, heads, parts, ring, rows...  32.5 us
    pallas_call x1, Pallas kernels, attend_backward(): pl.pallas_call(functools.partial(backward_kernel, heads, parts, ring, row...  30.9 us
    ppermute x18, starting transfers between devices, exchange(): return lax.ppermute(array, 'dp', [(i, i ^ distance) for i in range(n)])  11.7 us
  transfers between devices with their start and end apart: 52, of which 33 were waited for; matrix products, arithmetic and copies ran while one was open for 15% of the time, Pallas kernels for 6%

profile of v1, /device:TPU:0, one launch (start us, length us, event | category | flops | bytes accessed | tf_op | source)
XLA Modules:
  0.0 561.4 jit_solution(7926393315277514758)
XLA Ops:
  10.9 3.1 collective-permute-start
  14.0 13.9 %collective-permute-done = bf16[128,2048]{1,0:T(8,128)(2,1)S(1)} collective-permute-done((bf16[128,2048]{1,0:T(8,128)(2,1)S(1)}, bf16[128,2048]{1,0:T(8,128)(2,1)S(1)}, u32[]{:S(2)}, u32[]{:S(2)}) %collective-permute-start) | collective-permute-done | bytes 524320 | tf_op jit(solution)/shard_map/ppermute | solution.py:59
  28.0 15.0 %collective-permute-done.1 = bf16[128,2048]{1,0:T(8,128)(2,1)} collective-permute-done((bf16[128,2048]{1,0:T(8,128)(2,1)S(1)}, bf16[128,2048]{1,0:T(8,128)(2,1)}, u32[]{:S(2)}, u32[]{:S(2)}) %collective-permute-start.1) | collective-permute-done | bytes 524320 | tf_op jit(solution)/shard_map/ppermute | solution.py:59
  45.6 11.7 %collective-permute-done.2 = bf16[128,2048]{1,0:T(8,128)(2,1)} collective-permute-done((bf16[128,2048]{1,0:T(8,128)(2,1)}, bf16[128,2048]{1,0:T(8,128)(2,1)}, u32[]{:S(2)}, u32[]{:S(2)}) %collective-permute-start.2) | collective-permute-done | bytes 524320 | tf_op jit(solution)/shard_map/ppermute | solution.py:59
  59.1 3.2 convolution_multiply_fusion
  62.4 7.4 %fusion.7 = bf16[512,1536]{1,0:T(8,128)(2,1)S(1)} fusion(f32[512,1536]{1,0:T(8,128)} %convolution_multiply_fusion, bf16[2048,1536]{1,0:T(8,128)(2,1)} %all-gather.5.cloned.1.call-done, f32[1536]{0:T(1024)S(1)} %copy-done.53, bf16[128,2048]{1,0:T(8,128)(2,1)} %collective-permute-done.2, bf16[128,2048]{1,0:T(8,128)(2,1)} %collective-permute-done.1, ...), kind=kOutput, calls=%fused_computation.17 | convolution fusion | flops 3231973376 | bytes 13113344 | tf_op jit(solution)/shard_map/dot_general | solution.py:24
  73.7 9.0 %collective-permute-done.4.refs_2_ = bf16[512,384]{1,0:T(8,128)(2,1)} collective-permute-done((bf16[512,384]{1,0:T(8,128)(2,1)S(1)}, bf16[512,384]{1,0:T(8,128)(2,1)}, u32[]{:S(2)}, u32[]{:S(2)}) %collective-permute-start.4) | collective-permute-done | bytes 393248 | tf_op jit(solution)/shard_map/ppermute | solution.py:80
  82.8 13.3 %collective-permute-done.5.refs_3_ = bf16[512,384]{1,0:T(8,128)(2,1)} collective-permute-done((bf16[512,384]{1,0:T(8,128)(2,1)S(1)}, bf16[512,384]{1,0:T(8,128)(2,1)}, u32[]{:S(2)}, u32[]{:S(2)}) %collective-permute-start.5) | collective-permute-done | bytes 393248 | tf_op jit(solution)/shard_map/ppermute | solution.py:80
  96.0 32.5 %shard_map.303 = (bf16[2048,128]{1,0:T(8,128)(2,1)}, bf16[2048,384]{1,0:T(8,128)(2,1)}, f32[128,2048]{1,0:T(8,128)}, f32[8,2048]{1,0:T(8,128)}) custom-call(s32[5]{0:T(128)} %pad_add_fusion.meta_ref, f32[2]{0:T(128)} %multiply_exponential_fusion.slope_ref, bf16[512,384]{1,0:T(8,128)(2,1)} %get-tuple-element.33.refs_0_, ...), custom_call_target="tpu_custom_call" | custom-call | flops 4294967296 | bytes 5242880 | tf_op jit(solution)/shard_map/pallas_call | solution.py:335
  131.7 7.4 %collective-permute-done.7 = bf16[512,128]{1,0:T(8,128)(2,1)S(1)} collective-permute-done((bf16[512,128]{1,0:T(8,128)(2,1)S(1)}, bf16[512,128]{1,0:T(8,128)(2,1)S(1)}, u32[]{:S(2)}, u32[]{:S(2)}) %collective-permute-start.7) | collective-permute-done | bytes 131104 | tf_op jit(solution)/shard_map/ppermute | solution.py:80
  139.2 4.7 collective-permute-done.8
  145.0 3.6 fusion.45
  148.6 4.1 add_convert_fusion.3
  154.0 15.4 %collective-permute-done.9 = bf16[128,2048]{1,0:T(8,128)(2,1)S(1)} collective-permute-done((bf16[128,2048]{1,0:T(8,128)(2,1)S(1)}, bf16[128,2048]{1,0:T(8,128)(2,1)S(1)}, u32[]{:S(2)}, u32[]{:S(2)}) %collective-permute-start.9) | collective-permute-done | bytes 524320 | tf_op jit(solution)/shard_map/ppermute | solution.py:59
  169.8 16.4 %collective-permute-done.10 = bf16[128,2048]{1,0:T(8,128)(2,1)S(1)} collective-permute-done((bf16[128,2048]{1,0:T(8,128)(2,1)S(1)}, bf16[128,2048]{1,0:T(8,128)(2,1)S(1)}, u32[]{:S(2)}, u32[]{:S(2)}) %collective-permute-start.10) | collective-permute-done | bytes 524320 | tf_op jit(solution)/shard_map/ppermute | solution.py:59
  186.4 11.0 %collective-permute-done.18 = bf16[128,2048]{1,0:T(8,128)(2,1)S(1)} collective-permute-done((bf16[128,2048]{1,0:T(8,128)(2,1)S(1)}, bf16[128,2048]{1,0:T(8,128)(2,1)S(1)}, u32[]{:S(2)}, u32[]{:S(2)}) %collective-permute-start.18) | collective-permute-done | bytes 524320 | tf_op jit(solution)/shard_map/ppermute | solution.py:59
  197.4 11.2 %collective-permute-done.11 = bf16[128,2048]{1,0:T(8,128)(2,1)S(1)} collective-permute-done((bf16[128,2048]{1,0:T(8,128)(2,1)S(1)}, bf16[128,2048]{1,0:T(8,128)(2,1)S(1)}, u32[]{:S(2)}, u32[]{:S(2)}) %collective-permute-start.11) | collective-permute-done | bytes 524320 | tf_op jit(solution)/shard_map/ppermute | solution.py:59
  210.4 9.6 %collective-permute-done.19 = bf16[128,2048]{1,0:T(8,128)(2,1)} collective-permute-done((bf16[128,2048]{1,0:T(8,128)(2,1)S(1)}, bf16[128,2048]{1,0:T(8,128)(2,1)}, u32[]{:S(2)}, u32[]{:S(2)}) %collective-permute-start.19) | collective-permute-done | bytes 524320 | tf_op jit(solution)/shard_map/ppermute | solution.py:59
  220.9 10.4 %collective-permute-done.12 = bf16[128,2048]{1,0:T(8,128)(2,1)} collective-permute-done((bf16[128,2048]{1,0:T(8,128)(2,1)}, bf16[128,2048]{1,0:T(8,128)(2,1)}, u32[]{:S(2)}, u32[]{:S(2)}) %collective-permute-start.12) | collective-permute-done | bytes 524320 | tf_op jit(solution)/shard_map/ppermute | solution.py:59
  235.1 7.4 %collective-permute-done.20 = bf16[128,2048]{1,0:T(8,128)(2,1)} collective-permute-done((bf16[128,2048]{1,0:T(8,128)(2,1)}, bf16[128,2048]{1,0:T(8,128)(2,1)}, u32[]{:S(2)}, u32[]{:S(2)}) %collective-permute-start.20) | collective-permute-done | bytes 524320 | tf_op jit(solution)/shard_map/ppermute | solution.py:59
  244.4 8.4 %collective-permute-done.13 = bf16[128,2048]{1,0:T(8,128)(2,1)S(1)} collective-permute-done((bf16[128,2048]{1,0:T(8,128)(2,1)}, bf16[128,2048]{1,0:T(8,128)(2,1)S(1)}, u32[]{:S(2)}, u32[]{:S(2)}) %collective-permute-start.13) | collective-permute-done | bytes 524320 | tf_op jit(solution)/shard_map/ppermute | solution.py:59
  255.2 3.6 fusion.36
  258.9 9.0 %collective-permute-done.14 = bf16[128,2048]{1,0:T(8,128)(2,1)S(1)} collective-permute-done((bf16[128,2048]{1,0:T(8,128)(2,1)S(1)}, bf16[128,2048]{1,0:T(8,128)(2,1)S(1)}, u32[]{:S(2)}, u32[]{:S(2)}) %collective-permute-start.14) | collective-permute-done | bytes 524320 | tf_op jit(solution)/shard_map/ppermute | solution.py:59
  270.0 2.7 fusion.40
  272.7 12.1 %multiply_convert_fusion = (bf16[512,2048]{1,0:T(8,128)(2,1)}, f32[512,2048]{1,0:T(8,128)}) fusion(f32[2048]{0:T(1024)S(1)} %copy-done.54, f32[512,2048]{1,0:T(8,128)} %fusion.40, bf16[2048,2048]{1,0:T(8,128)(2,1)} %all-gather.9.cloned.1.call-done, bf16[128,2048]{1,0:T(8,128)(2,1)} %copy-done.46, bf16[128,2048]{1,0:T(8,128)(2,1)} %copy-done.44, ...), kind=kOutput, calls=%fused_computation.10 | convolution fusion | flops 4311744512 | bytes 20979712 | tf_op jit(solution)/shard_map/dot_general | solution.py:24
  284.8 10.5 %fusion.5 = bf16[512,2048]{1,0:T(8,128)(2,1)S(1)} fusion(f32[512,2048]{1,0:T(8,128)} %get-tuple-element.66, f32[512,2048]{1,0:T(8,128)} %fusion.36, bf16[512,2048]{1,0:T(8,128)(2,1)} %constant_dynamic-update-slice_fusion.6, bf16[2048,2048]{1,0:T(8,128)(2,1)} %all-gather.11.cloned.1.call-done), kind=kOutput, calls=%fused_computation.6 | convolution fusion | flops 4306501632 | bytes 20971520 | tf_op jit(solution)/shard_map/dot_general | solution.py:28
  295.9 8.0 %fusion.109 = f32[512,2048]{1,0:T(8,128)S(1)} fusion(bf16[512,2048]{1,0:T(8,128)(2,1)S(1)} %fusion.5, bf16[2048,2048]{1,0:T(8,128)(2,1)} %all-gather.9.cloned.1.call-done), kind=kOutput, calls=%fused_computation.209 | convolution fusion | flops 4294967296 | bytes 14680064 | tf_op jit(solution)/shard_map/dot_general | solution.py:28
  306.3 4.6 fusion.108
  314.1 8.8 %collective-permute-done.21 = bf16[128,2048]{1,0:T(8,128)(2,1)S(1)} collective-permute-done((bf16[128,2048]{1,0:T(8,128)(2,1)S(1)}, bf16[128,2048]{1,0:T(8,128)(2,1)S(1)}, u32[]{:S(2)}, u32[]{:S(2)}) %collective-permute-start.21) | collective-permute-done | bytes 524320 | tf_op jit(solution)/shard_map/ppermute | solution.py:59
  323.1 11.0 %collective-permute-done.15 = bf16[128,2048]{1,0:T(8,128)(2,1)S(1)} collective-permute-done((bf16[128,2048]{1,0:T(8,128)(2,1)S(1)}, bf16[128,2048]{1,0:T(8,128)(2,1)S(1)}, u32[]{:S(2)}, u32[]{:S(2)}) %collective-permute-start.15) | collective-permute-done | bytes 524320 | tf_op jit(solution)/shard_map/ppermute | solution.py:59
  334.3 11.0 %collective-permute-done.22 = bf16[128,2048]{1,0:T(8,128)(2,1)S(1)} collective-permute-done((bf16[128,2048]{1,0:T(8,128)(2,1)S(1)}, bf16[128,2048]{1,0:T(8,128)(2,1)S(1)}, u32[]{:S(2)}, u32[]{:S(2)}) %collective-permute-start.22) | collective-permute-done | bytes 524320 | tf_op jit(solution)/shard_map/ppermute | solution.py:59
  345.6 11.0 %collective-permute-done.16 = bf16[128,2048]{1,0:T(8,128)(2,1)S(1)} collective-permute-done((bf16[128,2048]{1,0:T(8,128)(2,1)S(1)}, bf16[128,2048]{1,0:T(8,128)(2,1)S(1)}, u32[]{:S(2)}, u32[]{:S(2)}) %collective-permute-start.16) | collective-permute-done | bytes 524320 | tf_op jit(solution)/shard_map/ppermute | solution.py:59
  356.8 11.0 %collective-permute-done.23 = bf16[128,2048]{1,0:T(8,128)(2,1)S(1)} collective-permute-done((bf16[128,2048]{1,0:T(8,128)(2,1)S(1)}, bf16[128,2048]{1,0:T(8,128)(2,1)S(1)}, u32[]{:S(2)}, u32[]{:S(2)}) %collective-permute-start.23) | collective-permute-done | bytes 524320 | tf_op jit(solution)/shard_map/ppermute | solution.py:59
  368.2 8.1 %collective-permute-done.17 = bf16[128,2048]{1,0:T(8,128)(2,1)S(1)} collective-permute-done((bf16[128,2048]{1,0:T(8,128)(2,1)S(1)}, bf16[128,2048]{1,0:T(8,128)(2,1)S(1)}, u32[]{:S(2)}, u32[]{:S(2)}) %collective-permute-start.17) | collective-permute-done | bytes 524320 | tf_op jit(solution)/shard_map/ppermute | solution.py:59
  379.1 13.1 %collective-permute-done.24 = bf16[128,2048]{1,0:T(8,128)(2,1)S(1)} collective-permute-done((bf16[128,2048]{1,0:T(8,128)(2,1)S(1)}, bf16[128,2048]{1,0:T(8,128)(2,1)S(1)}, u32[]{:S(2)}, u32[]{:S(2)}) %collective-permute-start.24) | collective-permute-done | bytes 524320 | tf_op jit(solution)/shard_map/ppermute | solution.py:59
  398.0 6.4 %collective-permute-done.25 = bf16[128,2048]{1,0:T(8,128)(2,1)} collective-permute-done((bf16[128,2048]{1,0:T(8,128)(2,1)S(1)}, bf16[128,2048]{1,0:T(8,128)(2,1)}, u32[]{:S(2)}, u32[]{:S(2)}) %collective-permute-start.25) | collective-permute-done | bytes 524320 | tf_op jit(solution)/shard_map/ppermute | solution.py:59
  406.7 9.3 %collective-permute-done.26 = bf16[128,2048]{1,0:T(8,128)(2,1)S(1)} collective-permute-done((bf16[128,2048]{1,0:T(8,128)(2,1)}, bf16[128,2048]{1,0:T(8,128)(2,1)S(1)}, u32[]{:S(2)}, u32[]{:S(2)}) %collective-permute-start.26) | collective-permute-done | bytes 524320 | tf_op jit(solution)/shard_map/ppermute | solution.py:59
  419.0 2.5 fusion.8
  425.6 3.1 collective-permute-done.28.refs_2_
  430.7 30.9 %shard_map.304 = bf16[2048,384]{1,0:T(8,128)(2,1)} custom-call(s32[5]{0:T(128)} %pad_add_fusion.meta_ref, f32[2]{0:T(128)} %multiply_exponential_fusion.slope_ref, bf16[512,128]{1,0:T(8,128)(2,1)} %get-tuple-element.41.refs_0_, bf16[512,128]{1,0:T(8,128)(2,1)} %collective-permute-done.27.refs_1_, bf16[512,128]{1,0:T(8,128)(2,1)} %collective-permute-done.28.refs_2_, ...), custom_call_target="tpu_custom_call" | custom-call | flops 8589934592 | bytes 5242880 | tf_op jit(solution)/shard_map/pallas_call | solution.py:364
  469.8 6.7 %collective-permute-done.31 = bf16[512,384]{1,0:T(8,128)(2,1)} collective-permute-done((bf16[512,384]{1,0:T(8,128)(2,1)}, bf16[512,384]{1,0:T(8,128)(2,1)}, u32[]{:S(2)}, u32[]{:S(2)}) %collective-permute-start.31) | collective-permute-done | bytes 393248 | tf_op jit(solution)/shard_map/ppermute | solution.py:80
  477.6 6.1 %collective-permute-done.32 = bf16[512,384]{1,0:T(8,128)(2,1)} collective-permute-done((bf16[512,384]{1,0:T(8,128)(2,1)}, bf16[512,384]{1,0:T(8,128)(2,1)}, u32[]{:S(2)}, u32[]{:S(2)}) %collective-permute-start.32) | collective-permute-done | bytes 393248 | tf_op jit(solution)/shard_map/ppermute | solution.py:80
  488.1 6.5 %add_convert_fusion = bf16[512,2048]{1,0:T(8,128)(2,1)S(1)} fusion(f32[512,2048]{1,0:T(8,128)S(1)} %fusion.47, bf16[512,1536]{1,0:T(8,128)(2,1)S(1)} %constant_dynamic-update-slice_fusion, bf16[2048,1536]{1,0:T(8,128)(2,1)} %all-gather.5.cloned.1.call-done), kind=kOutput, calls=%fused_computation.7 | convolution fusion | flops 3223322624 | bytes 14155776 | tf_op jit(solution)/shard_map/dot_general | solution.py:28
  501.6 3.6 collective-permute-start.38
  508.8 5.7 %collective-permute-done.38 = bf16[4,2,16,256]{3,2,1,0:T(8,128)(2,1)S(1)} collective-permute-done((bf16[4,2,16,256]{3,2,1,0:T(8,128)(2,1)S(1)}, bf16[4,2,16,256]{3,2,1,0:T(8,128)(2,1)S(1)}, u32[]{:S(2)}, u32[]{:S(2)}) %collective-permute-start.38) | collective-permute-done | bytes 65568 | tf_op jit(solution)/shard_map/ppermute | solution.py:405
  515.2 3.7 collective-permute-done.37
  527.1 10.2 %collective-permute-done.34 = bf16[128,2048]{1,0:T(8,128)(2,1)S(1)} collective-permute-done((bf16[128,2048]{1,0:T(8,128)(2,1)S(1)}, bf16[128,2048]{1,0:T(8,128)(2,1)S(1)}, u32[]{:S(2)}, u32[]{:S(2)}) %collective-permute-start.34) | collective-permute-done | bytes 524320 | tf_op jit(solution)/shard_map/ppermute | solution.py:59
  538.4 14.2 %collective-permute-done.35 = bf16[128,2048]{1,0:T(8,128)(2,1)S(1)} collective-permute-done((bf16[128,2048]{1,0:T(8,128)(2,1)S(1)}, bf16[128,2048]{1,0:T(8,128)(2,1)S(1)}, u32[]{:S(2)}, u32[]{:S(2)}) %collective-permute-start.35) | collective-permute-done | bytes 524320 | tf_op jit(solution)/shard_map/ppermute | solution.py:59
  (298 shorter events, 91.5 us)
Async XLA Ops:
  7.2 55.1 %all-gather.5.cloned.1.call-start = ((), (), s32[]{:S(2)}) async-start(), calls=%async_computation | async-start | bytes 7077888 | tf_op jit(solution)/shard_map/all_gather | solution.py:519
  8.0 140.6 %all-gather.7.cloned.1.call-start = ((), (), s32[]{:S(2)}) async-start(), calls=%async_computation.1 | async-start | bytes 2359296 | tf_op jit(solution)/shard_map/all_gather | solution.py:520
  8.7 263.9 %all-gather.9.cloned.1.call-start = ((), (), s32[]{:S(2)}) async-start(), calls=%async_computation.2 | async-start | bytes 9437184 | tf_op jit(solution)/shard_map/all_gather | solution.py:521
  9.5 275.3 %all-gather.11.cloned.1.call-start = ((), (), s32[]{:S(2)}) async-start(), calls=%async_computation.3 | async-start | bytes 9437184 | tf_op jit(solution)/shard_map/all_gather | solution.py:522
  10.9 17.0 %collective-permute-start = (bf16[128,2048]{1,0:T(8,128)(2,1)S(1)}, bf16[128,2048]{1,0:T(8,128)(2,1)S(1)}, u32[]{:S(2)}, u32[]{:S(2)}) collective-permute-start(bf16[128,2048]{1,0:T(8,128)(2,1)S(1)} %fusion.19), channel_id=1, source_target_pairs={{0,1},{1,2},{2,3},{3,0},{4,5},{5,6},{6,7},{7,4},{8,9},{9,10},{10,1... | collective-permute-start | bytes 1572872 | tf_op jit(solution)/shard_map/ppermute | solution.py:59
  28.0 15.0 %collective-permute-start.1 = (bf16[128,2048]{1,0:T(8,128)(2,1)S(1)}, bf16[128,2048]{1,0:T(8,128)(2,1)}, u32[]{:S(2)}, u32[]{:S(2)}) collective-permute-start(bf16[128,2048]{1,0:T(8,128)(2,1)S(1)} %collective-permute-done), channel_id=1, source_target_pairs={{0,1},{1,2},{2,3},{3,0},{4,5},{5,6},{6,7},{7,4},{8,9},{9,10},{10,1... | collective-permute-start | bytes 1572872 | tf_op jit(solution)/shard_map/ppermute | solution.py:59
  43.0 14.3 %collective-permute-start.2 = (bf16[128,2048]{1,0:T(8,128)(2,1)}, bf16[128,2048]{1,0:T(8,128)(2,1)}, u32[]{:S(2)}, u32[]{:S(2)}) collective-permute-start(bf16[128,2048]{1,0:T(8,128)(2,1)} %collective-permute-done.1), channel_id=1, source_target_pairs={{0,1},{1,2},{2,3},{3,0},{4,5},{5,6},{6,7},{7,4},{8,9},{9,10},{10,1... | collective-permute-start | bytes 1572872 | tf_op jit(solution)/shard_map/ppermute | solution.py:59
  70.7 12.0 %collective-permute-start.4 = (bf16[512,384]{1,0:T(8,128)(2,1)S(1)}, bf16[512,384]{1,0:T(8,128)(2,1)}, u32[]{:S(2)}, u32[]{:S(2)}) collective-permute-start(bf16[512,384]{1,0:T(8,128)(2,1)S(1)} %get-tuple-element.31), channel_id=1, source_target_pairs={{0,8},{4,12},{8,0},{12,4},{16,24},{20,28},{24,16},{28,20},{1,9},{5... | collective-permute-start | bytes 1179656 | tf_op jit(solution)/shard_map/ppermute | solution.py:80
  71.8 24.2 %collective-permute-start.5 = (bf16[512,384]{1,0:T(8,128)(2,1)S(1)}, bf16[512,384]{1,0:T(8,128)(2,1)}, u32[]{:S(2)}, u32[]{:S(2)}) collective-permute-start(bf16[512,384]{1,0:T(8,128)(2,1)S(1)} %get-tuple-element.30), channel_id=1, source_target_pairs={{0,12},{4,8},{8,4},{12,0},{16,28},{20,24},{24,20},{28,16},{1,13},{... | collective-permute-start | bytes 1179656 | tf_op jit(solution)/shard_map/ppermute | solution.py:80
  130.0 9.1 %collective-permute-start.7 = (bf16[512,128]{1,0:T(8,128)(2,1)S(1)}, bf16[512,128]{1,0:T(8,128)(2,1)S(1)}, u32[]{:S(2)}, u32[]{:S(2)}) collective-permute-start(bf16[512,128]{1,0:T(8,128)(2,1)S(1)} %get-tuple-element.43), channel_id=1, source_target_pairs={{0,8},{4,12},{8,0},{12,4},{16,24},{20,28},{24,16},{28,20},{1,9},{5... | collective-permute-start | bytes 393224 | tf_op jit(solution)/shard_map/ppermute | solution.py:80
  131.2 12.8 %collective-permute-start.8 = (bf16[512,128]{1,0:T(8,128)(2,1)S(1)}, bf16[512,128]{1,0:T(8,128)(2,1)S(1)}, u32[]{:S(2)}, u32[]{:S(2)}) collective-permute-start(bf16[512,128]{1,0:T(8,128)(2,1)S(1)} %get-tuple-element.42), channel_id=1, source_target_pairs={{0,12},{4,8},{8,4},{12,0},{16,28},{20,24},{24,20},{28,16},{1,13},{... | collective-permute-start | bytes 393224 | tf_op jit(solution)/shard_map/ppermute | solution.py:80
  152.8 16.6 %collective-permute-start.9 = (bf16[128,2048]{1,0:T(8,128)(2,1)S(1)}, bf16[128,2048]{1,0:T(8,128)(2,1)S(1)}, u32[]{:S(2)}, u32[]{:S(2)}) collective-permute-start(bf16[128,2048]{1,0:T(8,128)(2,1)S(1)} %slice.128), channel_id=1, source_target_pairs={{0,1},{1,2},{2,3},{3,0},{4,5},{5,6},{6,7},{7,4},{8,9},{9,10},{10,1... | collective-permute-start | bytes 1572872 | tf_op jit(solution)/shard_map/ppermute | solution.py:59
  169.6 16.6 %collective-permute-start.10 = (bf16[128,2048]{1,0:T(8,128)(2,1)S(1)}, bf16[128,2048]{1,0:T(8,128)(2,1)S(1)}, u32[]{:S(2)}, u32[]{:S(2)}) collective-permute-start(bf16[128,2048]{1,0:T(8,128)(2,1)S(1)} %add_convert_fusion.13), channel_id=1, source_target_pairs={{0,1},{1,2},{2,3},{3,0},{4,5},{5,6},{6,7},{7,4},{8,9},{9,10},{10,1... | collective-permute-start | bytes 1572872 | tf_op jit(solution)/shard_map/ppermute | solution.py:59
  169.7 27.8 %collective-permute-start.18 = (bf16[128,2048]{1,0:T(8,128)(2,1)S(1)}, bf16[128,2048]{1,0:T(8,128)(2,1)S(1)}, u32[]{:S(2)}, u32[]{:S(2)}) collective-permute-start(bf16[128,2048]{1,0:T(8,128)(2,1)S(1)} %copy-done.15), channel_id=1, source_target_pairs={{0,1},{1,2},{2,3},{3,0},{4,5},{5,6},{6,7},{7,4},{8,9},{9,10},{10,1... | collective-permute-start | bytes 1572872 | tf_op jit(solution)/shard_map/ppermute | solution.py:59
  186.4 22.3 %collective-permute-start.11 = (bf16[128,2048]{1,0:T(8,128)(2,1)S(1)}, bf16[128,2048]{1,0:T(8,128)(2,1)S(1)}, u32[]{:S(2)}, u32[]{:S(2)}) collective-permute-start(bf16[128,2048]{1,0:T(8,128)(2,1)S(1)} %add_convert_fusion.12), channel_id=1, source_target_pairs={{0,1},{1,2},{2,3},{3,0},{4,5},{5,6},{6,7},{7,4},{8,9},{9,10},{10,1... | collective-permute-start | bytes 1572872 | tf_op jit(solution)/shard_map/ppermute | solution.py:59
  197.4 22.6 %collective-permute-start.19 = (bf16[128,2048]{1,0:T(8,128)(2,1)S(1)}, bf16[128,2048]{1,0:T(8,128)(2,1)}, u32[]{:S(2)}, u32[]{:S(2)}) collective-permute-start(bf16[128,2048]{1,0:T(8,128)(2,1)S(1)} %collective-permute-done.18), channel_id=1, source_target_pairs={{0,1},{1,2},{2,3},{3,0},{4,5},{5,6},{6,7},{7,4},{8,9},{9,10},{10,1... | collective-permute-start | bytes 1572872 | tf_op jit(solution)/shard_map/ppermute | solution.py:59
  210.4 20.9 %collective-permute-start.12 = (bf16[128,2048]{1,0:T(8,128)(2,1)}, bf16[128,2048]{1,0:T(8,128)(2,1)}, u32[]{:S(2)}, u32[]{:S(2)}) collective-permute-start(bf16[128,2048]{1,0:T(8,128)(2,1)} %add_convert_fusion.11), channel_id=1, source_target_pairs={{0,1},{1,2},{2,3},{3,0},{4,5},{5,6},{6,7},{7,4},{8,9},{9,10},{10,1... | collective-permute-start | bytes 1572872 | tf_op jit(solution)/shard_map/ppermute | solution.py:59
  220.0 22.5 %collective-permute-start.20 = (bf16[128,2048]{1,0:T(8,128)(2,1)}, bf16[128,2048]{1,0:T(8,128)(2,1)}, u32[]{:S(2)}, u32[]{:S(2)}) collective-permute-start(bf16[128,2048]{1,0:T(8,128)(2,1)} %collective-permute-done.19), channel_id=1, source_target_pairs={{0,1},{1,2},{2,3},{3,0},{4,5},{5,6},{6,7},{7,4},{8,9},{9,10},{10,1... | collective-permute-start | bytes 1572872 | tf_op jit(solution)/shard_map/ppermute | solution.py:59
  231.3 21.5 %collective-permute-start.13 = (bf16[128,2048]{1,0:T(8,128)(2,1)}, bf16[128,2048]{1,0:T(8,128)(2,1)S(1)}, u32[]{:S(2)}, u32[]{:S(2)}) collective-permute-start(bf16[128,2048]{1,0:T(8,128)(2,1)} %collective-permute-done.12), channel_id=1, source_target_pairs={{0,1},{1,2},{2,3},{3,0},{4,5},{5,6},{6,7},{7,4},{8,9},{9,10},{10,1... | collective-permute-start | bytes 1572872 | tf_op jit(solution)/shard_map/ppermute | solution.py:59
  252.8 15.1 %collective-permute-start.14 = (bf16[128,2048]{1,0:T(8,128)(2,1)S(1)}, bf16[128,2048]{1,0:T(8,128)(2,1)S(1)}, u32[]{:S(2)}, u32[]{:S(2)}) collective-permute-start(bf16[128,2048]{1,0:T(8,128)(2,1)S(1)} %collective-permute-done.13), channel_id=1, source_target_pairs={{0,1},{1,2},{2,3},{3,0},{4,5},{5,6},{6,7},{7,4},{8,9},{9,10},{10,1... | collective-permute-start | bytes 1572872 | tf_op jit(solution)/shard_map/ppermute | solution.py:59
  305.8 17.1 %collective-permute-start.21 = (bf16[128,2048]{1,0:T(8,128)(2,1)S(1)}, bf16[128,2048]{1,0:T(8,128)(2,1)S(1)}, u32[]{:S(2)}, u32[]{:S(2)}) collective-permute-start(bf16[128,2048]{1,0:T(8,128)(2,1)S(1)} %slice.136), channel_id=1, source_target_pairs={{0,1},{1,2},{2,3},{3,0},{4,5},{5,6},{6,7},{7,4},{8,9},{9,10},{10,1... | collective-permute-start | bytes 1572872 | tf_op jit(solution)/shard_map/ppermute | solution.py:59
  314.0 20.1 %collective-permute-start.15 = (bf16[128,2048]{1,0:T(8,128)(2,1)S(1)}, bf16[128,2048]{1,0:T(8,128)(2,1)S(1)}, u32[]{:S(2)}, u32[]{:S(2)}) collective-permute-start(bf16[128,2048]{1,0:T(8,128)(2,1)S(1)} %slice.132), channel_id=1, source_target_pairs={{0,1},{1,2},{2,3},{3,0},{4,5},{5,6},{6,7},{7,4},{8,9},{9,10},{10,1... | collective-permute-start | bytes 1572872 | tf_op jit(solution)/shard_map/ppermute | solution.py:59
  323.0 22.3 %collective-permute-start.22 = (bf16[128,2048]{1,0:T(8,128)(2,1)S(1)}, bf16[128,2048]{1,0:T(8,128)(2,1)S(1)}, u32[]{:S(2)}, u32[]{:S(2)}) collective-permute-start(bf16[128,2048]{1,0:T(8,128)(2,1)S(1)} %add_convert_fusion.7), channel_id=1, source_target_pairs={{0,1},{1,2},{2,3},{3,0},{4,5},{5,6},{6,7},{7,4},{8,9},{9,10},{10,1... | collective-permute-start | bytes 1572872 | tf_op jit(solution)/shard_map/ppermute | solution.py:59
  334.3 22.3 %collective-permute-start.16 = (bf16[128,2048]{1,0:T(8,128)(2,1)S(1)}, bf16[128,2048]{1,0:T(8,128)(2,1)S(1)}, u32[]{:S(2)}, u32[]{:S(2)}) collective-permute-start(bf16[128,2048]{1,0:T(8,128)(2,1)S(1)} %add_convert_fusion.10), channel_id=1, source_target_pairs={{0,1},{1,2},{2,3},{3,0},{4,5},{5,6},{6,7},{7,4},{8,9},{9,10},{10,1... | collective-permute-start | bytes 1572872 | tf_op jit(solution)/shard_map/ppermute | solution.py:59
  345.5 22.3 %collective-permute-start.23 = (bf16[128,2048]{1,0:T(8,128)(2,1)S(1)}, bf16[128,2048]{1,0:T(8,128)(2,1)S(1)}, u32[]{:S(2)}, u32[]{:S(2)}) collective-permute-start(bf16[128,2048]{1,0:T(8,128)(2,1)S(1)} %add_convert_fusion.6), channel_id=1, source_target_pairs={{0,1},{1,2},{2,3},{3,0},{4,5},{5,6},{6,7},{7,4},{8,9},{9,10},{10,1... | collective-permute-start | bytes 1572872 | tf_op jit(solution)/shard_map/ppermute | solution.py:59
  356.7 19.7 %collective-permute-start.17 = (bf16[128,2048]{1,0:T(8,128)(2,1)S(1)}, bf16[128,2048]{1,0:T(8,128)(2,1)S(1)}, u32[]{:S(2)}, u32[]{:S(2)}) collective-permute-start(bf16[128,2048]{1,0:T(8,128)(2,1)S(1)} %add_convert_fusion.9), channel_id=1, source_target_pairs={{0,1},{1,2},{2,3},{3,0},{4,5},{5,6},{6,7},{7,4},{8,9},{9,10},{10,1... | collective-permute-start | bytes 1572872 | tf_op jit(solution)/shard_map/ppermute | solution.py:59
  379.1 13.1 %collective-permute-start.24 = (bf16[128,2048]{1,0:T(8,128)(2,1)S(1)}, bf16[128,2048]{1,0:T(8,128)(2,1)S(1)}, u32[]{:S(2)}, u32[]{:S(2)}) collective-permute-start(bf16[128,2048]{1,0:T(8,128)(2,1)S(1)} %get-tuple-element.22), channel_id=1, source_target_pairs={{0,1},{1,2},{2,3},{3,0},{4,5},{5,6},{6,7},{7,4},{8,9},{9,10},{10,1... | collective-permute-start | bytes 1572872 | tf_op jit(solution)/shard_map/ppermute | solution.py:59
  392.2 12.2 %collective-permute-start.25 = (bf16[128,2048]{1,0:T(8,128)(2,1)S(1)}, bf16[128,2048]{1,0:T(8,128)(2,1)}, u32[]{:S(2)}, u32[]{:S(2)}) collective-permute-start(bf16[128,2048]{1,0:T(8,128)(2,1)S(1)} %collective-permute-done.24), channel_id=1, source_target_pairs={{0,1},{1,2},{2,3},{3,0},{4,5},{5,6},{6,7},{7,4},{8,9},{9,10},{10,1... | collective-permute-start | bytes 1572872 | tf_op jit(solution)/shard_map/ppermute | solution.py:59
  404.4 11.6 %collective-permute-start.26 = (bf16[128,2048]{1,0:T(8,128)(2,1)}, bf16[128,2048]{1,0:T(8,128)(2,1)S(1)}, u32[]{:S(2)}, u32[]{:S(2)}) collective-permute-start(bf16[128,2048]{1,0:T(8,128)(2,1)} %collective-permute-done.25), channel_id=1, source_target_pairs={{0,1},{1,2},{2,3},{3,0},{4,5},{5,6},{6,7},{7,4},{8,9},{9,10},{10,1... | collective-permute-start | bytes 1572872 | tf_op jit(solution)/shard_map/ppermute | solution.py:59
  422.3 6.4 %collective-permute-start.28 = (bf16[512,128]{1,0:T(8,128)(2,1)S(1)}, bf16[512,128]{1,0:T(8,128)(2,1)}, u32[]{:S(2)}, u32[]{:S(2)}) collective-permute-start(bf16[512,128]{1,0:T(8,128)(2,1)S(1)} %get-tuple-element.39), channel_id=1, source_target_pairs={{0,8},{4,12},{8,0},{12,4},{16,24},{20,28},{24,16},{28,20},{1,9},{5... | collective-permute-start | bytes 393224 | tf_op jit(solution)/shard_map/ppermute | solution.py:80
  423.3 7.4 %collective-permute-start.29 = (bf16[512,128]{1,0:T(8,128)(2,1)S(1)}, bf16[512,128]{1,0:T(8,128)(2,1)}, u32[]{:S(2)}, u32[]{:S(2)}) collective-permute-start(bf16[512,128]{1,0:T(8,128)(2,1)S(1)} %get-tuple-element.38), channel_id=1, source_target_pairs={{0,12},{4,8},{8,4},{12,0},{16,28},{20,24},{24,20},{28,16},{1,13},{... | collective-permute-start | bytes 393224 | tf_op jit(solution)/shard_map/ppermute | solution.py:80
  464.1 4.7 collective-permute-start.30
  464.3 12.3 %collective-permute-start.31 = (bf16[512,384]{1,0:T(8,128)(2,1)}, bf16[512,384]{1,0:T(8,128)(2,1)}, u32[]{:S(2)}, u32[]{:S(2)}) collective-permute-start(bf16[512,384]{1,0:T(8,128)(2,1)} %get-tuple-element.27), channel_id=1, source_target_pairs={{0,8},{4,12},{8,0},{12,4},{16,24},{20,28},{24,16},{28,20},{1,9},{5... | collective-permute-start | bytes 1179656 | tf_op jit(solution)/shard_map/ppermute | solution.py:80
  467.2 16.6 %collective-permute-start.32 = (bf16[512,384]{1,0:T(8,128)(2,1)}, bf16[512,384]{1,0:T(8,128)(2,1)}, u32[]{:S(2)}, u32[]{:S(2)}) collective-permute-start(bf16[512,384]{1,0:T(8,128)(2,1)} %get-tuple-element.26), channel_id=1, source_target_pairs={{0,12},{4,8},{8,4},{12,0},{16,28},{20,24},{24,20},{28,16},{1,13},{... | collective-permute-start | bytes 1179656 | tf_op jit(solution)/shard_map/ppermute | solution.py:80
  496.8 24.4 %collective-permute-start.33 = (bf16[128,2048]{1,0:T(8,128)(2,1)}, bf16[128,2048]{1,0:T(8,128)(2,1)S(1)}, u32[]{:S(2)}, u32[]{:S(2)}) collective-permute-start(bf16[128,2048]{1,0:T(8,128)(2,1)} %slice.144), channel_id=1, source_target_pairs={{0,1},{1,2},{2,3},{3,0},{4,5},{5,6},{6,7},{7,4},{8,9},{9,10},{10,1... | collective-permute-start | bytes 1572872 | tf_op jit(solution)/shard_map/ppermute | solution.py:59
  499.1 6.1 %collective-permute-start.45 = (bf16[2,16,768]{2,1,0:T(8,128)(2,1)S(1)}, bf16[2,16,768]{2,1,0:T(8,128)(2,1)S(1)}, u32[]{:S(2)}, u32[]{:S(2)}) collective-permute-start(bf16[2,16,768]{2,1,0:T(8,128)(2,1)S(1)} %get-tuple-element.49), channel_id=1, source_target_pairs={{0,12},{4,8},{8,4},{12,0},{16,28},{20,24},{24,20},{28,16},{1,13},{... | collective-permute-start | bytes 147464 | tf_op jit(solution)/shard_map/ppermute | solution.py:80
  500.3 4.9 collective-permute-start.44
  501.3 6.0 %collective-permute-start.43 = (bf16[2,16,768]{2,1,0:T(8,128)(2,1)S(1)}, bf16[2,16,768]{2,1,0:T(8,128)(2,1)S(1)}, u32[]{:S(2)}, u32[]{:S(2)}) collective-permute-start(bf16[2,16,768]{2,1,0:T(8,128)(2,1)S(1)} %get-tuple-element.48), channel_id=1, source_target_pairs={{0,4},{4,0},{8,12},{12,8},{16,20},{20,16},{24,28},{28,24},{1,5},{5... | collective-permute-start | bytes 147464 | tf_op jit(solution)/shard_map/ppermute | solution.py:80
  501.6 13.0 %collective-permute-start.38 = (bf16[4,2,16,256]{3,2,1,0:T(8,128)(2,1)S(1)}, bf16[4,2,16,256]{3,2,1,0:T(8,128)(2,1)S(1)}, u32[]{:S(2)}, u32[]{:S(2)}) collective-permute-start(bf16[4,2,16,256]{3,2,1,0:T(8,128)(2,1)S(1)} %get-tuple-element.36), channel_id=1, source_target_pairs={{0,3},{1,0},{2,1},{3,2},{4,7},{5,4},{6,5},{7,6},{8,11},{9,8},{10,9... | collective-permute-start | bytes 196616 | tf_op jit(solution)/shard_map/ppermute | solution.py:405
  505.2 13.7 %collective-permute-start.37 = (bf16[4,2,16,256]{3,2,1,0:T(8,128)(2,1)S(1)}, bf16[4,2,16,256]{3,2,1,0:T(8,128)(2,1)S(1)}, u32[]{:S(2)}, u32[]{:S(2)}) collective-permute-start(bf16[4,2,16,256]{3,2,1,0:T(8,128)(2,1)S(1)} %get-tuple-element.37), channel_id=1, source_target_pairs={{0,2},{1,3},{2,0},{3,1},{4,6},{5,7},{6,4},{7,5},{8,10},{9,11},{10,... | collective-permute-start | bytes 196616 | tf_op jit(solution)/shard_map/ppermute | solution.py:405
  505.2 13.7 %collective-permute-start.36 = (bf16[4,2,16,256]{3,2,1,0:T(8,128)(2,1)S(1)}, bf16[4,2,16,256]{3,2,1,0:T(8,128)(2,1)S(1)}, u32[]{:S(2)}, u32[]{:S(2)}) collective-permute-start(bf16[4,2,16,256]{3,2,1,0:T(8,128)(2,1)S(1)} %get-tuple-element.35), channel_id=1, source_target_pairs={{0,1},{1,2},{2,3},{3,0},{4,5},{5,6},{6,7},{7,4},{8,9},{9,10},{10,1... | collective-permute-start | bytes 196616 | tf_op jit(solution)/shard_map/ppermute | solution.py:405
  507.3 13.5 %collective-permute-start.47 = (bf16[16,768]{1,0:T(8,128)(2,1)S(1)}, bf16[16,768]{1,0:T(8,128)(2,1)S(1)}, u32[]{:S(2)}, u32[]{:S(2)}) collective-permute-start(bf16[16,768]{1,0:T(8,128)(2,1)S(1)} %get-tuple-element.59), channel_id=1, source_target_pairs={{0,1},{1,9},{2,17},{3,25},{4,3},{5,11},{6,19},{7,27},{8,5},{9,13},... | collective-permute-start | bytes 73736 | tf_op jit(solution)/shard_map/ppermute | solution.py:448
  514.5 6.4 %collective-permute-start.46 = (bf16[16,768]{1,0:T(8,128)(2,1)S(1)}, bf16[16,768]{1,0:T(8,128)(2,1)S(1)}, u32[]{:S(2)}, u32[]{:S(2)}) collective-permute-start(bf16[16,768]{1,0:T(8,128)(2,1)S(1)} %get-tuple-element.58), channel_id=1, source_target_pairs={{0,0},{1,8},{2,16},{3,24},{4,2},{5,10},{6,18},{7,26},{8,4},{9,12},... | collective-permute-start | bytes 73736 | tf_op jit(solution)/shard_map/ppermute | solution.py:448
  519.0 5.6 collective-permute-start.41
  519.8 4.8 collective-permute-start.40
  521.3 16.0 %collective-permute-start.34 = (bf16[128,2048]{1,0:T(8,128)(2,1)S(1)}, bf16[128,2048]{1,0:T(8,128)(2,1)S(1)}, u32[]{:S(2)}, u32[]{:S(2)}) collective-permute-start(bf16[128,2048]{1,0:T(8,128)(2,1)S(1)} %add_convert_fusion.5), channel_id=1, source_target_pairs={{0,1},{1,2},{2,3},{3,0},{4,5},{5,6},{6,7},{7,4},{8,9},{9,10},{10,1... | collective-permute-start | bytes 1572872 | tf_op jit(solution)/shard_map/ppermute | solution.py:59
  524.6 12.9 %collective-permute-start.42 = (bf16[16,256]{1,0:T(8,128)(2,1)S(1)}, bf16[16,256]{1,0:T(8,128)(2,1)S(1)}, u32[]{:S(2)}, u32[]{:S(2)}) collective-permute-start(bf16[16,256]{1,0:T(8,128)(2,1)S(1)} %fusion.97), channel_id=1, source_target_pairs={{0,16},{4,20},{8,24},{12,28},{16,0},{20,4},{24,8},{28,12},{1,17},{... | collective-permute-start | bytes 24584 | tf_op jit(solution)/shard_map/ppermute | solution.py:418
  537.5 15.2 %collective-permute-start.35 = (bf16[128,2048]{1,0:T(8,128)(2,1)S(1)}, bf16[128,2048]{1,0:T(8,128)(2,1)S(1)}, u32[]{:S(2)}, u32[]{:S(2)}) collective-permute-start(bf16[128,2048]{1,0:T(8,128)(2,1)S(1)} %add_convert_fusion.4), channel_id=1, source_target_pairs={{0,1},{1,2},{2,3},{3,0},{4,5},{5,6},{6,7},{7,4},{8,9},{9,10},{10,1... | collective-permute-start | bytes 1572872 | tf_op jit(solution)/shard_map/ppermute | solution.py:59
  (62 other events, 1051.2 us)
Sparse Core Ops, SparseCore 0:
  9.9 48.2 all-gather.4
  60.1 36.2 all-gather.6
  98.3 59.7 all-gather.8
  159.8 55.9 all-gather.10

commit v2 on v1

--- a/solution.py
+++ b/solution.py
@@ -18,6 +18,8 @@
 F32 = jnp.float32
 BLOCK = 256
 VMEM_BYTES = 56 * 1024 * 1024
+SMALL_VMEM_BYTES = 28 * 1024 * 1024
+US = 10**9
 
 
 def dot(a, b):
@@ -30,6 +32,10 @@
 
 def dot_tn(a, b):
     return lax.dot_general(a, b, (((0,), (0,)), ((), ())), preferred_element_type=F32)
+
+
+def hold(value, *until):
+    return lax.optimization_barrier((value,) + until)[0]
 
 
 def gelu_and_slope(f):
@@ -59,18 +65,41 @@
     return lax.ppermute(array, axis, [(i, (i + 1) % n) for i in range(n)])
 
 
-def ring_gather(array, axis):
+def ring_gather(array, axis, hops=None):
     pieces = [array]
-    for _ in range(lax.axis_size(axis) - 1):
+    for _ in range(lax.axis_size(axis) - 1 if hops is None else hops):
         pieces.append(shift_one(pieces[-1], axis))
     return pieces
 
 
-def ring_scatter(pieces, axis):
+class Side:
+    def __init__(self, stages):
+        self.stages, self.result = stages, None
+        self.flying = next(stages)
+
+    def step(self, beside):
+        if self.flying is None:
+            return beside
+        unused, *landed = lax.optimization_barrier((beside,) + tuple(self.flying))
+        try:
+            self.flying = self.stages.send(landed)
+        except StopIteration as stop:
+            self.flying, self.result = None, stop.value
+        return beside
+
+
+def ring_scatter(pieces, axis, side=(), first=False):
     total = pieces[1].astype(BF)
-    for piece in pieces[2:] + pieces[:1]:
-        total = shift_one(total, axis).astype(F32) + piece.astype(F32)
-        if piece is not pieces[0]:
+    following = pieces[2:] + pieces[:1]
+    if first:
+        total = (total.astype(F32) + following[0].astype(F32)).astype(BF)
+        following = following[1:]
+    for i, piece in enumerate(following):
+        moved = shift_one(total, axis)
+        for work in side:
+            moved = work.step(moved) if isinstance(work, Side) else work(moved)
+        total = moved.astype(F32) + piece.astype(F32)
+        if i < len(following) - 1:
             total = total.astype(BF)
     return total
 
@@ -349,9 +378,7 @@
         ],
         compiler_params=pltpu.CompilerParams(vmem_limit_bytes=VMEM_BYTES),
         cost_estimate=pl.CostEstimate(
-            flops=heads * length * length * HD * 8,
-            bytes_accessed=length * heads * HD * 20,
-            transcendentals=heads * length * length // 2,
+            flops=2 * US, bytes_accessed=length * heads * HD * 20, transcendentals=0
         ),
     )(meta, slopes, *pieces)
 
@@ -379,75 +406,460 @@
         ],
         compiler_params=pltpu.CompilerParams(vmem_limit_bytes=VMEM_BYTES),
         cost_estimate=pl.CostEstimate(
-            flops=heads * length * length * HD * 16,
-            bytes_accessed=length * heads * HD * 20,
-            transcendentals=heads * length * length // 2,
+            flops=2 * US, bytes_accessed=length * heads * HD * 20, transcendentals=0
         ),
     )(meta, slopes, *pieces, qkv, out_t, logs)
 
 
-def reduce_full_width(stacks, groups):
+def take_columns(ref, part, e, width):
+    def each(use):
+        if width % 128 == 0:
+            start = pl.multiple_of((part ^ e) * width, width)
+            use(ref.at[:, pl.ds(start, width)])
+        else:
+            for p in range(SEQ_DEVS):
+
+                @pl.when(part == p)
+                def _():
+                    use(ref.at[:, pl.ds((p ^ e) * width, width)])
+
+    return each
+
+
+def column_loop(total, body):
+    step = min(256, total)
+
+    def one(i, unused):
+        body(pl.ds(pl.multiple_of(i * step, step), step))
+        return unused
+
+    lax.fori_loop(0, total // step, one, 0)
+
+
+def load_weights(w_pieces, w_ref, sems, starts_ref):
+    copies = []
+    for i, piece in enumerate(w_pieces):
+        count = piece.shape[0]
+        start = pl.multiple_of(starts_ref[i], min(128, count))
+        copy = pltpu.make_async_copy(piece, w_ref.at[pl.ds(start, count), :], sems.at[i])
+        copy.start()
+        copies.append(copy)
+    return copies
+
+
+def qkv_kernel(ring, n_w, meta_ref, starts_ref, *refs):
+    h_pieces = refs[:ring]
+    gain_ref, shift_ref, a_ref, b_ref, bias_ref = refs[ring : ring + 5]
+    w_pieces = refs[ring + 5 : ring + 5 + n_w]
+    outs = refs[ring + 5 + n_w :]
+    q_refs, u_ref, x_ref = outs[:SEQ_DEVS], outs[SEQ_DEVS], outs[SEQ_DEVS + 1]
+    o_ref, w_ref, sems = outs[SEQ_DEVS + 2 :]
+    copies = load_weights(w_pieces, w_ref, sems, starts_ref)
+    rows = h_pieces[0].shape[0]
+    for k in range(ring):
+        normed, unused, unused = norm_forward(
+            h_pieces[k][...].astype(F32), gain_ref[...], shift_ref[...]
+        )
+        x_ref[k * rows : (k + 1) * rows, :] = normed.astype(BF)
+    u_ref[...] = dot_nt(x_ref[...], a_ref[...]).astype(BF)
+    for copy in copies:
+        copy.wait()
+
+    def body(cols):
+        total = dot(x_ref[...], w_ref[:, cols])
+        total = total + FACTOR * dot(u_ref[...], b_ref[:, cols]) + bias_ref[:, cols]
+        o_ref[:, cols] = total.astype(BF)
+
+    column_loop(o_ref.shape[1], body)
+    for e in range(SEQ_DEVS):
+
+        def store(src, e=e):
+            q_refs[e][...] = src[...]
+
+        take_columns(o_ref, meta_ref[0], e, q_refs[e].shape[1])(store)
+
+
+def qkv_product(h_pieces, gain, shift, a, b, bias, w_pieces, starts, meta):
+    ring, n_w = len(h_pieces), len(w_pieces)
+    rows, depth = h_pieces[0].shape
+    cols = b.shape[1]
+    outs = pl.pallas_call(
+        functools.partial(qkv_kernel, ring, n_w),
+        out_shape=tuple(
+            [jax.ShapeDtypeStruct((ring * rows, cols // SEQ_DEVS), BF)] * SEQ_DEVS
+            + [
+                jax.ShapeDtypeStruct((ring * rows, a.shape[0]), BF),
+                jax.ShapeDtypeStruct((ring * rows, depth), BF),
+            ]
+        ),
+        in_specs=specs(2, ring + 5) + [pl.BlockSpec(memory_space=pl.ANY)] * n_w,
+        out_specs=tuple(specs(0, SEQ_DEVS + 2)),
+        scratch_shapes=[
+            pltpu.VMEM((ring * rows, cols), BF),
+            pltpu.VMEM((depth, cols), BF),
+            pltpu.SemaphoreType.DMA((n_w,)),
+        ],
+        compiler_params=pltpu.CompilerParams(vmem_limit_bytes=VMEM_BYTES),
+        cost_estimate=pl.CostEstimate(
+            flops=2 * US, bytes_accessed=2**20, transcendentals=0
+        ),
+    )(meta, starts, *h_pieces, gain, shift, a, b, bias, *w_pieces)
+    return list(outs[:SEQ_DEVS]), outs[SEQ_DEVS], outs[SEQ_DEVS + 1]
+
+
+def load_kernel(src_ref, dst_ref, sems):
+    count = src_ref.shape[0]
+    copies = [
+        pltpu.make_async_copy(src_ref.at[i], dst_ref.at[i], sems.at[i]) for i in range(count)
+    ]
+    for copy in copies:
+        copy.start()
+    for copy in copies:
+        copy.wait()
+
+
+def load_to_vmem(array):
+    return pl.pallas_call(
+        load_kernel,
+        out_shape=pltpu.VMEM(array.shape, array.dtype),
+        in_specs=[pl.BlockSpec(memory_space=pl.ANY)],
+        out_specs=pl.BlockSpec(memory_space=pltpu.VMEM),
+        scratch_shapes=[pltpu.SemaphoreType.DMA((array.shape[0],))],
+        compiler_params=pltpu.CompilerParams(vmem_limit_bytes=2 * 1024 * 1024),
+        cost_estimate=pl.CostEstimate(
+            flops=5 * US, bytes_accessed=2 * array.size, transcendentals=0
+        ),
+    )(pltpu.with_memory_space_constraint(array, pltpu.HBM))
+
+
+def out_kernel(ring, meta_ref, *refs):
+    c_pieces = refs[:SEQ_DEVS]
+    a_ref, b_ref, w_ref = refs[SEQ_DEVS : SEQ_DEVS + 3]
+    p_refs = refs[SEQ_DEVS + 3 : SEQ_DEVS + 3 + ring]
+    ctx_ref, u_ref = refs[SEQ_DEVS + 3 + ring :]
+    rows = p_refs[0].shape[0]
+    width = c_pieces[0].shape[1]
+    for e in range(SEQ_DEVS):
+
+        def store(dst, e=e):
+            dst[...] = c_pieces[e][...]
+
+        take_columns(ctx_ref, meta_ref[0], e, width)(store)
+    u_ref[...] = dot_nt(ctx_ref[...], a_ref[...]).astype(BF)
+    shards, unused, wide = w_ref.shape
+    for j in range(shards):
+        cols = slice(j * wide, (j + 1) * wide)
+        total = dot(ctx_ref[...], w_ref[j]) + FACTOR * dot(u_ref[...], b_ref[:, cols])
+        total = total.astype(BF)
+        for k in range(ring):
+            p_refs[k][:, cols] = total[k * rows : (k + 1) * rows]
+
+
+def out_product(c_pieces, a, b, w, meta, ring):
+    count, width = c_pieces[0].shape
+    rank, depth = b.shape
+    outs = pl.pallas_call(
+        functools.partial(out_kernel, ring),
+        out_shape=tuple(
+            [jax.ShapeDtypeStruct((count // ring, depth), BF)] * ring
+            + [
+                jax.ShapeDtypeStruct((count, width * SEQ_DEVS), BF),
+                jax.ShapeDtypeStruct((count, rank), BF),
+            ]
+        ),
+        in_specs=specs(1, SEQ_DEVS + 3),
+        out_specs=tuple(specs(0, ring + 2)),
+        compiler_params=pltpu.CompilerParams(vmem_limit_bytes=VMEM_BYTES),
+        cost_estimate=pl.CostEstimate(
+            flops=2 * count * depth * width * SEQ_DEVS,
+            bytes_accessed=8 * depth * width * SEQ_DEVS,
+            transcendentals=0,
+        ),
+    )(meta, *c_pieces, a, b, w)
+    return list(outs[:ring]), outs[ring], outs[ring + 1]
+
+
+def mlp_kernel(count, add, *refs):
+    n2_refs, gy_refs = refs[:count], refs[count : 2 * count]
+    refs = refs[2 * count :]
+    a1_ref, b2_ref, b1_ref, a2_ref, bias_ref, w_ref = refs[:6]
+    before, refs = refs[6 : 6 + add], refs[6 + add :]
+    p_refs, m_refs, grads = refs[:count], refs[count : 2 * count], refs[2 * count : 2 * count + 4]
+    x_ref, g_ref, act_ref, slope_ref, gf_ref = refs[2 * count + 4 :]
+    shards, double, depth, wide = w_ref.shape
+    chunks = double // 2
+    rows = n2_refs[0].shape[0]
+    for k in range(count):
+        x_ref[k * rows : (k + 1) * rows, :] = n2_refs[k][...]
+        g_ref[k * rows : (k + 1) * rows, :] = gy_refs[k][...]
+    u3 = dot_nt(x_ref[...], a1_ref[...]).astype(BF)
+    gu4 = (FACTOR * dot_nt(g_ref[...], b2_ref[...])).astype(BF)
+    for h in range(chunks):
+        cols = slice(h * wide, (h + 1) * wide)
+        f = dot(x_ref[...], w_ref[:, h].reshape(shards * depth, wide))
+        f = f + FACTOR * dot(u3, b1_ref[:, cols]) + bias_ref[:, cols]
+        act, slope = gelu_and_slope(f)
+        act_ref[:, cols] = act.astype(BF)
+        slope_ref[:, cols] = slope
+    for h in range(chunks):
+        cols = slice(h * wide, (h + 1) * wide)
+        gact = dot(gu4, a2_ref[:, cols])
+        for j in range(shards):
+            gact = gact + dot_nt(g_ref[:, j * wide : (j + 1) * wide], w_ref[j, chunks + h])
+        gf_ref[:, cols] = (gact * slope_ref[:, cols]).astype(BF)
+    gu3 = (FACTOR * dot_nt(gf_ref[...], b1_ref[...])).astype(BF)
+    for j in range(shards):
+        cols = slice(j * depth, (j + 1) * depth)
+        total = dot(gu3, a1_ref[:, cols])
+        for h in range(chunks):
+            total = total + dot_nt(gf_ref[:, h * wide : (h + 1) * wide], w_ref[j, h])
+        total = total.astype(BF)
+        for k in range(count):
+            p_refs[k][:, cols] = total[k * rows : (k + 1) * rows]
+    u4 = dot_nt(act_ref[...], a2_ref[...]).astype(BF)
+    for j in range(shards):
+        cols = slice(j * wide, (j + 1) * wide)
+        total = dot(act_ref[...], w_ref[j, chunks:].reshape(chunks * depth, wide))
+        total = (total + FACTOR * dot(u4, b2_ref[:, cols])).astype(BF)
+        for k in range(count):
+            m_refs[k][:, cols] = total[k * rows : (k + 1) * rows]
+    products = [
+        FACTOR * dot_tn(u3, gf_ref[...]),
+        dot_tn(gu4, act_ref[...]),
+        dot_tn(gu3, x_ref[...]),
+        FACTOR * dot_tn(u4, g_ref[...]),
+    ]
+    for i, product in enumerate(products):
+        grads[i][...] = product + before[i][...] if add else product
+
+
+def mlp_both_ways(n2_pieces, gy_pieces, a1, b1, a2, b2, bias, w_fc, before):
+    count = len(n2_pieces)
+    rows, depth = n2_pieces[0].shape
+    rank, hidden = b1.shape
+    total = count * rows
+    outs = pl.pallas_call(
+        functools.partial(mlp_kernel, count, len(before)),
+        out_shape=(
+            [jax.ShapeDtypeStruct((rows, depth), BF)] * (2 * count)
+            + [jax.ShapeDtypeStruct((rank, hidden), F32)] * 2
+            + [jax.ShapeDtypeStruct((rank, depth), F32)] * 2
+        ),
+        in_specs=specs(0, 2 * count + 6 + len(before)),
+        out_specs=specs(0, 2 * count + 4),
+        scratch_shapes=[
+            pltpu.VMEM((total, depth), BF),
+            pltpu.VMEM((total, depth), BF),
+            pltpu.VMEM((total, hidden), BF),
+            pltpu.VMEM((total, hidden), F32),
+            pltpu.VMEM((total, hidden), BF),
+        ],
+        compiler_params=pltpu.CompilerParams(vmem_limit_bytes=SMALL_VMEM_BYTES),
+        cost_estimate=pl.CostEstimate(
+            flops=10 * US, bytes_accessed=4 * depth * hidden, transcendentals=0
+        ),
+    )(*n2_pieces, *gy_pieces, a1, b2, b1, a2, bias, w_fc, *before)
+    return list(outs[:count]), list(outs[count : 2 * count]), list(outs[2 * count :])
+
+
+def gctx_kernel(ring, meta_ref, *refs):
+    g_pieces = refs[:ring]
+    a_ref, b_ref, w_ref, ctx_ref, u2_ref = refs[ring : ring + 5]
+    c_refs = refs[ring + 5 : ring + 5 + SEQ_DEVS]
+    gb_ref, ga_ref, g_ref, o_ref = refs[ring + 5 + SEQ_DEVS :]
+    rows = g_pieces[0].shape[0]
+    for k in range(ring):
+        g_ref[k * rows : (k + 1) * rows, :] = g_pieces[k][...]
+    gu2 = (FACTOR * dot_nt(g_ref[...], b_ref[...])).astype(BF)
+    shards, unused, wide = w_ref.shape
+    total = dot(gu2, a_ref[...])
+    for j in range(shards):
+        total = total + dot_nt(g_ref[:, j * wide : (j + 1) * wide], w_ref[j])
+    o_ref[...] = total.astype(BF)
+    for e in range(SEQ_DEVS):
+
+        def store(src, e=e):
+            c_refs[e][...] = src[...]
+
+        take_columns(o_ref, meta_ref[0], e, c_refs[e].shape[1])(store)
+    gb_ref[...] = FACTOR * dot_tn(u2_ref[...], g_ref[...])
+    ga_ref[...] = dot_tn(gu2, ctx_ref[...])
+
+
+def gctx_product(g_pieces, a, b, w, ctx, u2, meta):
+    ring = len(g_pieces)
+    rows, depth = g_pieces[0].shape
+    count, cols = ctx.shape
+    rank = a.shape[0]
+    outs = pl.pallas_call(
+        functools.partial(gctx_kernel, ring),
+        out_shape=tuple(
+            [jax.ShapeDtypeStruct((count, cols // SEQ_DEVS), BF)] * SEQ_DEVS
+            + [jax.ShapeDtypeStruct((rank, depth), F32), jax.ShapeDtypeStruct((rank, cols), F32)]
+        ),
+        in_specs=specs(1, ring + 5),
+        out_specs=tuple(specs(0, SEQ_DEVS + 2)),
+        scratch_shapes=[pltpu.VMEM((count, depth), BF), pltpu.VMEM((count, cols), BF)],
+        compiler_params=pltpu.CompilerParams(vmem_limit_bytes=VMEM_BYTES),
+        cost_estimate=pl.CostEstimate(
+            flops=2 * count * depth * cols, bytes_accessed=8 * depth * cols, transcendentals=0
+        ),
+    )(meta, *g_pieces, a, b, w, ctx, u2)
+    return list(outs[:SEQ_DEVS]), outs[SEQ_DEVS], outs[SEQ_DEVS + 1]
+
+
+def joined_kernel(meta_ref, *refs):
+    q_pieces = refs[:SEQ_DEVS]
+    x_ref, b_ref, u1_ref, gb_ref, ga_ref, gu_ref, q_ref = refs[SEQ_DEVS:]
+    for e in range(SEQ_DEVS):
+
+        def store(dst, e=e):
+            dst[...] = q_pieces[e][...]
+
+        take_columns(q_ref, meta_ref[0], e, q_pieces[e].shape[1])(store)
+    gu1 = (FACTOR * dot_nt(q_ref[...], b_ref[...])).astype(BF)
+    gu_ref[...] = gu1
+    gb_ref[...] = FACTOR * dot_tn(u1_ref[...], q_ref[...])
+    ga_ref[...] = dot_tn(gu1, x_ref[...])
+
+
+def joined_gradients(q_pieces, n1, b, u1, meta):
+    rank, cols = b.shape
+    count, depth = n1.shape
+    return pl.pallas_call(
+        joined_kernel,
+        out_shape=(
+            jax.ShapeDtypeStruct((rank, cols), F32),
+            jax.ShapeDtypeStruct((rank, depth), F32),
+            jax.ShapeDtypeStruct((count, rank), BF),
+            jax.ShapeDtypeStruct((count, cols), BF),
+        ),
+        in_specs=specs(1, SEQ_DEVS + 3),
+        out_specs=tuple(specs(0, 4)),
+        compiler_params=pltpu.CompilerParams(vmem_limit_bytes=VMEM_BYTES),
+        cost_estimate=pl.CostEstimate(
+            flops=4 * US, bytes_accessed=2 * count * (cols + depth), transcendentals=0
+        ),
+    )(meta, *q_pieces, n1, b, u1)
+
+
+def gn1_kernel(ring, n_w, starts_ref, q_ref, gu_ref, a_ref, *refs):
+    w_pieces, p_refs = refs[:n_w], refs[n_w : n_w + ring]
+    w_ref, sems = refs[n_w + ring :]
+    copies = load_weights(w_pieces, w_ref, sems, starts_ref)
+    rows = p_refs[0].shape[0]
+    for copy in copies:
+        copy.wait()
+
+    def body(cols):
+        total = dot_nt(q_ref[...], w_ref[cols, :]) + dot(gu_ref[...], a_ref[:, cols])
+        total = total.astype(BF)
+        for k in range(ring):
+            p_refs[k][:, cols] = total[k * rows : (k + 1) * rows]
+
+    column_loop(w_ref.shape[0], body)
+
+
+def gn1_product(gqkv, gu1, a, w_pieces, starts, ring):
+    n_w = len(w_pieces)
+    count, cols = gqkv.shape
+    rank, depth = a.shape
+    return list(
+        pl.pallas_call(
+            functools.partial(gn1_kernel, ring, n_w),
+            out_shape=tuple([jax.ShapeDtypeStruct((count // ring, depth), BF)] * ring),
+            in_specs=specs(1, 3) + [pl.BlockSpec(memory_space=pl.ANY)] * n_w,
+            out_specs=tuple(specs(0, ring)),
+            scratch_shapes=[pltpu.VMEM((depth, cols), BF), pltpu.SemaphoreType.DMA((n_w,))],
+            compiler_params=pltpu.CompilerParams(vmem_limit_bytes=VMEM_BYTES),
+            cost_estimate=pl.CostEstimate(
+                flops=6 * US, bytes_accessed=2 * depth * cols, transcendentals=0
+            ),
+        )(starts, gqkv, gu1, a, *w_pieces)
+    )
+
+
+def pack_kernel(n_full, ring, groups, meta_ref, *refs):
+    stacks, (full_ref, cols_ref) = refs[:-2], refs[-2:]
+    part, spot = meta_ref[0], meta_ref[1]
+    at = 0
+    for ref in stacks[:n_full]:
+        width = ref.shape[1] // (ring * SEQ_DEVS * groups)
+        for g in range(groups):
+            for p in range(SEQ_DEVS):
+                for z in range(ring):
+                    k = z - spot
+                    k = jnp.where(k < 0, k + ring, k)
+                    column = ((g * SEQ_DEVS + p) * ring + z) * width
+                    full_ref[k, part ^ p, g, :, at : at + width] = ref[
+                        :, column : column + width
+                    ].astype(BF)
+        at += width
+    at = 0
+    for ref in stacks[n_full:]:
+        width = ref.shape[1] // (SEQ_DEVS * groups)
+        for p in range(SEQ_DEVS):
+            for r in range(groups):
+                column = (p * groups + r) * width
+                cols_ref[part ^ p, r, :, at : at + width] = ref[:, column : column + width].astype(
+                    BF
+                )
+        at += width
+
+
+def pack(full, own, meta, groups):
+    ring, n = lax.axis_size("tensor"), lax.axis_size("dp")
+    rank = full[0].shape[0]
+    full_widths = [g.shape[1] // (ring * n) for g in full]
+    own_widths = [g.shape[1] // n for g in own]
+    packed, packed_own = pl.pallas_call(
+        functools.partial(pack_kernel, len(full), ring, groups),
+        out_shape=(
+            jax.ShapeDtypeStruct((ring, SEQ_DEVS, groups, rank, sum(full_widths)), BF),
+            jax.ShapeDtypeStruct((SEQ_DEVS, groups, rank, sum(own_widths)), BF),
+        ),
+        in_specs=specs(1, len(full) + len(own)),
+        out_specs=tuple(specs(0, 2)),
+        compiler_params=pltpu.CompilerParams(vmem_limit_bytes=VMEM_BYTES),
+        cost_estimate=pl.CostEstimate(flops=2 * US, bytes_accessed=2**20, transcendentals=0),
+    )(meta, *full, *own)
+    return Side(reduce_stages(packed, packed_own, full_widths, own_widths, groups))
+
+
+def reduce_stages(packed, packed_own, full_widths, own_widths, groups):
     ring, n = lax.axis_size("tensor"), lax.axis_size("dp")
     spot, data = lax.axis_index("tensor"), lax.axis_index("dp")
-    group, part = data // SEQ_DEVS, data % SEQ_DEVS
-    widths = [s.shape[1] // (ring * n) for s in stacks]
-    rank = stacks[0].shape[0]
-    joined = jnp.concatenate(
-        [s.reshape(rank, groups, SEQ_DEVS, ring, w) for s, w in zip(stacks, widths)], axis=4
-    )
-    joined = jnp.transpose(joined, (3, 2, 1, 0, 4))
-
-    def spot_block(k):
-        return lax.dynamic_index_in_dim(joined, (spot + k) % ring, 0, keepdims=False)
-
-    total = spot_block(0)
-    for k in range(1, ring):
-        moved = lax.ppermute(
-            spot_block(k).astype(BF), "tensor", [(i, (i + k) % ring) for i in range(ring)]
-        )
-        total = total + moved.astype(F32)
-
-    own = lax.dynamic_index_in_dim(total, part, 0, keepdims=False)
-    for e in range(1, SEQ_DEVS):
-        block = lax.dynamic_index_in_dim(total, part ^ e, 0, keepdims=False)
-        own = own + exchange(block.astype(BF), e).astype(F32)
-    pieces = [lax.dynamic_index_in_dim(own, group, 0, keepdims=False)]
+    group = data // SEQ_DEVS
+    wide = sum(full_widths)
+    landed = yield [
+        lax.ppermute(packed[k], "tensor", [(i, (i + k) % ring) for i in range(ring)])
+        for k in range(1, ring)
+    ]
+    total = sum([x.astype(F32) for x in landed], packed[0].astype(F32)).astype(BF)
+    total = jnp.concatenate([total, packed_own], axis=3)
+    landed = yield [exchange(total[e], e) for e in range(1, SEQ_DEVS)]
+    own = sum([x.astype(F32) for x in landed], total[0].astype(F32)).astype(BF)
+
+    def block(k):
+        return lax.dynamic_index_in_dim(own, (group + k) % groups, 0, keepdims=False)
+
+    flying = []
     for k in range(1, groups):
-        block = lax.dynamic_index_in_dim(own, (group + k) % groups, 0, keepdims=False)
-        pieces.append(
-            lax.ppermute(
-                block.astype(BF), "dp", [(i, (i + k * SEQ_DEVS) % n) for i in range(n)]
-            ).astype(F32)
-        )
-    return [(piece, (group - k) % groups) for k, piece in enumerate(pieces)], widths
-
-
-def reduce_own_columns(stacks, groups):
-    ring, n = lax.axis_size("tensor"), lax.axis_size("dp")
-    spot, data = lax.axis_index("tensor"), lax.axis_index("dp")
-    group, part = data // SEQ_DEVS, data % SEQ_DEVS
-    widths = [s.shape[1] // n for s in stacks]
-    rank = stacks[0].shape[0]
-    joined = jnp.concatenate(
-        [s.reshape(rank, SEQ_DEVS, groups, w) for s, w in zip(stacks, widths)], axis=3
-    )
-    joined = jnp.transpose(joined, (1, 2, 0, 3))
-    own = lax.dynamic_index_in_dim(joined, part, 0, keepdims=False)
-    for e in range(1, SEQ_DEVS):
-        block = lax.dynamic_index_in_dim(joined, part ^ e, 0, keepdims=False)
-        own = own + exchange(block.astype(BF), e).astype(F32)
-    pieces = []
-    mine = (data * ring + spot) % groups
+        pairs = [(i, (i + k * SEQ_DEVS) % n) for i in range(n)]
+        flying.append(lax.ppermute(block(k)[:, :wide], "dp", pairs))
     for k in range(groups):
         pairs = []
         for i in range(n):
             for z in range(ring):
                 r = (i // SEQ_DEVS + k) % groups
                 pairs.append((i * ring + z, z * n + (i % SEQ_DEVS) * groups + r))
-        block = lax.dynamic_index_in_dim(own, (group + k) % groups, 0, keepdims=False)
-        moved = lax.ppermute(block.astype(BF), ("dp", "tensor"), pairs).astype(F32)
-        pieces.append((moved, (mine - k) % groups))
-    return pieces, widths
+        flying.append(lax.ppermute(block(k)[:, wide:], ("dp", "tensor"), pairs))
+    landed = yield flying
+    full = [block(0)[:, :wide]] + list(landed[: groups - 1])
+    full = [(piece, (group - k) % groups) for k, piece in enumerate(full)]
+    mine = (data * ring + spot) % groups
+    cols = [(piece, (mine - k) % groups) for k, piece in enumerate(landed[groups - 1 :])]
+    return (full, full_widths), (cols, own_widths)
 
 
 def place(pieces, widths, seq_adapter):
@@ -455,12 +867,43 @@
     whole = 0.0
     for piece, sequence in pieces:
         slot = lax.dynamic_index_in_dim(seq_adapter, sequence, 0, keepdims=False)
-        whole = whole + jnp.where((slots == slot)[:, None, None], piece[None], 0.0)
+        whole = whole + jnp.where((slots == slot)[:, None, None], piece[None].astype(F32), 0.0)
     outs, at = [], 0
     for width in widths:
         outs.append(whole[:, :, at : at + width])
         at += width
     return outs
+
+
+def gather_first(shard, rows_in, data, small):
+    n, count = lax.axis_size("dp"), shard.shape[0]
+    if n != 8 or lax.axis_size("tensor") != 4:
+        whole = lax.all_gather(shard, "dp", axis=0, tiled=True)
+        return [whole], [0 * data], ring_gather(rows_in, "tensor"), (), small
+    half = count // 2
+    by_x, by_y, by_c = exchange(shard, 2), exchange(shard, 4), exchange(shard, 1)
+    ring = [rows_in, shift_one(rows_in, "tensor")]
+    by_x, by_y, by_c, ring[1], *small = lax.optimization_barrier(
+        (by_x, by_y, by_c, ring[1]) + small
+    )
+    corner_a, corner_b = exchange(by_x[:half], 4), exchange(by_y[half:], 2)
+    by_xc, by_yc = exchange(by_x, 1), exchange(by_y, 1)
+    ring.append(shift_one(ring[1], "tensor"))
+    corner_a, corner_b, by_xc, by_yc, ring[2] = lax.optimization_barrier(
+        (corner_a, corner_b, by_xc, by_yc, ring[2])
+    )
+    far_a, far_b = exchange(corner_a, 1), exchange(corner_b, 1)
+    ring.append(shift_one(ring[2], "tensor"))
+    pieces = [shard, by_c, by_x, by_xc, by_y, by_yc, corner_a, far_a, corner_b, far_b]
+    starts = [(data ^ e) * count for e in range(8)]
+    starts += [(data ^ e) * count + half for e in (6, 7)]
+    return pieces, starts, ring, (corner_a, corner_b), small
+
+
+def swap_heads(pieces):
+    across, far, near = exchange(pieces[2], 2), exchange(pieces[3], 2), exchange(pieces[1], 1)
+    across, far, near = lax.optimization_barrier((across, far, near))
+    return [pieces[0], near, across, exchange(far, 1)]
 
 
 def local(
@@ -516,82 +959,104 @@
     a_1, b_1 = pick(fc1_down), own_cols(pick(fc1_up), hidden_cols)
     a_2, b_2 = own_cols(pick(fc2_down), hidden_cols), pick(fc2_up)
 
-    w_qkv = lax.all_gather(qkv_weight, "dp", axis=0, tiled=True)
-    w_out = lax.all_gather(out_weight, "dp", axis=1, tiled=True)
-    w_fc1 = lax.all_gather(fc1_weight, "dp", axis=0, tiled=True)
-    w_fc2 = lax.all_gather(fc2_weight, "dp", axis=1, tiled=True)
-
-    def split(array):
-        return [array[k * rows : (k + 1) * rows] for k in range(ring)]
-
-    def up(low, matrix):
-        return FACTOR * dot(low.astype(BF), matrix)
+    n = lax.axis_size("dp")
+    shard = fc1_weight.shape[0]
+    chunks = hidden_cols // shard
+    fc_shard = jnp.concatenate(
+        [
+            jnp.transpose(fc1_weight.reshape(shard, chunks, shard), (1, 0, 2)).reshape(-1, shard),
+            fc2_weight,
+        ],
+        axis=0,
+    )
+    w_qkv, w_starts, h_pieces, corners, small = gather_first(
+        qkv_weight, hidden_in, data, (fc_shard, a_q, b_q, a_o, b_o, a_1, b_1, a_2, b_2, slopes)
+    )
+    fc_shard, a_q, b_q, a_o, b_o, a_1, b_1, a_2, b_2, slopes = small
+    w_starts = jnp.stack(w_starts).astype(jnp.int32)
+    held_out, *unused = lax.optimization_barrier((out_weight,) + corners)
+    w_out = lax.all_gather(held_out, "dp", axis=0, tiled=False)
 
     x = hidden_in.astype(F32)
-    normed1, unit1, inverse1 = norm_forward(x, ln1_gain, ln1_bias)
-    n1 = jnp.concatenate(ring_gather(normed1.astype(BF), "tensor"), axis=0)
-    gy = jnp.concatenate(ring_gather(cotangent, "tensor"), axis=0)
-    u1 = dot_nt(n1, a_q).astype(BF)
-    qkv = (dot(n1, w_qkv) + up(u1, b_q) + joined_bias).astype(BF)
-    pieces = []
-    for e in range(SEQ_DEVS):
-        piece = lax.dynamic_slice_in_dim(qkv, (part ^ e) * (heads * 3 * HD), heads * 3 * HD, 1)
-        pieces.append(exchange(piece, e) if e else piece)
+    unused, unit1, inverse1 = norm_forward(x, ln1_gain, ln1_bias)
+    h_pieces[-1], cotangent_held = lax.optimization_barrier((h_pieces[-1], cotangent))
+    gy = [cotangent, shift_one(cotangent_held, "tensor")]
+    pieces, u1, n1 = qkv_product(
+        h_pieces, ln1_gain[None], ln1_bias[None], a_q, b_q, joined_bias[None], w_qkv, w_starts, meta
+    )
+    pieces, gy = lax.optimization_barrier((pieces, gy))
+    gy.append(shift_one(gy[-1], "tensor"))
+    pieces = swap_heads(pieces)
+    fc_shard, pieces, gy = lax.optimization_barrier((fc_shard, pieces, gy))
+    gy += ring_gather(gy[-1], "tensor", ring - 3)[1:]
+    w_fc = lax.all_gather(fc_shard, "dp", axis=0, tiled=True)
+    w_fc = w_fc.reshape(n, 2 * chunks, shard, shard)
     ctx_rel, qkv_true, out_t, logs = attend_forward(pieces, meta, slopes, ring, rows)
+    ctx_rel, gy = lax.optimization_barrier((ctx_rel, gy))
     count = ring * rows
-    ctx = jnp.zeros((count, ctx_cols), BF)
-    for e in range(SEQ_DEVS):
-        piece = ctx_rel[e * count : (e + 1) * count]
-        piece = exchange(piece, e) if e else piece
-        ctx = lax.dynamic_update_slice_in_dim(ctx, piece, (part ^ e) * (heads * HD), 1)
-    u2 = dot_nt(ctx, a_o).astype(BF)
-    part_out = (dot(ctx, w_out) + up(u2, b_o)).astype(BF)
-    mid = x + (ring_scatter(split(part_out), "tensor") + output_bias)
+    pieces = swap_heads([ctx_rel[e * count : (e + 1) * count] for e in range(SEQ_DEVS)])
+    part_out, ctx, u2 = out_product(pieces, a_o, b_o, w_out, meta, ring)
+    loads = []
+
+    def load_beside(moved):
+        loads.append(moved)
+        if len(loads) == ring - 1:
+            moved, loads[-1] = lax.optimization_barrier(
+                (moved, load_to_vmem(hold(w_fc, loads[-2])))
+            )
+        return moved
+
+    mid = x + (ring_scatter(part_out, "tensor", (load_beside,)) + output_bias)
+    w_near = loads[-1]
 
     normed2, unit2, inverse2 = norm_forward(mid, ln2_gain, ln2_bias)
-    n2 = jnp.concatenate(ring_gather(normed2.astype(BF), "tensor"), axis=0)
-    u3 = dot_nt(n2, a_1).astype(BF)
-    act, slope = gelu_and_slope(dot(n2, w_fc1) + up(u3, b_1) + first_feed_bias)
-    act = act.astype(BF)
-    u4 = dot_nt(act, a_2).astype(BF)
-    part_mlp = (dot(act, w_fc2) + up(u4, b_2)).astype(BF)
-
-    gu4 = (FACTOR * dot_nt(gy, b_2)).astype(BF)
-    gact = dot_nt(gy, w_fc2) + dot(gu4, a_2)
-    gf = (gact * slope).astype(BF)
-    gu3 = (FACTOR * dot_nt(gf, b_1)).astype(BF)
-    part_in2 = (dot_nt(gf, w_fc1) + dot(gu3, a_1)).astype(BF)
-    grad_n2 = ring_scatter(split(part_in2), "tensor")
+    n2 = ring_gather(normed2.astype(BF), "tensor")
+    part_in2, part_mlp, fc_grads = [], [], []
+    for k in range(ring):
+        grad_pieces, out_pieces, fc_grads = mlp_both_ways(
+            n2[k : k + 1],
+            gy[k : k + 1],
+            a_1,
+            b_1,
+            a_2,
+            b_2,
+            first_feed_bias[None],
+            w_near,
+            fc_grads,
+        )
+        part_in2 += grad_pieces
+        part_mlp += out_pieces
+    g_b1, g_a2, g_a1, g_b2 = fc_grads
+    grad_n2 = ring_scatter(part_in2, "tensor")
     grad_mid = cotangent.astype(F32) + norm_backward(grad_n2, unit2, inverse2, ln2_gain)
-    gm = jnp.concatenate(ring_gather(grad_mid.astype(BF), "tensor"), axis=0)
-    layer_output = (mid + (ring_scatter(split(part_mlp), "tensor") + second_feed_bias)).astype(BF)
-
-    gu2 = (FACTOR * dot_nt(gm, b_o)).astype(BF)
-    gctx = (dot_nt(gm, w_out) + dot(gu2, a_o)).astype(BF)
-    pieces = []
-    for e in range(SEQ_DEVS):
-        piece = lax.dynamic_slice_in_dim(gctx, (part ^ e) * (heads * HD), heads * HD, 1)
-        pieces.append(exchange(piece, e) if e else piece)
+    gm = ring_gather(grad_mid.astype(BF), "tensor")
+
+    mlp_total, gm = lax.optimization_barrier((part_mlp[1], gm))
+    mlp_total = shift_one(mlp_total, "tensor")
+    pieces, g_bo, g_ao = gctx_product(gm, a_o, b_o, w_out, ctx, u2, meta)
+    early = pack([g_a1, g_b2, g_bo], [g_b1, g_a2, g_ao], meta, groups)
+    pieces = swap_heads(pieces)
     grad_rel = attend_backward(pieces, qkv_true, out_t, logs, meta, slopes, ring, rows)
-    gqkv = jnp.zeros((count, qkv_cols), BF)
-    for e in range(SEQ_DEVS):
-        piece = grad_rel[e * count : (e + 1) * count]
-        piece = exchange(piece, e) if e else piece
-        gqkv = lax.dynamic_update_slice_in_dim(gqkv, piece, (part ^ e) * (heads * 3 * HD), 1)
-    gu1 = (FACTOR * dot_nt(gqkv, b_q)).astype(BF)
-    part_in1 = (dot_nt(gqkv, w_qkv) + dot(gu1, a_q)).astype(BF)
-    grad_n1 = ring_scatter(split(part_in1), "tensor")
+    grad_rel, mlp_total = lax.optimization_barrier((grad_rel, mlp_total))
+    mlp_total = shift_one((mlp_total.astype(F32) + part_mlp[2].astype(F32)).astype(BF), "tensor")
+    early.step(grad_rel)
+    pieces = swap_heads([grad_rel[e * count : (e + 1) * count] for e in range(SEQ_DEVS)])
+    pieces, mlp_total = lax.optimization_barrier((pieces, mlp_total))
+    early.step(pieces[3])
+    mlp_total = ring_scatter([part_mlp[0], mlp_total] + part_mlp[3:], "tensor", first=True)
+    g_bq, g_aq, gu1, gqkv = joined_gradients(pieces, n1, b_q, u1, meta)
+    late = pack([g_aq], [g_bq], meta, groups)
+    part_in1 = gn1_product(gqkv, gu1, a_q, w_qkv, w_starts, ring)
+    part_in1, mlp_total = lax.optimization_barrier((part_in1, mlp_total))
+    layer_output = (mid + (mlp_total + second_feed_bias)).astype(BF)
+    early.step(part_in1[0])
+    grad_n1 = ring_scatter(part_in1, "tensor", (late,))
     hidden_grad = grad_mid + norm_backward(grad_n1, unit1, inverse1, ln1_gain)
 
-    full_pieces, full_widths = reduce_full_width(
-        [dot_tn(gu1, n1), FACTOR * dot_tn(u2, gm), dot_tn(gu3, n2), FACTOR * dot_tn(u4, gy)], groups
-    )
-    g_aq, g_bo, g_a1, g_b2 = place(full_pieces, full_widths, seq_adapter)
-    col_pieces, col_widths = reduce_own_columns(
-        [FACTOR * dot_tn(u1, gqkv), dot_tn(gu2, ctx), FACTOR * dot_tn(u3, gf), dot_tn(gu4, act)],
-        groups,
-    )
-    g_bq, g_ao, g_b1, g_a2 = place(col_pieces, col_widths, seq_adapter)
+    g_a1, g_b2, g_bo = place(*early.result[0], seq_adapter)
+    g_b1, g_a2, g_ao = place(*early.result[1], seq_adapter)
+    (g_aq,) = place(*late.result[0], seq_adapter)
+    (g_bq,) = place(*late.result[1], seq_adapter)
     return (layer_output, hidden_grad, g_aq, g_bq, g_ao, g_bo, g_a1, g_b1, g_a2, g_b2)
 
 

time: 572 us -> 497 us (0.87)
  waiting for transfers between devices: 318 us -> 218 us
  matrix products: 95.5 us -> 0 us
  Pallas kernels: 63.4 us -> 150 us
  starting transfers between devices: 29 us -> 61.6 us
    ppermute x24, waiting for transfers between devices: 254 us -> 154 us  [shift_one(): return lax.ppermute(array, axis, [(i, (i + 1) % n) for i in range(n)])]
    dot_general x32 -> x0, matrix products: 95.5 us -> none  [the longest x12 47.4 us: dot(): return jnp.dot(a, b, preferred_element_type=F32)]
    pallas_call x0 -> x12, Pallas kernels: none -> 85 us  [the longest x4 36.6 us: mlp_both_ways(): pl.pallas_call(functools.partial(mlp_kernel, count, len(before)), out_sha...]
    ppermute x24, starting transfers between devices: 6.93 us -> 20.8 us  [shift_one(): return lax.ppermute(array, axis, [(i, (i + 1) % n) for i in range(n)])]
    ppermute x18 -> x31, starting transfers between devices: 11.7 us -> 21.9 us  [exchange(): return lax.ppermute(array, 'dp', [(i, i ^ distance) for i in range(n)])]
    ppermute x6 -> x12, waiting for transfers between devices: 9.45 us -> 0.03 us  [the longest x6 0.02 us: reduce_stages(): lax.ppermute(packed[k], 'tensor', [(i, (i + k) % ring) for i in range(rin...]
    ppermute x6 -> x12, starting transfers between devices: 10.2 us -> 18.8 us  [the longest x6 11.2 us: reduce_stages(): lax.ppermute(packed[k], 'tensor', [(i, (i + k) % ring) for i in range(rin...]
    ppermute x18 -> x31, waiting for transfers between devices: 52.5 us -> 59.5 us  [exchange(): return lax.ppermute(array, 'dp', [(i, i ^ distance) for i in range(n)])]
  transfers between devices with their start and end apart: 52 -> 69, of which waited for: 33 -> 34; matrix products, arithmetic and copies ran while one was open for 15% -> 6% of each run, Pallas kernels for 6% -> 29%
where the time goes in v2:
time: 497 us; the launch traced here: 488 us
  waiting for transfers between devices  218 us (44%)
  Pallas kernels  150 us (30%)
  starting transfers between devices  61.6 us (12%)
  local copies, waits for them, and re-layouts  24.6 us (5%)
  between operations  17.4 us (4%)
  other arithmetic  16.3 us (3%)
    ppermute x24, waiting for transfers between devices, shift_one(): return lax.ppermute(array, axis, [(i, (i + 1) % n) for i in range(n)])  154 us
    ppermute x31, waiting for transfers between devices, exchange(): return lax.ppermute(array, 'dp', [(i, i ^ distance) for i in range(n)])  59.5 us
    pallas_call x4, Pallas kernels, mlp_both_ways(): pl.pallas_call(functools.partial(mlp_kernel, count, len(before)), out_sha...  36.6 us
    pallas_call x1, Pallas kernels, attend_forward(): pl.pallas_call(functools.partial(forward_kernel, heads, parts, ring, rows...  33.2 us
    pallas_call x1, Pallas kernels, attend_backward(): pl.pallas_call(functools.partial(backward_kernel, heads, parts, ring, row...  31.5 us
    ppermute x31, starting transfers between devices, exchange(): return lax.ppermute(array, 'dp', [(i, i ^ distance) for i in range(n)])  21.9 us
    ppermute x24, starting transfers between devices, shift_one(): return lax.ppermute(array, axis, [(i, (i + 1) % n) for i in range(n)])  20.8 us
    ppermute x6, starting transfers between devices, reduce_stages(): lax.ppermute(packed[k], 'tensor', [(i, (i + k) % ring) for i in range(rin...  11.2 us
  transfers between devices with their start and end apart: 69, of which 34 were waited for; matrix products, arithmetic and copies ran while one was open for 6% of the time, Pallas kernels for 29%

profile of v2, /device:TPU:0, one launch (start us, length us, event | category | flops | bytes accessed | tf_op | source)
XLA Modules:
  0.0 487.8 jit_solution(5664451188861004499)
XLA Ops:
  7.2 3.0 collective-permute-start
  26.5 1.8 collective-permute-done.3.refs_1_
  34.8 8.7 %collective-permute-done.4.refs_15_.refs_6_ = bf16[128,1536]{1,0:T(8,128)(2,1)S(1)} collective-permute-done((bf16[128,1536]{1,0:T(8,128)(2,1)S(1)}, bf16[128,1536]{1,0:T(8,128)(2,1)S(1)}, u32[]{:S(2)}, u32[]{:S(2)}) %collective-permute-start.4) | collective-permute-done | bytes 393248 | tf_op jit(solution)/shard_map/ppermute | solution.py:109
  47.9 14.1 %collective-permute-done.9.refs_3_ = bf16[128,2048]{1,0:T(8,128)(2,1)S(1)} collective-permute-done((bf16[128,2048]{1,0:T(8,128)(2,1)}, bf16[128,2048]{1,0:T(8,128)(2,1)S(1)}, u32[]{:S(2)}, u32[]{:S(2)}) %collective-permute-start.9) | collective-permute-done | bytes 524320 | tf_op jit(solution)/shard_map/ppermute | solution.py:65
  64.6 11.1 %shard_map.303 = (bf16[512,384]{1,0:T(8,128)(2,1)}, bf16[512,384]{1,0:T(8,128)(2,1)}, bf16[512,384]{1,0:T(8,128)(2,1)}, bf16[512,384]{1,0:T(8,128)(2,1)}, bf16[5...) custom-call(s32[5]{0:T(128)} %pad_add_fusion.meta_ref, s32[10]{0:T(128)} %stack.51.starts_ref, bf16[128,2048]{1,0:T(8,128)(2,1)} %refs_0_.2, ...), custom_call_target="tpu_custom_call" | custom-call | flops 2000000000 | bytes 1048576 | tf_op jit(solution)/shard_map/pallas_call | solution.py:486
  78.7 10.2 %collective-permute-done.13.refs_2_ = bf16[512,384]{1,0:T(8,128)(2,1)S(1)} collective-permute-done((bf16[512,384]{1,0:T(8,128)(2,1)}, bf16[512,384]{1,0:T(8,128)(2,1)S(1)}, u32[]{:S(2)}, u32[]{:S(2)}) %collective-permute-start.13) | collective-permute-done | bytes 393248 | tf_op jit(solution)/shard_map/ppermute | solution.py:109
  89.0 4.8 collective-permute-done.14
  95.8 33.2 %shard_map.304 = (bf16[2048,128]{1,0:T(8,128)(2,1)}, bf16[2048,384]{1,0:T(8,128)(2,1)}, f32[128,2048]{1,0:T(8,128)}, f32[8,2048]{1,0:T(8,128)}) custom-call(s32[5]{0:T(128)} %pad_add_fusion.meta_ref, f32[2]{0:T(128)} %multiply_exponential_fusion.slope_ref, bf16[512,384]{1,0:T(8,128)(2,1)} %get-tuple-element.187.refs_0_, bf16[512,384]{1,0:T(8,128)(2,1)} %copy-done.57, ...), custom_call_target="tpu_custom_call" | custom-call | flops 2000000000 | bytes 5242880 | tf_op jit(solution)/shard_map/pallas_call | solution.py:364
  129.0 2.0 fusion.41
  133.0 4.3 collective-permute-done.19.refs_2_
  137.4 3.1 collective-permute-done.20
  142.6 5.7 %shard_map.305 = (bf16[128,2048]{1,0:T(8,128)(2,1)}, bf16[128,2048]{1,0:T(8,128)(2,1)}, bf16[128,2048]{1,0:T(8,128)(2,1)}, bf16[128,2048]{1,0:T(8,128)(2,1)}, bf...) custom-call(s32[5]{0:T(128)} %pad_add_fusion.meta_ref, bf16[512,128]{1,0:T(8,128)(2,1)} %get-tuple-element.324.refs_0_, ...), custom_call_target="tpu_custom_call" | custom-call | flops 1073741824 | bytes 8388608 | tf_op jit(solution)/shard_map/pallas_call | solution.py:561
  148.4 16.3 %collective-permute-done.23 = bf16[128,2048]{1,0:T(8,128)(2,1)S(1)} collective-permute-done((bf16[128,2048]{1,0:T(8,128)(2,1)}, bf16[128,2048]{1,0:T(8,128)(2,1)S(1)}, u32[]{:S(2)}, u32[]{:S(2)}) %collective-permute-start.23) | collective-permute-done | bytes 524320 | tf_op jit(solution)/shard_map/ppermute | solution.py:65
  167.6 13.6 %collective-permute-done.24 = bf16[128,2048]{1,0:T(8,128)(2,1)S(1)} collective-permute-done((bf16[128,2048]{1,0:T(8,128)(2,1)S(1)}, bf16[128,2048]{1,0:T(8,128)(2,1)S(1)}, u32[]{:S(2)}, u32[]{:S(2)}) %collective-permute-start.24) | collective-permute-done | bytes 524320 | tf_op jit(solution)/shard_map/ppermute | solution.py:65
  181.4 4.9 all-gather.4.cloned.1.call-done
  186.3 6.0 %shard_map.306.refs_7_ = bf16[8,16,256,256]{3,2,1,0:T(8,128)(2,1)S(1)} custom-call(bf16[8,16,256,256]{3,2,1,0:T(8,128)(2,1)} %bitcast.99), custom_call_target="tpu_custom_call" | custom-call | flops 5000000000 | bytes 16777216 | tf_op jit(solution)/shard_map/pallas_call | solution.py:522
  192.3 3.4 collective-permute-done.25
  197.2 9.1 %shard_map.307 = (bf16[128,2048]{1,0:T(8,128)(2,1)S(1)}, bf16[128,2048]{1,0:T(8,128)(2,1)S(1)}, f32[16,2048]{1,0:T(8,128)S(1)}, f32[16,2048]{1,0:T(8,128)S(1)}, ...) custom-call(bf16[128,2048]{1,0:T(8,128)(2,1)S(1)} %add_convert_fusion.7.refs_0_, bf16[128,2048]{1,0:T(8,128)(2,1)S(1)} %copy-done.6, ...), custom_call_target="tpu_custom_call" | custom-call | flops 10000000000 | bytes 16777216 | tf_op jit(solution)/shard_map/pallas_call | solution.py:641
  207.1 3.4 collective-permute-done.26.refs_0_
  210.6 9.2 %shard_map.308 = (bf16[128,2048]{1,0:T(8,128)(2,1)S(1)}, bf16[128,2048]{1,0:T(8,128)(2,1)S(1)}, f32[16,2048]{1,0:T(8,128)S(1)}, f32[16,2048]{1,0:T(8,128)S(1)}, ...) custom-call(bf16[128,2048]{1,0:T(8,128)(2,1)S(1)} %collective-permute-done.26.refs_0_, bf16[128,2048]{1,0:T(8,128)(2,1)S(1)} %copy-done.11, ...), custom_call_target="tpu_custom_call" | custom-call | flops 10000000000 | bytes 16777216 | tf_op jit(solution)/shard_map/pallas_call | solution.py:641
  220.6 13.1 %collective-permute-start.27 = (bf16[128,2048]{1,0:T(8,128)(2,1)S(1)}, bf16[128,2048]{1,0:T(8,128)(2,1)S(1)}, u32[]{:S(2)}, u32[]{:S(2)}) collective-permute-start(bf16[128,2048]{1,0:T(8,128)(2,1)S(1)} %get-tuple-element.221), channel_id=1, source_target_pairs={{0,1},{1,2},{2,3},{3,0},{4,5},{5,6},{6,7},{7,4},{8,9},{9,10},{10,1... | collective-permute-start | bytes 1572872 | tf_op jit(solution)/shard_map/ppermute | solution.py:65
  234.1 9.2 %shard_map.309 = (bf16[128,2048]{1,0:T(8,128)(2,1)S(1)}, bf16[128,2048]{1,0:T(8,128)(2,1)S(1)}, f32[16,2048]{1,0:T(8,128)S(1)}, f32[16,2048]{1,0:T(8,128)S(1)}, ...) custom-call(bf16[128,2048]{1,0:T(8,128)(2,1)S(1)} %collective-permute-done.28.refs_0_, bf16[128,2048]{1,0:T(8,128)(2,1)S(1)} %copy-done.15, ...), custom_call_target="tpu_custom_call" | custom-call | flops 10000000000 | bytes 16777216 | tf_op jit(solution)/shard_map/pallas_call | solution.py:641
  243.2 5.7 %collective-permute-done.27 = bf16[128,2048]{1,0:T(8,128)(2,1)S(1)} collective-permute-done((bf16[128,2048]{1,0:T(8,128)(2,1)S(1)}, bf16[128,2048]{1,0:T(8,128)(2,1)S(1)}, u32[]{:S(2)}, u32[]{:S(2)}) %collective-permute-start.27) | collective-permute-done | bytes 524320 | tf_op jit(solution)/shard_map/ppermute | solution.py:65
  249.1 11.0 %collective-permute-done.30.refs_0_ = bf16[128,2048]{1,0:T(8,128)(2,1)S(1)} collective-permute-done((bf16[128,2048]{1,0:T(8,128)(2,1)S(1)}, bf16[128,2048]{1,0:T(8,128)(2,1)S(1)}, u32[]{:S(2)}, u32[]{:S(2)}) %collective-permute-start.30) | collective-permute-done | bytes 524320 | tf_op jit(solution)/shard_map/ppermute | solution.py:65
  260.2 9.2 %shard_map.310 = (bf16[128,2048]{1,0:T(8,128)(2,1)S(1)}, bf16[128,2048]{1,0:T(8,128)(2,1)S(1)}, f32[16,2048]{1,0:T(8,128)S(1)}, f32[16,2048]{1,0:T(8,128)S(1)}, ...) custom-call(bf16[128,2048]{1,0:T(8,128)(2,1)S(1)} %collective-permute-done.30.refs_0_, bf16[128,2048]{1,0:T(8,128)(2,1)S(1)} %copy-done.17, ...), custom_call_target="tpu_custom_call" | custom-call | flops 10000000000 | bytes 16777216 | tf_op jit(solution)/shard_map/pallas_call | solution.py:641
  269.6 11.9 %collective-permute-done.31 = bf16[128,2048]{1,0:T(8,128)(2,1)S(1)} collective-permute-done((bf16[128,2048]{1,0:T(8,128)(2,1)S(1)}, bf16[128,2048]{1,0:T(8,128)(2,1)S(1)}, u32[]{:S(2)}, u32[]{:S(2)}) %collective-permute-start.31) | collective-permute-done | bytes 524320 | tf_op jit(solution)/shard_map/ppermute | solution.py:65
  282.8 12.3 %collective-permute-done.32.refs_1_ = bf16[128,2048]{1,0:T(8,128)(2,1)S(1)} collective-permute-done((bf16[128,2048]{1,0:T(8,128)(2,1)S(1)}, bf16[128,2048]{1,0:T(8,128)(2,1)S(1)}, u32[]{:S(2)}, u32[]{:S(2)}) %collective-permute-start.32) | collective-permute-done | bytes 524320 | tf_op jit(solution)/shard_map/ppermute | solution.py:65
  295.1 13.4 %collective-permute-done.33.refs_2_ = bf16[128,2048]{1,0:T(8,128)(2,1)S(1)} collective-permute-done((bf16[128,2048]{1,0:T(8,128)(2,1)S(1)}, bf16[128,2048]{1,0:T(8,128)(2,1)S(1)}, u32[]{:S(2)}, u32[]{:S(2)}) %collective-permute-start.33) | collective-permute-done | bytes 524320 | tf_op jit(solution)/shard_map/ppermute | solution.py:65
  311.0 8.5 %collective-permute-done.34.refs_3_ = bf16[128,2048]{1,0:T(8,128)(2,1)} collective-permute-done((bf16[128,2048]{1,0:T(8,128)(2,1)S(1)}, bf16[128,2048]{1,0:T(8,128)(2,1)}, u32[]{:S(2)}, u32[]{:S(2)}) %collective-permute-start.34) | collective-permute-done | bytes 524320 | tf_op jit(solution)/shard_map/ppermute | solution.py:65
  319.6 6.7 %shard_map.311 = (bf16[512,128]{1,0:T(8,128)(2,1)}, bf16[512,128]{1,0:T(8,128)(2,1)}, bf16[512,128]{1,0:T(8,128)(2,1)}, bf16[512,128]{1,0:T(8,128)(2,1)}, f32[16,2048]{1,0:T(8,128)}, /*index=5*/f32[16,512]{1,0:T(8,128)}) custom-call(s32[5]{0:T(128)} %pad_add_fusion.meta_ref, bf16[128,2048]{1,0:T(8,128)(2,1)} %copy-done.29, bf16[128,2048]{1,0:T(8,128)(2,1)} %copy-done.38, ...), custom_call_target="tpu_custom_call" | custom-call | flops 1073741824 | bytes 8388608 | tf_op jit(solution)/shard_map/pallas_call | solution.py:694
  326.3 4.2 collective-permute-start.35
  330.6 2.1 shard_map.316
  333.6 2.0 collective-permute-done.36
  338.4 2.3 collective-permute-start.60
  341.4 31.5 %shard_map.312 = bf16[2048,384]{1,0:T(8,128)(2,1)} custom-call(s32[5]{0:T(128)} %pad_add_fusion.meta_ref, f32[2]{0:T(128)} %multiply_exponential_fusion.slope_ref, bf16[512,128]{1,0:T(8,128)(2,1)} %get-tuple-element.241.refs_0_, bf16[512,128]{1,0:T(8,128)(2,1)} %copy-done.59, bf16[512,128]{1,0:T(8,128)(2,1)} %copy-done.58, bf16[512,128]{1,0:T(8,128)(2,1)} %copy-done.62, ...), custom_call_target="tpu_custom_call" | custom-call | flops 2000000000 | bytes 5242880 | tf_op jit(solution)/shard_map/pallas_call | solution.py:391
  372.9 2.3 fusion.40
  378.0 9.2 %collective-permute-done.40.refs_2_ = bf16[512,384]{1,0:T(8,128)(2,1)S(1)} collective-permute-done((bf16[512,384]{1,0:T(8,128)(2,1)S(1)}, bf16[512,384]{1,0:T(8,128)(2,1)S(1)}, u32[]{:S(2)}, u32[]{:S(2)}) %collective-permute-start.40) | collective-permute-done | bytes 393248 | tf_op jit(solution)/shard_map/ppermute | solution.py:109
  387.2 7.3 %collective-permute-done.41 = bf16[512,384]{1,0:T(8,128)(2,1)S(1)} collective-permute-done((bf16[512,384]{1,0:T(8,128)(2,1)S(1)}, bf16[512,384]{1,0:T(8,128)(2,1)S(1)}, u32[]{:S(2)}, u32[]{:S(2)}) %collective-permute-start.41) | collective-permute-done | bytes 393248 | tf_op jit(solution)/shard_map/ppermute | solution.py:109
  397.6 2.6 collective-permute-done.62
  402.6 4.4 shard_map.313
  411.4 2.1 collective-permute-start.50
  414.1 10.6 %shard_map.314 = (bf16[128,2048]{1,0:T(8,128)(2,1)}, bf16[128,2048]{1,0:T(8,128)(2,1)}, bf16[128,2048]{1,0:T(8,128)(2,1)}, bf16[128,2048]{1,0:T(8,128)(2,1)}) custom-call(s32[10]{0:T(128)} %stack.51.starts_ref, bf16[512,1536]{1,0:T(8,128)(2,1)} %get-tuple-element.264.q_ref, bf16[512,16]{1,0:T(8,128)(2,1)} %get-tuple-element.265.gu_ref, ...), custom_call_target="tpu_custom_call" | custom-call | flops 6000000000 | bytes 6291456 | tf_op jit(solution)/shard_map/pallas_call | solution.py:768
  424.8 3.4 collective-permute-start.66
  428.4 3.3 collective-permute-start.51
  433.7 13.8 %collective-permute-done.46 = bf16[128,2048]{1,0:T(8,128)(2,1)S(1)} collective-permute-done((bf16[128,2048]{1,0:T(8,128)(2,1)S(1)}, bf16[128,2048]{1,0:T(8,128)(2,1)S(1)}, u32[]{:S(2)}, u32[]{:S(2)}) %collective-permute-start.46) | collective-permute-done | bytes 524320 | tf_op jit(solution)/shard_map/ppermute | solution.py:65
  451.9 10.8 %collective-permute-done.47 = bf16[128,2048]{1,0:T(8,128)(2,1)S(1)} collective-permute-done((bf16[128,2048]{1,0:T(8,128)(2,1)S(1)}, bf16[128,2048]{1,0:T(8,128)(2,1)S(1)}, u32[]{:S(2)}, u32[]{:S(2)}) %collective-permute-start.47) | collective-permute-done | bytes 524320 | tf_op jit(solution)/shard_map/ppermute | solution.py:65
  464.2 2.4 collective-permute-start.57
  466.6 10.5 %collective-permute-done.48 = bf16[128,2048]{1,0:T(8,128)(2,1)S(1)} collective-permute-done((bf16[128,2048]{1,0:T(8,128)(2,1)S(1)}, bf16[128,2048]{1,0:T(8,128)(2,1)S(1)}, u32[]{:S(2)}, u32[]{:S(2)}) %collective-permute-start.48) | collective-permute-done | bytes 524320 | tf_op jit(solution)/shard_map/ppermute | solution.py:65
  (312 shorter events, 76.6 us)
Async XLA Ops:
  7.2 134.8 %all-gather.6.cloned.1.call-start = ((), (), s32[]{:S(2)}) async-start(), calls=%async_computation.1 | async-start | bytes 2359296 | tf_op jit(solution)/shard_map/all_gather | solution.py:978
  7.2 21.0 %collective-permute-start = (bf16[256,1536]{1,0:T(8,128)(2,1)}, bf16[256,1536]{1,0:T(8,128)(2,1)S(1)}, u32[]{:S(2)}, u32[]{:S(2)}) collective-permute-start(bf16[256,1536]{1,0:T(8,128)(2,1)} %refs_0_.3), channel_id=1, source_target_pairs={{0,8},{4,12},{8,0},{12,4},{16,24},{20,28},{24,16},{28,20},{1,9},{5... | collective-permute-start | bytes 2359304 | tf_op jit(solution)/shard_map/ppermute | solution.py:109
  10.3 19.3 %collective-permute-start.1 = (bf16[256,1536]{1,0:T(8,128)(2,1)}, bf16[256,1536]{1,0:T(8,128)(2,1)}, u32[]{:S(2)}, u32[]{:S(2)}) collective-permute-start(bf16[256,1536]{1,0:T(8,128)(2,1)} %refs_0_.3), channel_id=1, source_target_pairs={{0,16},{4,20},{8,24},{12,28},{16,0},{20,4},{24,8},{28,12},{1,17},{... | collective-permute-start | bytes 2359304 | tf_op jit(solution)/shard_map/ppermute | solution.py:109
  11.8 17.8 %collective-permute-start.2 = (bf16[256,1536]{1,0:T(8,128)(2,1)}, bf16[256,1536]{1,0:T(8,128)(2,1)}, u32[]{:S(2)}, u32[]{:S(2)}) collective-permute-start(bf16[256,1536]{1,0:T(8,128)(2,1)} %refs_0_.3), channel_id=1, source_target_pairs={{0,4},{4,0},{8,12},{12,8},{16,20},{20,16},{24,28},{28,24},{1,5},{5... | collective-permute-start | bytes 2359304 | tf_op jit(solution)/shard_map/ppermute | solution.py:109
  11.8 16.5 %collective-permute-start.3 = (bf16[128,2048]{1,0:T(8,128)(2,1)}, bf16[128,2048]{1,0:T(8,128)(2,1)}, u32[]{:S(2)}, u32[]{:S(2)}) collective-permute-start(bf16[128,2048]{1,0:T(8,128)(2,1)} %refs_0_.2), channel_id=1, source_target_pairs={{0,1},{1,2},{2,3},{3,0},{4,5},{5,6},{6,7},{7,4},{8,9},{9,10},{10,1... | collective-permute-start | bytes 1572872 | tf_op jit(solution)/shard_map/ppermute | solution.py:65
  29.6 16.4 %collective-permute-start.6 = (bf16[256,1536]{1,0:T(8,128)(2,1)S(1)}, bf16[256,1536]{1,0:T(8,128)(2,1)S(1)}, u32[]{:S(2)}, u32[]{:S(2)}) collective-permute-start(bf16[256,1536]{1,0:T(8,128)(2,1)S(1)} %collective-permute-done.refs_11_.refs_2_), channel_id=1, source_target_pairs={{0,4},{4,0},{8,12},{12,8},{16,20},{20,16},{24,28},{28,24},{1,5},{5... | collective-permute-start | bytes 2359304 | tf_op jit(solution)/shard_map/ppermute | solution.py:109
  29.6 17.2 %collective-permute-start.7 = (bf16[256,1536]{1,0:T(8,128)(2,1)}, bf16[256,1536]{1,0:T(8,128)(2,1)S(1)}, u32[]{:S(2)}, u32[]{:S(2)}) collective-permute-start(bf16[256,1536]{1,0:T(8,128)(2,1)} %collective-permute-done.1.refs_13_.refs_4_), channel_id=1, source_target_pairs={{0,4},{4,0},{8,12},{12,8},{16,20},{20,16},{24,28},{28,24},{1,5},{5... | collective-permute-start | bytes 2359304 | tf_op jit(solution)/shard_map/ppermute | solution.py:109
  30.1 15.9 %collective-permute-start.8 = (bf16[128,2048]{1,0:T(8,128)(2,1)}, bf16[128,2048]{1,0:T(8,128)(2,1)S(1)}, u32[]{:S(2)}, u32[]{:S(2)}) collective-permute-start(bf16[128,2048]{1,0:T(8,128)(2,1)} %collective-permute-done.3.refs_1_), channel_id=1, source_target_pairs={{0,1},{1,2},{2,3},{3,0},{4,5},{5,6},{6,7},{7,4},{8,9},{9,10},{10,1... | collective-permute-start | bytes 1572872 | tf_op jit(solution)/shard_map/ppermute | solution.py:65
  46.8 139.4 %all-gather.4.cloned.1.call-start = ((), (), s32[]{:S(2)}) async-start(), calls=%async_computation | async-start | bytes 18874368 | tf_op jit(solution)/shard_map/all_gather | solution.py:992
  46.9 15.1 %collective-permute-start.9 = (bf16[128,2048]{1,0:T(8,128)(2,1)}, bf16[128,2048]{1,0:T(8,128)(2,1)S(1)}, u32[]{:S(2)}, u32[]{:S(2)}) collective-permute-start(bf16[128,2048]{1,0:T(8,128)(2,1)} %copy-done.36), channel_id=1, source_target_pairs={{0,1},{1,2},{2,3},{3,0},{4,5},{5,6},{6,7},{7,4},{8,9},{9,10},{10,1... | collective-permute-start | bytes 1572872 | tf_op jit(solution)/shard_map/ppermute | solution.py:65
  47.4 17.2 %collective-permute-start.10 = (bf16[128,1536]{1,0:T(8,128)(2,1)}, bf16[128,1536]{1,0:T(8,128)(2,1)}, u32[]{:S(2)}, u32[]{:S(2)}) collective-permute-start(bf16[128,1536]{1,0:T(8,128)(2,1)} %copy-done.43), channel_id=1, source_target_pairs={{0,4},{4,0},{8,12},{12,8},{16,20},{20,16},{24,28},{28,24},{1,5},{5... | collective-permute-start | bytes 1179656 | tf_op jit(solution)/shard_map/ppermute | solution.py:109
  47.4 17.2 %collective-permute-start.11 = (bf16[128,1536]{1,0:T(8,128)(2,1)}, bf16[128,1536]{1,0:T(8,128)(2,1)}, u32[]{:S(2)}, u32[]{:S(2)}) collective-permute-start(bf16[128,1536]{1,0:T(8,128)(2,1)} %copy-done.44), channel_id=1, source_target_pairs={{0,4},{4,0},{8,12},{12,8},{16,20},{20,16},{24,28},{28,24},{1,5},{5... | collective-permute-start | bytes 1179656 | tf_op jit(solution)/shard_map/ppermute | solution.py:109
  62.8 13.9 %collective-permute-start.12 = (bf16[128,2048]{1,0:T(8,128)(2,1)S(1)}, bf16[128,2048]{1,0:T(8,128)(2,1)S(1)}, u32[]{:S(2)}, u32[]{:S(2)}) collective-permute-start(bf16[128,2048]{1,0:T(8,128)(2,1)S(1)} %copy-done.6), channel_id=1, source_target_pairs={{0,1},{1,2},{2,3},{3,0},{4,5},{5,6},{6,7},{7,4},{8,9},{9,10},{10,1... | collective-permute-start | bytes 1572872 | tf_op jit(solution)/shard_map/ppermute | solution.py:65
  77.6 16.2 %collective-permute-start.14 = (bf16[512,384]{1,0:T(8,128)(2,1)}, bf16[512,384]{1,0:T(8,128)(2,1)S(1)}, u32[]{:S(2)}, u32[]{:S(2)}) collective-permute-start(bf16[512,384]{1,0:T(8,128)(2,1)} %get-tuple-element.180), channel_id=1, source_target_pairs={{0,8},{4,12},{8,0},{12,4},{16,24},{20,28},{24,16},{28,20},{1,9},{5... | collective-permute-start | bytes 1179656 | tf_op jit(solution)/shard_map/ppermute | solution.py:109
  78.7 15.1 %collective-permute-start.15 = (bf16[512,384]{1,0:T(8,128)(2,1)}, bf16[512,384]{1,0:T(8,128)(2,1)S(1)}, u32[]{:S(2)}, u32[]{:S(2)}) collective-permute-start(bf16[512,384]{1,0:T(8,128)(2,1)} %get-tuple-element.181), channel_id=1, source_target_pairs={{0,4},{4,0},{8,12},{12,8},{16,20},{20,16},{24,28},{28,24},{1,5},{5... | collective-permute-start | bytes 1179656 | tf_op jit(solution)/shard_map/ppermute | solution.py:109
  78.7 16.1 %collective-permute-start.17 = (bf16[128,2048]{1,0:T(8,128)(2,1)S(1)}, bf16[128,2048]{1,0:T(8,128)(2,1)S(1)}, u32[]{:S(2)}, u32[]{:S(2)}) collective-permute-start(bf16[128,2048]{1,0:T(8,128)(2,1)S(1)} %collective-permute-done.12.refs_1_), channel_id=1, source_target_pairs={{0,1},{1,2},{2,3},{3,0},{4,5},{5,6},{6,7},{7,4},{8,9},{9,10},{10,1... | collective-permute-start | bytes 1572872 | tf_op jit(solution)/shard_map/ppermute | solution.py:65
  95.7 33.3 %collective-permute-start.18 = (bf16[128,2048]{1,0:T(8,128)(2,1)S(1)}, bf16[128,2048]{1,0:T(8,128)(2,1)S(1)}, u32[]{:S(2)}, u32[]{:S(2)}) collective-permute-start(bf16[128,2048]{1,0:T(8,128)(2,1)S(1)} %collective-permute-done.17.refs_1_), channel_id=1, source_target_pairs={{0,1},{1,2},{2,3},{3,0},{4,5},{5,6},{6,7},{7,4},{8,9},{9,10},{10,1... | collective-permute-start | bytes 1572872 | tf_op jit(solution)/shard_map/ppermute | solution.py:65
  148.3 16.4 %collective-permute-start.23 = (bf16[128,2048]{1,0:T(8,128)(2,1)}, bf16[128,2048]{1,0:T(8,128)(2,1)S(1)}, u32[]{:S(2)}, u32[]{:S(2)}) collective-permute-start(bf16[128,2048]{1,0:T(8,128)(2,1)} %get-tuple-element.202), channel_id=1, source_target_pairs={{0,1},{1,2},{2,3},{3,0},{4,5},{5,6},{6,7},{7,4},{8,9},{9,10},{10,1... | collective-permute-start | bytes 1572872 | tf_op jit(solution)/shard_map/ppermute | solution.py:65
  165.9 15.3 %collective-permute-start.24 = (bf16[128,2048]{1,0:T(8,128)(2,1)S(1)}, bf16[128,2048]{1,0:T(8,128)(2,1)S(1)}, u32[]{:S(2)}, u32[]{:S(2)}) collective-permute-start(bf16[128,2048]{1,0:T(8,128)(2,1)S(1)} %add_convert_fusion.9), channel_id=1, source_target_pairs={{0,1},{1,2},{2,3},{3,0},{4,5},{5,6},{6,7},{7,4},{8,9},{9,10},{10,1... | collective-permute-start | bytes 1572872 | tf_op jit(solution)/shard_map/ppermute | solution.py:65
  181.3 14.4 %collective-permute-start.25 = (bf16[128,2048]{1,0:T(8,128)(2,1)S(1)}, bf16[128,2048]{1,0:T(8,128)(2,1)S(1)}, u32[]{:S(2)}, u32[]{:S(2)}) collective-permute-start(bf16[128,2048]{1,0:T(8,128)(2,1)S(1)} %add_convert_fusion.8), channel_id=1, source_target_pairs={{0,1},{1,2},{2,3},{3,0},{4,5},{5,6},{6,7},{7,4},{8,9},{9,10},{10,1... | collective-permute-start | bytes 1572872 | tf_op jit(solution)/shard_map/ppermute | solution.py:65
  196.8 13.7 %collective-permute-start.26 = (bf16[128,2048]{1,0:T(8,128)(2,1)S(1)}, bf16[128,2048]{1,0:T(8,128)(2,1)S(1)}, u32[]{:S(2)}, u32[]{:S(2)}) collective-permute-start(bf16[128,2048]{1,0:T(8,128)(2,1)S(1)} %add_convert_fusion.7.refs_0_), channel_id=1, source_target_pairs={{0,1},{1,2},{2,3},{3,0},{4,5},{5,6},{6,7},{7,4},{8,9},{9,10},{10,1... | collective-permute-start | bytes 1572872 | tf_op jit(solution)/shard_map/ppermute | solution.py:65
  210.5 23.2 %collective-permute-start.28 = (bf16[128,2048]{1,0:T(8,128)(2,1)S(1)}, bf16[128,2048]{1,0:T(8,128)(2,1)S(1)}, u32[]{:S(2)}, u32[]{:S(2)}) collective-permute-start(bf16[128,2048]{1,0:T(8,128)(2,1)S(1)} %collective-permute-done.26.refs_0_), channel_id=1, source_target_pairs={{0,1},{1,2},{2,3},{3,0},{4,5},{5,6},{6,7},{7,4},{8,9},{9,10},{10,1... | collective-permute-start | bytes 1572872 | tf_op jit(solution)/shard_map/ppermute | solution.py:65
  220.6 28.4 %collective-permute-start.27 = (bf16[128,2048]{1,0:T(8,128)(2,1)S(1)}, bf16[128,2048]{1,0:T(8,128)(2,1)S(1)}, u32[]{:S(2)}, u32[]{:S(2)}) collective-permute-start(bf16[128,2048]{1,0:T(8,128)(2,1)S(1)} %get-tuple-element.221), channel_id=1, source_target_pairs={{0,1},{1,2},{2,3},{3,0},{4,5},{5,6},{6,7},{7,4},{8,9},{9,10},{10,1... | collective-permute-start | bytes 1572872 | tf_op jit(solution)/shard_map/ppermute | solution.py:65
  233.7 26.5 %collective-permute-start.30 = (bf16[128,2048]{1,0:T(8,128)(2,1)S(1)}, bf16[128,2048]{1,0:T(8,128)(2,1)S(1)}, u32[]{:S(2)}, u32[]{:S(2)}) collective-permute-start(bf16[128,2048]{1,0:T(8,128)(2,1)S(1)} %collective-permute-done.28.refs_0_), channel_id=1, source_target_pairs={{0,1},{1,2},{2,3},{3,0},{4,5},{5,6},{6,7},{7,4},{8,9},{9,10},{10,1... | collective-permute-start | bytes 1572872 | tf_op jit(solution)/shard_map/ppermute | solution.py:65
  249.1 20.3 %collective-permute-start.29 = (bf16[128,2048]{1,0:T(8,128)(2,1)S(1)}, bf16[128,2048]{1,0:T(8,128)(2,1)S(1)}, u32[]{:S(2)}, u32[]{:S(2)}) collective-permute-start(bf16[128,2048]{1,0:T(8,128)(2,1)S(1)} %add_convert_fusion.6), channel_id=1, source_target_pairs={{0,1},{1,2},{2,3},{3,0},{4,5},{5,6},{6,7},{7,4},{8,9},{9,10},{10,1... | collective-permute-start | bytes 1572872 | tf_op jit(solution)/shard_map/ppermute | solution.py:65
  295.1 13.4 %collective-permute-start.33 = (bf16[128,2048]{1,0:T(8,128)(2,1)S(1)}, bf16[128,2048]{1,0:T(8,128)(2,1)S(1)}, u32[]{:S(2)}, u32[]{:S(2)}) collective-permute-start(bf16[128,2048]{1,0:T(8,128)(2,1)S(1)} %collective-permute-done.32.refs_1_), channel_id=1, source_target_pairs={{0,1},{1,2},{2,3},{3,0},{4,5},{5,6},{6,7},{7,4},{8,9},{9,10},{10,1... | collective-permute-start | bytes 1572872 | tf_op jit(solution)/shard_map/ppermute | solution.py:65
  330.6 42.3 %collective-permute-start.39 = (bf16[128,2048]{1,0:T(8,128)(2,1)S(1)}, bf16[128,2048]{1,0:T(8,128)(2,1)S(1)}, u32[]{:S(2)}, u32[]{:S(2)}) collective-permute-start(bf16[128,2048]{1,0:T(8,128)(2,1)S(1)} %copy-done.13), channel_id=1, source_target_pairs={{0,1},{1,2},{2,3},{3,0},{4,5},{5,6},{6,7},{7,4},{8,9},{9,10},{10,1... | collective-permute-start | bytes 1572872 | tf_op jit(solution)/shard_map/ppermute | solution.py:65
  336.6 40.6 %collective-permute-start.58 = (bf16[4,2,16,192]{3,2,1,0:T(8,128)(2,1)S(1)}, bf16[4,2,16,192]{3,2,1,0:T(8,128)(2,1)S(1)}, u32[]{:S(2)}, u32[]{:S(2)}) collective-permute-start(bf16[4,2,16,192]{3,2,1,0:T(8,128)(2,1)S(1)} %get-tuple-element.329), channel_id=1, source_target_pairs={{0,1},{1,2},{2,3},{3,0},{4,5},{5,6},{6,7},{7,4},{8,9},{9,10},{10,1... | collective-permute-start | bytes 147464 | tf_op jit(solution)/shard_map/ppermute | solution.py:835
  336.7 40.7 %collective-permute-start.59 = (bf16[4,2,16,192]{3,2,1,0:T(8,128)(2,1)S(1)}, bf16[4,2,16,192]{3,2,1,0:T(8,128)(2,1)S(1)}, u32[]{:S(2)}, u32[]{:S(2)}) collective-permute-start(bf16[4,2,16,192]{3,2,1,0:T(8,128)(2,1)S(1)} %get-tuple-element.328), channel_id=1, source_target_pairs={{0,2},{1,3},{2,0},{3,1},{4,6},{5,7},{6,4},{7,5},{8,10},{9,11},{10,... | collective-permute-start | bytes 147464 | tf_op jit(solution)/shard_map/ppermute | solution.py:835
  338.4 39.7 %collective-permute-start.60 = (bf16[4,2,16,192]{3,2,1,0:T(8,128)(2,1)S(1)}, bf16[4,2,16,192]{3,2,1,0:T(8,128)(2,1)S(1)}, u32[]{:S(2)}, u32[]{:S(2)}) collective-permute-start(bf16[4,2,16,192]{3,2,1,0:T(8,128)(2,1)S(1)} %get-tuple-element.327), channel_id=1, source_target_pairs={{0,3},{1,0},{2,1},{3,2},{4,7},{5,4},{6,5},{7,6},{8,11},{9,8},{10,9... | collective-permute-start | bytes 147464 | tf_op jit(solution)/shard_map/ppermute | solution.py:835
  376.6 17.9 %collective-permute-start.41 = (bf16[512,384]{1,0:T(8,128)(2,1)S(1)}, bf16[512,384]{1,0:T(8,128)(2,1)S(1)}, u32[]{:S(2)}, u32[]{:S(2)}) collective-permute-start(bf16[512,384]{1,0:T(8,128)(2,1)S(1)} %get-tuple-element.317), channel_id=1, source_target_pairs={{0,8},{4,12},{8,0},{12,4},{16,24},{20,28},{24,16},{28,20},{1,9},{5... | collective-permute-start | bytes 1179656 | tf_op jit(solution)/shard_map/ppermute | solution.py:109
  377.2 17.3 %collective-permute-start.42 = (bf16[512,384]{1,0:T(8,128)(2,1)S(1)}, bf16[512,384]{1,0:T(8,128)(2,1)S(1)}, u32[]{:S(2)}, u32[]{:S(2)}) collective-permute-start(bf16[512,384]{1,0:T(8,128)(2,1)S(1)} %get-tuple-element.316), channel_id=1, source_target_pairs={{0,4},{4,0},{8,12},{12,8},{16,20},{20,16},{24,28},{28,24},{1,5},{5... | collective-permute-start | bytes 1179656 | tf_op jit(solution)/shard_map/ppermute | solution.py:109
  377.4 20.2 %collective-permute-start.44 = (bf16[128,2048]{1,0:T(8,128)(2,1)S(1)}, bf16[128,2048]{1,0:T(8,128)(2,1)S(1)}, u32[]{:S(2)}, u32[]{:S(2)}) collective-permute-start(bf16[128,2048]{1,0:T(8,128)(2,1)S(1)} %add_convert_fusion.4), channel_id=1, source_target_pairs={{0,1},{1,2},{2,3},{3,0},{4,5},{5,6},{6,7},{7,4},{8,9},{9,10},{10,1... | collective-permute-start | bytes 1572872 | tf_op jit(solution)/shard_map/ppermute | solution.py:65
  402.0 22.8 %collective-permute-start.45 = (bf16[128,2048]{1,0:T(8,128)(2,1)S(1)}, bf16[128,2048]{1,0:T(8,128)(2,1)S(1)}, u32[]{:S(2)}, u32[]{:S(2)}) collective-permute-start(bf16[128,2048]{1,0:T(8,128)(2,1)S(1)} %add_convert_fusion.3), channel_id=1, source_target_pairs={{0,1},{1,2},{2,3},{3,0},{4,5},{5,6},{6,7},{7,4},{8,9},{9,10},{10,1... | collective-permute-start | bytes 1572872 | tf_op jit(solution)/shard_map/ppermute | solution.py:65
  409.6 39.4 %collective-permute-start.49 = (bf16[4,2,16,64]{3,2,1,0:T(8,128)(2,1)S(1)}, bf16[4,2,16,64]{3,2,1,0:T(8,128)(2,1)S(1)}, u32[]{:S(2)}, u32[]{:S(2)}) collective-permute-start(bf16[4,2,16,64]{3,2,1,0:T(8,128)(2,1)S(1)} %get-tuple-element.338), channel_id=1, source_target_pairs={{0,1},{1,2},{2,3},{3,0},{4,5},{5,6},{6,7},{7,4},{8,9},{9,10},{10,1... | collective-permute-start | bytes 49160 | tf_op jit(solution)/shard_map/ppermute | solution.py:835
  411.4 37.7 %collective-permute-start.50 = (bf16[4,2,16,64]{3,2,1,0:T(8,128)(2,1)S(1)}, bf16[4,2,16,64]{3,2,1,0:T(8,128)(2,1)S(1)}, u32[]{:S(2)}, u32[]{:S(2)}) collective-permute-start(bf16[4,2,16,64]{3,2,1,0:T(8,128)(2,1)S(1)} %get-tuple-element.337), channel_id=1, source_target_pairs={{0,2},{1,3},{2,0},{3,1},{4,6},{5,7},{6,4},{7,5},{8,10},{9,11},{10,... | collective-permute-start | bytes 49160 | tf_op jit(solution)/shard_map/ppermute | solution.py:835
  413.5 14.9 %collective-permute-start.64 = (bf16[16,192]{1,0:T(8,128)(2,1)S(1)}, bf16[16,192]{1,0:T(8,128)(2,1)S(1)}, u32[]{:S(2)}, u32[]{:S(2)}) collective-permute-start(bf16[16,192]{1,0:T(8,128)(2,1)S(1)} %slice.176), channel_id=1, source_target_pairs={{0,16},{4,20},{8,24},{12,28},{16,0},{20,4},{24,8},{28,12},{1,17},{... | collective-permute-start | bytes 18440 | tf_op jit(solution)/shard_map/ppermute | solution.py:849
  413.5 18.2 %collective-permute-start.65 = (bf16[16,576]{1,0:T(8,128)(2,1)S(1)}, bf16[16,576]{1,0:T(8,128)(2,1)S(1)}, u32[]{:S(2)}, u32[]{:S(2)}) collective-permute-start(bf16[16,576]{1,0:T(8,128)(2,1)S(1)} %slice.177), channel_id=1, source_target_pairs={{0,0},{1,8},{2,16},{3,24},{4,2},{5,10},{6,18},{7,26},{8,4},{9,12},... | collective-permute-start | bytes 55304 | tf_op jit(solution)/shard_map/ppermute | solution.py:856
  428.4 20.7 %collective-permute-start.51 = (bf16[4,2,16,64]{3,2,1,0:T(8,128)(2,1)S(1)}, bf16[4,2,16,64]{3,2,1,0:T(8,128)(2,1)S(1)}, u32[]{:S(2)}, u32[]{:S(2)}) collective-permute-start(bf16[4,2,16,64]{3,2,1,0:T(8,128)(2,1)S(1)} %get-tuple-element.336), channel_id=1, source_target_pairs={{0,3},{1,0},{2,1},{3,2},{4,7},{5,4},{6,5},{7,6},{8,11},{9,8},{10,9... | collective-permute-start | bytes 49160 | tf_op jit(solution)/shard_map/ppermute | solution.py:835
  431.7 15.8 %collective-permute-start.46 = (bf16[128,2048]{1,0:T(8,128)(2,1)S(1)}, bf16[128,2048]{1,0:T(8,128)(2,1)S(1)}, u32[]{:S(2)}, u32[]{:S(2)}) collective-permute-start(bf16[128,2048]{1,0:T(8,128)(2,1)S(1)} %copy-done.52), channel_id=1, source_target_pairs={{0,1},{1,2},{2,3},{3,0},{4,5},{5,6},{6,7},{7,4},{8,9},{9,10},{10,1... | collective-permute-start | bytes 1572872 | tf_op jit(solution)/shard_map/ppermute | solution.py:65
  447.6 15.0 %collective-permute-start.47 = (bf16[128,2048]{1,0:T(8,128)(2,1)S(1)}, bf16[128,2048]{1,0:T(8,128)(2,1)S(1)}, u32[]{:S(2)}, u32[]{:S(2)}) collective-permute-start(bf16[128,2048]{1,0:T(8,128)(2,1)S(1)} %add_convert_fusion.1), channel_id=1, source_target_pairs={{0,1},{1,2},{2,3},{3,0},{4,5},{5,6},{6,7},{7,4},{8,9},{9,10},{10,1... | collective-permute-start | bytes 1572872 | tf_op jit(solution)/shard_map/ppermute | solution.py:65
  450.0 12.9 %collective-permute-start.52 = (bf16[2,16,256]{2,1,0:T(8,128)(2,1)S(1)}, bf16[2,16,256]{2,1,0:T(8,128)(2,1)S(1)}, u32[]{:S(2)}, u32[]{:S(2)}) collective-permute-start(bf16[2,16,256]{2,1,0:T(8,128)(2,1)S(1)} %get-tuple-element.340), channel_id=1, source_target_pairs={{0,4},{4,0},{8,12},{12,8},{16,20},{20,16},{24,28},{28,24},{1,5},{5... | collective-permute-start | bytes 49160 | tf_op jit(solution)/shard_map/ppermute | solution.py:109
  450.0 12.9 %collective-permute-start.53 = (bf16[2,16,256]{2,1,0:T(8,128)(2,1)S(1)}, bf16[2,16,256]{2,1,0:T(8,128)(2,1)S(1)}, u32[]{:S(2)}, u32[]{:S(2)}) collective-permute-start(bf16[2,16,256]{2,1,0:T(8,128)(2,1)S(1)} %get-tuple-element.341), channel_id=1, source_target_pairs={{0,8},{4,12},{8,0},{12,4},{16,24},{20,28},{24,16},{28,20},{1,9},{5... | collective-permute-start | bytes 49160 | tf_op jit(solution)/shard_map/ppermute | solution.py:109
  450.1 12.8 %collective-permute-start.54 = (bf16[2,16,256]{2,1,0:T(8,128)(2,1)S(1)}, bf16[2,16,256]{2,1,0:T(8,128)(2,1)S(1)}, u32[]{:S(2)}, u32[]{:S(2)}) collective-permute-start(bf16[2,16,256]{2,1,0:T(8,128)(2,1)S(1)} %get-tuple-element.339), channel_id=1, source_target_pairs={{0,12},{4,8},{8,4},{12,0},{16,28},{20,24},{24,20},{28,16},{1,13},{... | collective-permute-start | bytes 49160 | tf_op jit(solution)/shard_map/ppermute | solution.py:109
  462.8 14.3 %collective-permute-start.48 = (bf16[128,2048]{1,0:T(8,128)(2,1)S(1)}, bf16[128,2048]{1,0:T(8,128)(2,1)S(1)}, u32[]{:S(2)}, u32[]{:S(2)}) collective-permute-start(bf16[128,2048]{1,0:T(8,128)(2,1)S(1)} %add_convert_fusion), channel_id=1, source_target_pairs={{0,1},{1,2},{2,3},{3,0},{4,5},{5,6},{6,7},{7,4},{8,9},{9,10},{10,1... | collective-permute-start | bytes 1572872 | tf_op jit(solution)/shard_map/ppermute | solution.py:65
  463.1 14.5 %collective-permute-start.55 = (bf16[16,64]{1,0:T(8,128)(2,1)S(1)}, bf16[16,64]{1,0:T(8,128)(2,1)S(1)}, u32[]{:S(2)}, u32[]{:S(2)}) collective-permute-start(bf16[16,64]{1,0:T(8,128)(2,1)S(1)} %slice.167), channel_id=1, source_target_pairs={{0,16},{4,20},{8,24},{12,28},{16,0},{20,4},{24,8},{28,12},{1,17},{... | collective-permute-start | bytes 6152 | tf_op jit(solution)/shard_map/ppermute | solution.py:849
  463.6 14.0 %collective-permute-start.56 = (bf16[16,192]{1,0:T(8,128)(2,1)S(1)}, bf16[16,192]{1,0:T(8,128)(2,1)S(1)}, u32[]{:S(2)}, u32[]{:S(2)}) collective-permute-start(bf16[16,192]{1,0:T(8,128)(2,1)S(1)} %slice.168), channel_id=1, source_target_pairs={{0,0},{1,8},{2,16},{3,24},{4,2},{5,10},{6,18},{7,26},{8,4},{9,12},... | collective-permute-start | bytes 18440 | tf_op jit(solution)/shard_map/ppermute | solution.py:856
  464.2 13.4 %collective-permute-start.57 = (bf16[16,192]{1,0:T(8,128)(2,1)S(1)}, bf16[16,192]{1,0:T(8,128)(2,1)S(1)}, u32[]{:S(2)}, u32[]{:S(2)}) collective-permute-start(bf16[16,192]{1,0:T(8,128)(2,1)S(1)} %slice.169), channel_id=1, source_target_pairs={{0,1},{1,9},{2,17},{3,25},{4,3},{5,11},{6,19},{7,27},{8,5},{9,13},... | collective-permute-start | bytes 18440 | tf_op jit(solution)/shard_map/ppermute | solution.py:856
  (86 other events, 1208.4 us)
Sparse Core Ops, SparseCore 0:
  46.9 26.3 all-gather.5
  95.8 90.4 all-gather.3
